TPU v7x, 512 devices: a whole 4x8x8 slice. The times are simulated.
512 devices in a mesh: shot: 32 (over z, y_hi, core), dom: 16 (over y_lo, x).
Axes of the slice: x: 4, y: 8 (y_hi: 2, y_lo: 4; y = y_hi * 4 + y_lo), z: 8, core: 2. Of those that a mesh axis runs over, the one named last changes fastest.
Arguments:
- vel_coef: float32 [32, 256, 64, 128], P('shot', 'dom'), may hold values from 0.06 to 0.32
- wave_now: float32 [32, 256, 64, 128], P('shot', 'dom'), may hold values from -0.9 to 0.9
- wave_prev: float32 [32, 256, 64, 128], P('shot', 'dom'), may hold values from -0.9 to 0.9
- adjoint_now: float32 [32, 256, 64, 128], P('shot', 'dom'), may hold values from -0.9 to 0.9
- adjoint_prev: float32 [32, 256, 64, 128], P('shot', 'dom'), may hold values from -0.9 to 0.9
- residuals: float32 [32, 4, 64, 128], P('shot'), may hold values from -0.9 to 0.9
- aperture_offset: int32 [32], P('shot'), may hold values from 0 to 16, as said below
- block_count: int32 [32], P('shot'), may hold values from 8 to 16, as said below
Outputs:
- gradient: float32 [32, 256, 4, 128], P('shot', 'dom')
Inputs may be any that keep to these rules, and one draw needn't show every extreme that they name: `aperture_offset`: a shot's aperture covers the 16 consecutive model blocks from its offset. The first block_count aperture blocks of a shot lie in the model and add to the gradient.
All inputs are finite; a program needn't handle non-finite values.
Results may differ from a plain program's by a relative error of at most 0.0003.
Values sent between devices are 32-bit elements; how exact they have to be, the bound alone decides.
No kernel may reach another device: no remote copies, remote signals or barrier semaphores. Data moves between devices by JAX's collectives and lax.ppermute only.
A program may use at most 64 MiB of HBM per device.

v0:
```python
import jax
import jax.numpy as jnp
from jax import lax
from jax.sharding import PartitionSpec as P


def padded(block, sides, width):
    for axis, dim in sides:
        count = lax.axis_size(axis)
        forward = [(i, i + 1) for i in range(count - 1)]
        backward = [(target, source) for source, target in forward]
        low = lax.ppermute(
            lax.slice_in_dim(block, block.shape[dim] - width, None, axis=dim), axis, forward
        )
        high = lax.ppermute(lax.slice_in_dim(block, 0, width, axis=dim), axis, backward)
        block = jnp.concatenate([low, block, high], axis=dim)
    return block


def lateral_laplace(padded_in):
    middle = padded_in[1:-1]
    lateral = jnp.pad(middle, ((0, 0), (1, 1), (1, 1)))
    total = padded_in[2:] + padded_in[:-2]
    total = total + lateral[:, 2:, 1:-1] + lateral[:, :-2, 1:-1]
    total = total + lateral[:, 1:-1, 2:] + lateral[:, 1:-1, :-2]
    return total - 6.0 * middle


def stencil(values_in):
    padded_in = padded(values_in, (("dom", 0),), 1)
    return lateral_laplace(padded_in)


def shards(
    vel_coef,
    wave_now,
    wave_prev,
    adjoint_now,
    adjoint_prev,
    residuals,
    aperture_offset,
    block_count,
):
    depth_size = vel_coef.shape[1]
    steps = residuals.shape[1]
    slab_index = lax.axis_index("dom")
    injection = residuals[0]
    laplacians = []
    adjoints = []
    depth_index = slab_index * depth_size + jnp.arange(depth_size, dtype=jnp.int32)
    surface = (depth_index == 0).astype(jnp.float32)[:, None, None]
    coefficient = vel_coef[0]
    wavefield, previous = (wave_now[0], wave_prev[0])
    for step_index in range(steps):
        laplacian = stencil(wavefield)
        laplacians.append(laplacian)
        wavefield, previous = (2.0 * wavefield - previous + coefficient * laplacian, wavefield)
    adjoint, adjoint_old = (adjoint_now[0], adjoint_prev[0])
    for step_index in range(steps):
        updated = 2.0 * adjoint - adjoint_old + stencil(coefficient * adjoint)
        updated = updated + surface * injection[step_index][None]
        adjoints.append(updated)
        adjoint, adjoint_old = (updated, adjoint)
    imaging = laplacians[0] * adjoints[steps - 1]
    for step_index in range(1, steps):
        imaging = imaging + laplacians[step_index] * adjoints[steps - 1 - step_index]
    model_blocks = lax.axis_size("shot")
    aperture_blocks = model_blocks // 2
    block_width = imaging.shape[1] // aperture_blocks
    width_y = imaging.shape[2]
    columns = imaging.reshape(depth_size, aperture_blocks, block_width, width_y)
    first_block = aperture_offset[0]
    live_count = block_count[0]
    model_index = jnp.arange(lax.axis_size("shot") * 1, dtype=jnp.int32)
    block_index = jnp.arange(aperture_blocks, dtype=jnp.int32)
    select_rows = (
        (first_block + block_index[None, :] == model_index[:, None])
        & (block_index[None, :] < live_count)
    ).astype(jnp.float32)
    return lax.psum_scatter(
        jnp.einsum("mj,zjxy->mzxy", select_rows, columns, precision=lax.Precision.HIGHEST),
        "shot",
        scatter_dimension=0,
        tiled=True,
    )


def solution(mesh):
    placed = (
        P("shot", "dom", None, None),
        P("shot", "dom", None, None),
        P("shot", "dom", None, None),
        P("shot", "dom", None, None),
        P("shot", "dom", None, None),
        P("shot", None, None, None),
        P("shot"),
        P("shot"),
    )
    return jax.shard_map(
        shards, mesh=mesh, in_specs=placed, out_specs=P("shot", "dom", None, None), check_vma=False
    )
```

profile of v0, /device:TPU:6, one launch (start us, length us, event | category | flops | bytes accessed | tf_op | source)
XLA Modules:
  0.0 238.4 jit_solution(16426524314976189209)
XLA Ops:
  6.5 0.8 slice_bitcast_fusion.5
  7.3 2.7 %collective-permute-start = (f32[1,64,128]{2,1,0:T(8,128)S(1)}, f32[1,64,128]{2,1,0:T(8,128)S(1)}, u32[]{:S(2)}, u32[]{:S(2)}) collective-permute-start(f32[1,64,128]{2,1,0:T(8,128)S(1)} %get-tuple-element.32), channel_id=1, source_target_pairs={{1,0},{2,1},{3,2},{4,3},{5,4},{6,5},{7,6},{8,7},{9,8},{10,9},{11,1... | collective-permute-start | bytes 98312 | tf_op jit(solution)/shard_map/ppermute | solution.py:15
  10.1 5.2 %collective-permute-start.1 = (f32[1,64,128]{2,1,0:T(8,128)S(1)}, f32[1,64,128]{2,1,0:T(8,128)S(1)}, u32[]{:S(2)}, u32[]{:S(2)}) collective-permute-start(f32[1,64,128]{2,1,0:T(8,128)S(1)} %get-tuple-element.33), channel_id=1, source_target_pairs={{0,1},{1,2},{2,3},{3,4},{4,5},{5,6},{6,7},{7,8},{8,9},{9,10},{10,1... | collective-permute-start | bytes 98312 | tf_op jit(solution)/shard_map/ppermute | solution.py:12
  15.3 1.6 collective-permute-done.1
  16.9 4.0 %fusion.61 = (f32[16,64,128]{2,1,0:T(8,128)S(1)}, f32[16,64,128]{2,1,0:T(8,128)S(1)}) fusion(f32[1,16,64,128]{3,2,1,0:T(8,128)} %param.10, f32[1,16,64,128]{3,2,1,0:T(8,128)} %param.8, f32[1,16,64,128]{3,2,1,0:T(8,128)} %param.9, f32[16,64,128]{2,1,0:T(8,128)} %bitcast.69, f32[1,64,128]{2,1,0:T(8,128)S(1)} %collective-permute-done.1, ...), kind=kLoop, calls=%fused_computation.110 | loop fusion | flops 1703936 | bytes 3211264 | tf_op jit(solution)/shard_map/add | solution.py:57
  20.9 5.3 %collective-permute-start.10 = (f32[1,64,128]{2,1,0:T(8,128)S(1)}, f32[1,64,128]{2,1,0:T(8,128)S(1)}, u32[]{:S(2)}, u32[]{:S(2)}) collective-permute-start(f32[1,64,128]{2,1,0:T(8,128)S(1)} %get-tuple-element.24), channel_id=1, source_target_pairs={{1,0},{2,1},{3,2},{4,3},{5,4},{6,5},{7,6},{8,7},{9,8},{10,9},{11,1... | collective-permute-start | bytes 98312 | tf_op jit(solution)/shard_map/ppermute | solution.py:15
  26.2 2.9 %collective-permute-start.11 = (f32[1,64,128]{2,1,0:T(8,128)S(1)}, f32[1,64,128]{2,1,0:T(8,128)S(1)}, u32[]{:S(2)}, u32[]{:S(2)}) collective-permute-start(f32[1,64,128]{2,1,0:T(8,128)S(1)} %get-tuple-element.25), channel_id=1, source_target_pairs={{0,1},{1,2},{2,3},{3,4},{4,5},{5,6},{6,7},{7,8},{8,9},{9,10},{10,1... | collective-permute-start | bytes 98312 | tf_op jit(solution)/shard_map/ppermute | solution.py:12
  29.2 2.9 %collective-permute-done.11 = f32[1,64,128]{2,1,0:T(8,128)S(1)} collective-permute-done((f32[1,64,128]{2,1,0:T(8,128)S(1)}, f32[1,64,128]{2,1,0:T(8,128)S(1)}, u32[]{:S(2)}, u32[]{:S(2)}) %collective-permute-start.11) | collective-permute-done | bytes 32800 | tf_op jit(solution)/shard_map/ppermute | solution.py:12
  32.6 0.8 copy-done.4
  33.4 4.0 %collective-permute-start.12 = (f32[1,64,128]{2,1,0:T(8,128)S(1)}, f32[1,64,128]{2,1,0:T(8,128)S(1)}, u32[]{:S(2)}, u32[]{:S(2)}) collective-permute-start(f32[1,64,128]{2,1,0:T(8,128)S(1)} %get-tuple-element.22), channel_id=1, source_target_pairs={{1,0},{2,1},{3,2},{4,3},{5,4},{6,5},{7,6},{8,7},{9,8},{10,9},{11,1... | collective-permute-start | bytes 98312 | tf_op jit(solution)/shard_map/ppermute | solution.py:15
  37.5 3.9 %collective-permute-start.13 = (f32[1,64,128]{2,1,0:T(8,128)S(1)}, f32[1,64,128]{2,1,0:T(8,128)S(1)}, u32[]{:S(2)}, u32[]{:S(2)}) collective-permute-start(f32[1,64,128]{2,1,0:T(8,128)S(1)} %get-tuple-element.23), channel_id=1, source_target_pairs={{0,1},{1,2},{2,3},{3,4},{4,5},{5,6},{6,7},{7,8},{8,9},{9,10},{10,1... | collective-permute-start | bytes 98312 | tf_op jit(solution)/shard_map/ppermute | solution.py:12
  41.4 1.9 collective-permute-done.13
  43.3 3.6 %fusion.63 = (f32[16,64,128]{2,1,0:T(8,128)S(1)}, f32[16,64,128]{2,1,0:T(8,128)S(1)}, f32[16,64,128]{2,1,0:T(8,128)S(1)}) fusion(f32[1,16,64,128]{3,2,1,0:T(8,128)S(1)} %copy-done, f32[16,64,128]{2,1,0:T(8,128)S(1)} %get-tuple-element.8, f32[16,64,128]{2,1,0:T(8,128)S(1)} %get-tuple-element.10, f32[1,16,64,128]{3,2,1,0:T(8,128)S(1)} %copy-done.2, ...), kind=kLoop, calls=%fused_computation.119 | loop fusion | flops 2883584 | bytes 5308416 | tf_op jit(solution)/shard_map/add | solution.py:57
  46.9 1.9 collective-permute-start.2
  48.8 6.0 %collective-permute-start.3 = (f32[1,64,128]{2,1,0:T(8,128)S(1)}, f32[1,64,128]{2,1,0:T(8,128)S(1)}, u32[]{:S(2)}, u32[]{:S(2)}) collective-permute-start(f32[1,64,128]{2,1,0:T(8,128)S(1)} %get-tuple-element.31), channel_id=1, source_target_pairs={{0,1},{1,2},{2,3},{3,4},{4,5},{5,6},{6,7},{7,8},{8,9},{9,10},{10,1... | collective-permute-start | bytes 98312 | tf_op jit(solution)/shard_map/ppermute | solution.py:12
  55.5 0.9 collective-permute-done.3
  56.9 1.9 collective-permute-start.4
  58.9 6.3 %collective-permute-start.5 = (f32[1,64,128]{2,1,0:T(8,128)S(1)}, f32[1,64,128]{2,1,0:T(8,128)S(1)}, u32[]{:S(2)}, u32[]{:S(2)}) collective-permute-start(f32[1,64,128]{2,1,0:T(8,128)S(1)} %get-tuple-element.29), channel_id=1, source_target_pairs={{0,1},{1,2},{2,3},{3,4},{4,5},{5,6},{6,7},{7,8},{8,9},{9,10},{10,1... | collective-permute-start | bytes 98312 | tf_op jit(solution)/shard_map/ppermute | solution.py:12
  65.9 0.9 collective-permute-done.5
  67.3 1.9 collective-permute-start.6
  69.2 6.3 %collective-permute-start.7 = (f32[1,64,128]{2,1,0:T(8,128)S(1)}, f32[1,64,128]{2,1,0:T(8,128)S(1)}, u32[]{:S(2)}, u32[]{:S(2)}) collective-permute-start(f32[1,64,128]{2,1,0:T(8,128)S(1)} %get-tuple-element.27), channel_id=1, source_target_pairs={{0,1},{1,2},{2,3},{3,4},{4,5},{5,6},{6,7},{7,8},{8,9},{9,10},{10,1... | collective-permute-start | bytes 98312 | tf_op jit(solution)/shard_map/ppermute | solution.py:12
  75.6 1.9 collective-permute-start.14
  77.5 6.0 %collective-permute-start.15 = (f32[1,64,128]{2,1,0:T(8,128)S(1)}, f32[1,64,128]{2,1,0:T(8,128)S(1)}, u32[]{:S(2)}, u32[]{:S(2)}) collective-permute-start(f32[1,64,128]{2,1,0:T(8,128)S(1)} %get-tuple-element.20), channel_id=1, source_target_pairs={{0,1},{1,2},{2,3},{3,4},{4,5},{5,6},{6,7},{7,8},{8,9},{9,10},{10,1... | collective-permute-start | bytes 98312 | tf_op jit(solution)/shard_map/ppermute | solution.py:12
  83.6 0.6 bitcast_multiply_fusion.3
  84.1 1.9 collective-permute-start.8
  86.1 6.0 %collective-permute-start.9 = (f32[1,64,128]{2,1,0:T(8,128)S(1)}, f32[1,64,128]{2,1,0:T(8,128)S(1)}, u32[]{:S(2)}, u32[]{:S(2)}) collective-permute-start(f32[1,64,128]{2,1,0:T(8,128)S(1)} %get-tuple-element.18), channel_id=1, source_target_pairs={{0,1},{1,2},{2,3},{3,4},{4,5},{5,6},{6,7},{7,8},{8,9},{9,10},{10,1... | collective-permute-start | bytes 98312 | tf_op jit(solution)/shard_map/ppermute | solution.py:12
  92.2 1.5 collective-permute-done.9
  93.7 0.9 fusion.36
  94.6 0.7 fusion.64
  95.2 1.6 copy.12
  96.9 133.3 %reduce-scatter.2.cloned.1.call-done = f32[1,16,4,128]{3,1,2,0:T(8,128)} async-done(((f32[32,16,4,128]{3,1,2,0:T(8,128)}), f32[1,16,4,128]{3,1,2,0:T(8,128)}) %reduce-scatter.2.cloned.1.call-update) | async-done | bytes 32784 | tf_op jit(solution)/shard_map/reduce_scatter | solution.py:80
  230.1 1.4 copy.13
  (39 shorter events, 1.6 us)
Async XLA Ops:
  6.5 223.6 %reduce-scatter.2.cloned.1.call-start = ((), (), s32[]{:S(2)}) async-start(), calls=%async_computation.1 | async-start | bytes 1081344 | tf_op jit(solution)/shard_map/reduce_scatter | solution.py:80
  7.3 8.0 %collective-permute-start = (f32[1,64,128]{2,1,0:T(8,128)S(1)}, f32[1,64,128]{2,1,0:T(8,128)S(1)}, u32[]{:S(2)}, u32[]{:S(2)}) collective-permute-start(f32[1,64,128]{2,1,0:T(8,128)S(1)} %get-tuple-element.32), channel_id=1, source_target_pairs={{1,0},{2,1},{3,2},{4,3},{5,4},{6,5},{7,6},{8,7},{9,8},{10,9},{11,1... | collective-permute-start | bytes 98312 | tf_op jit(solution)/shard_map/ppermute | solution.py:15
  10.1 6.8 %collective-permute-start.1 = (f32[1,64,128]{2,1,0:T(8,128)S(1)}, f32[1,64,128]{2,1,0:T(8,128)S(1)}, u32[]{:S(2)}, u32[]{:S(2)}) collective-permute-start(f32[1,64,128]{2,1,0:T(8,128)S(1)} %get-tuple-element.33), channel_id=1, source_target_pairs={{0,1},{1,2},{2,3},{3,4},{4,5},{5,6},{6,7},{7,8},{8,9},{9,10},{10,1... | collective-permute-start | bytes 98312 | tf_op jit(solution)/shard_map/ppermute | solution.py:12
  16.8 15.2 %copy-start = (f32[1,16,64,128]{3,2,1,0:T(8,128)S(1)}, f32[1,16,64,128]{3,2,1,0:T(8,128)}, u32[]{:S(2)}) copy-start(f32[1,16,64,128]{3,2,1,0:T(8,128)} %param.8) | copy-start | bytes 1572868
  16.9 15.2 %copy-start.1 = (f32[1,16,64,128]{3,2,1,0:T(8,128)S(1)}, f32[1,16,64,128]{3,2,1,0:T(8,128)}, u32[]{:S(2)}) copy-start(f32[1,16,64,128]{3,2,1,0:T(8,128)} %param.9) | copy-start | bytes 1572868
  16.9 15.2 %copy-start.2 = (f32[1,16,64,128]{3,2,1,0:T(8,128)S(1)}, f32[1,16,64,128]{3,2,1,0:T(8,128)}, u32[]{:S(2)}) copy-start(f32[1,16,64,128]{3,2,1,0:T(8,128)} %param.10) | copy-start | bytes 1572868
  20.9 8.3 %collective-permute-start.10 = (f32[1,64,128]{2,1,0:T(8,128)S(1)}, f32[1,64,128]{2,1,0:T(8,128)S(1)}, u32[]{:S(2)}, u32[]{:S(2)}) collective-permute-start(f32[1,64,128]{2,1,0:T(8,128)S(1)} %get-tuple-element.24), channel_id=1, source_target_pairs={{1,0},{2,1},{3,2},{4,3},{5,4},{6,5},{7,6},{8,7},{9,8},{10,9},{11,1... | collective-permute-start | bytes 98312 | tf_op jit(solution)/shard_map/ppermute | solution.py:15
  26.2 5.8 %collective-permute-start.11 = (f32[1,64,128]{2,1,0:T(8,128)S(1)}, f32[1,64,128]{2,1,0:T(8,128)S(1)}, u32[]{:S(2)}, u32[]{:S(2)}) collective-permute-start(f32[1,64,128]{2,1,0:T(8,128)S(1)} %get-tuple-element.25), channel_id=1, source_target_pairs={{0,1},{1,2},{2,3},{3,4},{4,5},{5,6},{6,7},{7,8},{8,9},{9,10},{10,1... | collective-permute-start | bytes 98312 | tf_op jit(solution)/shard_map/ppermute | solution.py:12
  32.1 9.3 %copy-start.6 = (f32[1,4,64,128]{3,2,1,0:T(8,128)S(1)}, f32[1,4,64,128]{3,2,1,0:T(8,128)}, u32[]{:S(2)}) copy-start(f32[1,4,64,128]{3,2,1,0:T(8,128)} %param.13) | copy-start | bytes 393220
  32.1 11.2 %copy-start.3 = (f32[1,16,64,128]{3,2,1,0:T(8,128)S(1)}, f32[1,16,64,128]{3,2,1,0:T(8,128)}, u32[]{:S(2)}) copy-start(f32[1,16,64,128]{3,2,1,0:T(8,128)} %param.11) | copy-start | bytes 1572868
  32.6 0.8 copy-start.4
  33.4 8.0 %collective-permute-start.12 = (f32[1,64,128]{2,1,0:T(8,128)S(1)}, f32[1,64,128]{2,1,0:T(8,128)S(1)}, u32[]{:S(2)}, u32[]{:S(2)}) collective-permute-start(f32[1,64,128]{2,1,0:T(8,128)S(1)} %get-tuple-element.22), channel_id=1, source_target_pairs={{1,0},{2,1},{3,2},{4,3},{5,4},{6,5},{7,6},{8,7},{9,8},{10,9},{11,1... | collective-permute-start | bytes 98312 | tf_op jit(solution)/shard_map/ppermute | solution.py:15
  37.5 5.8 %collective-permute-start.13 = (f32[1,64,128]{2,1,0:T(8,128)S(1)}, f32[1,64,128]{2,1,0:T(8,128)S(1)}, u32[]{:S(2)}, u32[]{:S(2)}) collective-permute-start(f32[1,64,128]{2,1,0:T(8,128)S(1)} %get-tuple-element.23), channel_id=1, source_target_pairs={{0,1},{1,2},{2,3},{3,4},{4,5},{5,6},{6,7},{7,8},{8,9},{9,10},{10,1... | collective-permute-start | bytes 98312 | tf_op jit(solution)/shard_map/ppermute | solution.py:12
  43.3 13.2 %copy-start.5 = (f32[1,16,64,128]{3,2,1,0:T(8,128)S(1)}, f32[1,16,64,128]{3,2,1,0:T(8,128)}, u32[]{:S(2)}) copy-start(f32[1,16,64,128]{3,2,1,0:T(8,128)} %param.12) | copy-start | bytes 1572868
  46.9 8.6 %collective-permute-start.2 = (f32[1,64,128]{2,1,0:T(8,128)S(1)}, f32[1,64,128]{2,1,0:T(8,128)S(1)}, u32[]{:S(2)}, u32[]{:S(2)}) collective-permute-start(f32[1,64,128]{2,1,0:T(8,128)S(1)} %get-tuple-element.30), channel_id=1, source_target_pairs={{1,0},{2,1},{3,2},{4,3},{5,4},{6,5},{7,6},{8,7},{9,8},{10,9},{11,1... | collective-permute-start | bytes 98312 | tf_op jit(solution)/shard_map/ppermute | solution.py:15
  48.8 7.6 %collective-permute-start.3 = (f32[1,64,128]{2,1,0:T(8,128)S(1)}, f32[1,64,128]{2,1,0:T(8,128)S(1)}, u32[]{:S(2)}, u32[]{:S(2)}) collective-permute-start(f32[1,64,128]{2,1,0:T(8,128)S(1)} %get-tuple-element.31), channel_id=1, source_target_pairs={{0,1},{1,2},{2,3},{3,4},{4,5},{5,6},{6,7},{7,8},{8,9},{9,10},{10,1... | collective-permute-start | bytes 98312 | tf_op jit(solution)/shard_map/ppermute | solution.py:12
  56.9 8.9 %collective-permute-start.4 = (f32[1,64,128]{2,1,0:T(8,128)S(1)}, f32[1,64,128]{2,1,0:T(8,128)S(1)}, u32[]{:S(2)}, u32[]{:S(2)}) collective-permute-start(f32[1,64,128]{2,1,0:T(8,128)S(1)} %get-tuple-element.28), channel_id=1, source_target_pairs={{1,0},{2,1},{3,2},{4,3},{5,4},{6,5},{7,6},{8,7},{9,8},{10,9},{11,1... | collective-permute-start | bytes 98312 | tf_op jit(solution)/shard_map/ppermute | solution.py:15
  58.9 7.9 %collective-permute-start.5 = (f32[1,64,128]{2,1,0:T(8,128)S(1)}, f32[1,64,128]{2,1,0:T(8,128)S(1)}, u32[]{:S(2)}, u32[]{:S(2)}) collective-permute-start(f32[1,64,128]{2,1,0:T(8,128)S(1)} %get-tuple-element.29), channel_id=1, source_target_pairs={{0,1},{1,2},{2,3},{3,4},{4,5},{5,6},{6,7},{7,8},{8,9},{9,10},{10,1... | collective-permute-start | bytes 98312 | tf_op jit(solution)/shard_map/ppermute | solution.py:12
  67.3 16.3 %collective-permute-start.6 = (f32[1,64,128]{2,1,0:T(8,128)S(1)}, f32[1,64,128]{2,1,0:T(8,128)S(1)}, u32[]{:S(2)}, u32[]{:S(2)}) collective-permute-start(f32[1,64,128]{2,1,0:T(8,128)S(1)} %get-tuple-element.26), channel_id=1, source_target_pairs={{1,0},{2,1},{3,2},{4,3},{5,4},{6,5},{7,6},{8,7},{9,8},{10,9},{11,1... | collective-permute-start | bytes 98312 | tf_op jit(solution)/shard_map/ppermute | solution.py:15
  69.2 14.3 %collective-permute-start.7 = (f32[1,64,128]{2,1,0:T(8,128)S(1)}, f32[1,64,128]{2,1,0:T(8,128)S(1)}, u32[]{:S(2)}, u32[]{:S(2)}) collective-permute-start(f32[1,64,128]{2,1,0:T(8,128)S(1)} %get-tuple-element.27), channel_id=1, source_target_pairs={{0,1},{1,2},{2,3},{3,4},{4,5},{5,6},{6,7},{7,8},{8,9},{9,10},{10,1... | collective-permute-start | bytes 98312 | tf_op jit(solution)/shard_map/ppermute | solution.py:12
  75.6 16.5 %collective-permute-start.14 = (f32[1,64,128]{2,1,0:T(8,128)S(1)}, f32[1,64,128]{2,1,0:T(8,128)S(1)}, u32[]{:S(2)}, u32[]{:S(2)}) collective-permute-start(f32[1,64,128]{2,1,0:T(8,128)S(1)} %get-tuple-element.19), channel_id=1, source_target_pairs={{1,0},{2,1},{3,2},{4,3},{5,4},{6,5},{7,6},{8,7},{9,8},{10,9},{11,1... | collective-permute-start | bytes 98312 | tf_op jit(solution)/shard_map/ppermute | solution.py:15
  77.5 14.6 %collective-permute-start.15 = (f32[1,64,128]{2,1,0:T(8,128)S(1)}, f32[1,64,128]{2,1,0:T(8,128)S(1)}, u32[]{:S(2)}, u32[]{:S(2)}) collective-permute-start(f32[1,64,128]{2,1,0:T(8,128)S(1)} %get-tuple-element.20), channel_id=1, source_target_pairs={{0,1},{1,2},{2,3},{3,4},{4,5},{5,6},{6,7},{7,8},{8,9},{9,10},{10,1... | collective-permute-start | bytes 98312 | tf_op jit(solution)/shard_map/ppermute | solution.py:12
  84.1 8.0 %collective-permute-start.8 = (f32[1,64,128]{2,1,0:T(8,128)S(1)}, f32[1,64,128]{2,1,0:T(8,128)S(1)}, u32[]{:S(2)}, u32[]{:S(2)}) collective-permute-start(f32[1,64,128]{2,1,0:T(8,128)S(1)} %get-tuple-element.17), channel_id=1, source_target_pairs={{1,0},{2,1},{3,2},{4,3},{5,4},{6,5},{7,6},{8,7},{9,8},{10,9},{11,1... | collective-permute-start | bytes 98312 | tf_op jit(solution)/shard_map/ppermute | solution.py:15
  86.1 7.6 %collective-permute-start.9 = (f32[1,64,128]{2,1,0:T(8,128)S(1)}, f32[1,64,128]{2,1,0:T(8,128)S(1)}, u32[]{:S(2)}, u32[]{:S(2)}) collective-permute-start(f32[1,64,128]{2,1,0:T(8,128)S(1)} %get-tuple-element.18), channel_id=1, source_target_pairs={{0,1},{1,2},{2,3},{3,4},{4,5},{5,6},{6,7},{7,8},{8,9},{9,10},{10,1... | collective-permute-start | bytes 98312 | tf_op jit(solution)/shard_map/ppermute | solution.py:12
Sparse Core Ops, SparseCore 0:
  97.0 133.1 reduce-scatter.1
where the time goes:
time: 239 us; the launch traced here: 238 us
  waiting for transfers between devices  143 us (60%)
  starting transfers between devices  64.5 us (27%)
  between operations  15 us (6%)
  other arithmetic  10.5 us (4%)
  local copies, waits for them, and re-layouts  4.62 us (2%)
    reduce_scatter x1, waiting for transfers between devices, shards(): lax.psum_scatter(jnp.einsum('mj,zjxy->mzxy', select_rows, columns, precis...  133 us
    ppermute x8, starting transfers between devices, padded(): lax.ppermute(lax.slice_in_dim(block, block.shape[dim] - width, None, axis...  42.8 us
    ppermute x8, starting transfers between devices, padded(): lax.ppermute(lax.slice_in_dim(block, 0, width, axis=dim), axis, backward)  21.7 us
    ppermute x8, waiting for transfers between devices, padded(): lax.ppermute(lax.slice_in_dim(block, block.shape[dim] - width, None, axis...  9.65 us
    add x3, other arithmetic, shards(): 2.0 * wavefield - previous + coefficient * laplacian  8.14 us
  transfers between devices with their start and end apart: 17, of which 7 were waited for; matrix products, arithmetic and copies ran while one was open for 0% of the time, Pallas kernels for 0%

commit v1 on v0

v1 whole, which is shorter than its diff:
```python
import functools

import jax
import jax.numpy as jnp
from jax import lax
from jax.experimental import pallas as pl
from jax.experimental.pallas import tpu as pltpu
from jax.sharding import PartitionSpec as P

PAD = 8


def lateral(ref, z, width, first, last):
    middle = ref[z, PAD : PAD + width, :]
    total = ref[z, PAD - 1 : PAD - 1 + width, :] + ref[z, PAD + 1 : PAD + 1 + width, :]
    size = middle.shape[1]
    left = jnp.where(first, 0.0, pltpu.roll(middle, 1, 1))
    right = jnp.where(last, 0.0, pltpu.roll(middle, size - 1, 1))
    return total + (left + right) - 6.0 * middle, middle


def replay(
    steps, depth, width, size, blocks,
    offset, count, vel, wave, wave_old, adj, adj_old, low, high, residuals,
    own, other,
    p0, p1, v, w0, w1, q, img,
):
    h = steps
    slab = lax.axis_index("dom")
    core = lax.rem(lax.axis_index("shot"), 2)
    column = lax.broadcasted_iota(jnp.int32, (width, size), 1)
    first, last = column == 0, column == size - 1
    rows = slice(PAD, PAD + width)
    edge = jnp.zeros((depth + 2 * h, PAD, size), jnp.float32)
    for ref in (p0, p1, w0, w1):
        ref[:, 0:PAD, :] = edge
        ref[:, PAD + width : 2 * PAD + width, :] = edge
    at = [0, h, 2 * h - 1, 3 * h - 1, 4 * h - 1]
    n = depth
    p0[0:h, rows, :] = low[at[0] : at[0] + h]
    p0[h + n : 2 * h + n, rows, :] = high[at[0] : at[0] + h]
    p0[h : h + n, rows, :] = wave[0]
    p1[1:h, rows, :] = low[at[1] : at[1] + h - 1]
    p1[h + n : 2 * h + n - 1, rows, :] = high[at[1] : at[1] + h - 1]
    p1[h : h + n, rows, :] = wave_old[0]
    v[0:h] = low[at[2] : at[2] + h]
    v[h + n : 2 * h + n] = high[at[2] : at[2] + h]
    v[h : h + n] = vel[0]
    q[1, 0:h] = low[at[3] : at[3] + h]
    q[1, h + n : 2 * h + n] = high[at[3] : at[3] + h]
    q[1, h : h + n] = adj[0]
    q[0, 1:h] = low[at[4] : at[4] + h - 1]
    q[0, h + n : 2 * h + n - 1] = high[at[4] : at[4] + h - 1]
    q[0, h : h + n] = adj_old[0]

    @pl.loop(0, n + 2 * h)
    def _(z):
        w0[z, rows, :] = v[z] * q[1, z]

    ws = (w0, w1)
    for step in range(steps):
        source, target = ws[step % 2], ws[(step + 1) % 2]

        @pl.loop(step + 1, n + 2 * h - step - 1)
        def _(z):
            lap, _ = lateral(source, z, width, first, last)
            lap = lap + (source[z - 1, rows, :] + source[z + 1, rows, :])
            new = 2.0 * q[step + 1, z] - q[step, z] + lap
            q[step + 2, z] = new
            target[z, rows, :] = v[z] * new

        @pl.when(slab == 0)
        def _():
            new = q[step + 2, h] + residuals[0, step]
            q[step + 2, h] = new
            target[h, rows, :] = v[h] * new

    ps = (p0, p1)
    for step in range(steps):
        source, target = ps[step % 2], ps[(step + 1) % 2]
        inner = step < steps - 1

        def lap_of(z):
            lap, middle = lateral(source, z, width, first, last)
            lap = lap + (source[z - 1, rows, :] + source[z + 1, rows, :])
            if inner:
                target[z, rows, :] = 2.0 * middle - target[z, rows, :] + v[z] * lap
            return lap

        if inner:
            for begin, end in ((step + 1, h), (h + n, n + 2 * h - step - 1)):

                @pl.loop(begin, end)
                def _(z):
                    lap_of(z)

        @pl.loop(h, h + n)
        def _(z):
            term = lap_of(z) * q[steps + 1 - step, z]
            if step == 0:
                img[z - h] = term
            else:
                img[z - h] += term

    span = width // blocks
    zero = jnp.zeros((n * span, size), jnp.float32)

    @pl.loop(0, blocks)
    def _(k):
        own[k] = zero
        other[k] = zero

    start, live = offset[0], count[0]
    odd = lax.rem(start + core, 2)
    for j in range(blocks):
        k = lax.div(start + j, 2)
        mine = odd == j % 2
        for ref, take in ((own, mine), (other, jnp.logical_not(mine))):

            @pl.when(jnp.logical_and(take, j < live))
            def _(ref=ref):
                for z in range(n):
                    ref[k, z * span : (z + 1) * span, :] = img[z, j * span : (j + 1) * span, :]


def total(parts, out):
    out[...] = jnp.sum(parts[...], axis=0)


def shards(vel, wave, wave_old, adj, adj_old, residuals, offset, count):
    _, depth, width, size = vel.shape
    steps = residuals.shape[1]
    shots, doms = lax.axis_size("shot"), lax.axis_size("dom")
    blocks = shots // 2
    span = width // blocks
    h = steps

    up = [a[0, depth - m :] for a, m in ((wave, h), (wave_old, h - 1), (vel, h), (adj, h), (adj_old, h - 1))]
    down = [a[0, :m] for a, m in ((wave, h), (wave_old, h - 1), (vel, h), (adj, h), (adj_old, h - 1))]
    forward = [(i, i + 1) for i in range(doms - 1)]
    backward = [(i + 1, i) for i in range(doms - 1)]
    low = lax.ppermute(jnp.concatenate(up), "dom", forward)
    high = lax.ppermute(jnp.concatenate(down), "dom", backward)

    smem = pl.BlockSpec(memory_space=pltpu.SMEM)
    vmem = pl.BlockSpec(memory_space=pltpu.VMEM)
    planes = depth + 2 * h
    padded = pltpu.VMEM((planes, width + 2 * PAD, size), jnp.float32)
    block = jax.ShapeDtypeStruct((blocks, depth * span, size), jnp.float32)
    own, other = pl.pallas_call(
        functools.partial(replay, steps, depth, width, size, blocks),
        out_shape=(block, block),
        in_specs=[smem, smem] + [vmem] * 8,
        out_specs=(vmem, vmem),
        scratch_shapes=[
            padded, padded,
            pltpu.VMEM((planes, width, size), jnp.float32),
            padded, padded,
            pltpu.VMEM((steps + 2, planes, width, size), jnp.float32),
            pltpu.VMEM((depth, width, size), jnp.float32),
        ],
        compiler_params=pltpu.CompilerParams(vmem_limit_bytes=40 * 2**20),
    )(offset, count, vel, wave, wave_old, adj, adj_old, low, high, residuals)

    pair = [(s, s + 1 - 2 * (s % 2)) for s in range(shots)]
    both = own + lax.ppermute(other, "shot", pair)
    groups = [[2 * k + c for k in range(blocks)] for c in range(2)]
    parts = lax.all_to_all(both, "shot", 0, 0, tiled=True, axis_index_groups=groups)
    out = pl.pallas_call(
        total,
        out_shape=jax.ShapeDtypeStruct((depth * span, size), jnp.float32),
        in_specs=[vmem],
        out_specs=vmem,
    )(parts)
    return out.reshape(1, depth, span, size)


def solution(mesh):
    field = P("shot", "dom", None, None)
    placed = (field,) * 5 + (P("shot", None, None, None), P("shot"), P("shot"))
    return jax.shard_map(shards, mesh=mesh, in_specs=placed, out_specs=field, check_vma=False)
```

time: 239 us -> 82.3 us (0.34)
  the two profiles are of different devices: /device:TPU:6 before, /device:TPU:8 now
where the time goes in v1:
time: 82.3 us; the launch traced here: 82 us
  blocking collectives  37.1 us (45%)
  Pallas kernels  16.4 us (20%)
  waiting for transfers between devices  12.9 us (16%)
  starting transfers between devices  9.87 us (12%)
  local copies, waits for them, and re-layouts  4.27 us (5%)
  between operations  1.4 us (2%)
    all_to_all x1, blocking collectives, shards(): lax.all_to_all(both, 'shot', 0, 0, tiled=True, axis_index_groups=groups)  37.1 us
    pallas_call x1, Pallas kernels, shards(): pl.pallas_call(functools.partial(replay, steps, depth, width, size, block...  14.7 us
    ppermute x1, waiting for transfers between devices, shards(): low = lax.ppermute(jnp.concatenate(up), 'dom', forward)  9.81 us
    ppermute x1, starting transfers between devices, shards(): high = lax.ppermute(jnp.concatenate(down), 'dom', backward)  4.55 us
    ppermute x1, starting transfers between devices, shards(): low = lax.ppermute(jnp.concatenate(up), 'dom', forward)  3.4 us
    unnamed x16, local copies, waits for them, and re-layouts  3.24 us
    ppermute x1, starting transfers between devices, shards(): both = own + lax.ppermute(other, 'shot', pair)  1.92 us
    ppermute x1, waiting for transfers between devices, shards(): both = own + lax.ppermute(other, 'shot', pair)  1.88 us
  transfers between devices with their start and end apart: 3, of which 3 were waited for; matrix products, arithmetic and copies ran while one was open for 0% of the time, Pallas kernels for 0%

profile of v1, /device:TPU:8, one launch (start us, length us, event | category | flops | bytes accessed | tf_op | source)
XLA Modules:
  0.0 82.0 jit_solution(2347022782625366761)
XLA Ops:
  0.0 0.0 copy-start
  0.0 1.0 %bitcast_dynamic-update-slice_fusion.2 = (f32[18,64,128]{2,1,0:T(8,128)S(1)}, f32[18,64,128]{2,1,0:T(8,128)S(1)}) fusion(f32[1,16,64,128]{3,2,1,0:T(8,128)} %wave.1), kind=kLoop, calls=%fused_computation.2 | loop fusion | bytes 524288
  1.0 0.0 copy-start.2
  1.1 1.0 %bitcast_dynamic-update-slice_fusion.7 = (f32[18,64,128]{2,1,0:T(8,128)S(1)}, f32[18,64,128]{2,1,0:T(8,128)S(1)}) fusion(f32[18,64,128]{2,1,0:T(8,128)S(1)} %get-tuple-element.17, f32[1,16,64,128]{3,2,1,0:T(8,128)} %wave_old.1, f32[18,64,128]{2,1,0:T(8,128)S(1)} %get-tuple-element.18), kind=kLoop, calls=%fused_computation.7 | loop fusion | bytes 393216
  2.1 0.0 copy-done
  2.1 0.0 copy-start.3
  2.1 0.0 copy-start.1
  2.1 0.1 copy-done.2
  2.2 0.0 copy-start.5
  2.2 1.0 %bitcast_dynamic-update-slice_fusion.6 = (f32[18,64,128]{2,1,0:T(8,128)S(1)}, f32[18,64,128]{2,1,0:T(8,128)S(1)}) fusion(f32[18,64,128]{2,1,0:T(8,128)S(1)} %get-tuple-element.11, f32[1,16,64,128]{3,2,1,0:T(8,128)} %adj_old.1, f32[18,64,128]{2,1,0:T(8,128)S(1)} %get-tuple-element.12), kind=kLoop, calls=%fused_computation.6 | loop fusion | bytes 393216 | tf_op jit(solution)/shard_map/concatenate | solution.py:143
  3.3 3.4 %collective-permute-start = (f32[18,64,128]{2,1,0:T(8,128)S(1)}, f32[18,64,128]{2,1,0:T(8,128)S(1)}, u32[]{:S(2)}, u32[]{:S(2)}) collective-permute-start(f32[18,64,128]{2,1,0:T(8,128)S(1)} %get-tuple-element.10), channel_id=1, source_target_pairs={{0,1},{1,2},{2,3},{3,4},{4,5},{5,6},{6,7},{7,8},{8,9},{9,10},{10,1... | collective-permute-start | bytes 1769480 | tf_op jit(solution)/shard_map/ppermute | solution.py:142
  6.7 4.6 %collective-permute-start.1 = (f32[18,64,128]{2,1,0:T(8,128)S(1)}, f32[18,64,128]{2,1,0:T(8,128)S(1)}, u32[]{:S(2)}, u32[]{:S(2)}) collective-permute-start(f32[18,64,128]{2,1,0:T(8,128)S(1)} %get-tuple-element.9), channel_id=1, source_target_pairs={{1,0},{2,1},{3,2},{4,3},{5,4},{6,5},{7,6},{8,7},{9,8},{10,9},{11,1... | collective-permute-start | bytes 1769480 | tf_op jit(solution)/shard_map/ppermute | solution.py:143
  12.6 9.8 %collective-permute-done.low = f32[18,64,128]{2,1,0:T(8,128)S(1)} collective-permute-done((f32[18,64,128]{2,1,0:T(8,128)S(1)}, f32[18,64,128]{2,1,0:T(8,128)S(1)}, u32[]{:S(2)}, u32[]{:S(2)}) %collective-permute-start) | collective-permute-done | bytes 589856 | tf_op jit(solution)/shard_map/ppermute | solution.py:142
  22.4 1.2 %collective-permute-done.1.high = f32[18,64,128]{2,1,0:T(8,128)S(1)} collective-permute-done((f32[18,64,128]{2,1,0:T(8,128)S(1)}, f32[18,64,128]{2,1,0:T(8,128)S(1)}, u32[]{:S(2)}, u32[]{:S(2)}) %collective-permute-start.1) | collective-permute-done | bytes 589856 | tf_op jit(solution)/shard_map/ppermute | solution.py:143
  23.5 0.0 copy-done.3
  23.5 0.0 copy-done.1
  23.5 0.0 copy-done.5
  23.5 0.0 copy-start.4
  23.6 1.0 %copy-done.4 = f32[1,16,64,128]{3,2,1,0:T(8,128)S(1)} copy-done((f32[1,16,64,128]{3,2,1,0:T(8,128)S(1)}, f32[1,16,64,128]{3,2,1,0:T(8,128)}, u32[]{:S(2)}) %copy-start.4) | copy-done | bytes 524312
  24.6 14.7 %shard_map.82 = (f32[16,64,128]{2,1,0:T(8,128)S(1)}, f32[16,64,128]{2,1,0:T(8,128)S(1)}) custom-call(s32[1]{0:T(128)S(6)} %copy.17.offset, s32[1]{0:T(128)S(6)} %copy.18.count, f32[1,16,64,128]{3,2,1,0:T(8,128)S(1)} %copy-done, f32[1,16,64,128]{3,2,1,0:T(8,128)S(1)} %copy-done.1, f32[1,16,64,128]{3,2,1,0:T(8,128)S(1)} %copy-done.3, ...), custom_call_target="tpu_custom_call" | custom-call | tf_op jit(solution)/shard_map/pallas_call | solution.py:150
  39.3 1.9 %collective-permute-start.2 = (f32[16,64,128]{2,1,0:T(8,128)S(1)}, f32[16,64,128]{2,1,0:T(8,128)S(1)}, u32[]{:S(2)}, u32[]{:S(2)}) collective-permute-start(f32[16,64,128]{2,1,0:T(8,128)S(1)} %get-tuple-element.8), channel_id=1, source_target_pairs={{0,16},{16,0},{32,48},{48,32},{64,80},{80,64},{96,112},{112,96},{1... | collective-permute-start | bytes 1572872 | tf_op jit(solution)/shard_map/ppermute | solution.py:166
  41.3 1.9 %collective-permute-done.2 = f32[16,64,128]{2,1,0:T(8,128)S(1)} collective-permute-done((f32[16,64,128]{2,1,0:T(8,128)S(1)}, f32[16,64,128]{2,1,0:T(8,128)S(1)}, u32[]{:S(2)}, u32[]{:S(2)}) %collective-permute-start.2) | collective-permute-done | bytes 524320 | tf_op jit(solution)/shard_map/ppermute | solution.py:166
  43.2 0.1 add.3
  43.2 37.1 %all_to_all.5.parts = f32[16,64,128]{2,1,0:T(8,128)} all-to-all(f32[16,64,128]{2,1,0:T(8,128)S(1)} %add.3), channel_id=1, replica_groups={{0,32,64,96,128,160,192,224,256,288,320,352,384,416,448,480},{16,48,80,..., dimensions={0} | all-to-all | bytes 1048576 | tf_op jit(solution)/shard_map/all_to_all | solution.py:168
  80.3 1.7 %shard_map.83 = f32[64,128]{1,0:T(8,128)} custom-call(f32[16,64,128]{2,1,0:T(8,128)} %all_to_all.5.parts), custom_call_target="tpu_custom_call" | custom-call | tf_op jit(solution)/shard_map/pallas_call | solution.py:169
  (2 shorter events, 0.0 us)
Async XLA Ops:
  0.0 2.1 %copy-start = (f32[1,16,64,128]{3,2,1,0:T(8,128)S(1)}, f32[1,16,64,128]{3,2,1,0:T(8,128)}, u32[]{:S(2)}) copy-start(f32[1,16,64,128]{3,2,1,0:T(8,128)} %vel.1) | copy-start | bytes 1572868
  1.0 1.2 %copy-start.2 = (f32[1,16,64,128]{3,2,1,0:T(8,128)S(1)}, f32[1,16,64,128]{3,2,1,0:T(8,128)}, u32[]{:S(2)}) copy-start(f32[1,16,64,128]{3,2,1,0:T(8,128)} %adj.1) | copy-start | bytes 1572868
  2.1 21.5 %copy-start.3 = (f32[1,16,64,128]{3,2,1,0:T(8,128)S(1)}, f32[1,16,64,128]{3,2,1,0:T(8,128)}, u32[]{:S(2)}) copy-start(f32[1,16,64,128]{3,2,1,0:T(8,128)} %wave_old.1) | copy-start | bytes 1572868
  2.1 21.4 %copy-start.1 = (f32[1,16,64,128]{3,2,1,0:T(8,128)S(1)}, f32[1,16,64,128]{3,2,1,0:T(8,128)}, u32[]{:S(2)}) copy-start(f32[1,16,64,128]{3,2,1,0:T(8,128)} %wave.1) | copy-start | bytes 1572868
  2.2 21.3 %copy-start.5 = (f32[1,4,64,128]{3,2,1,0:T(8,128)S(1)}, f32[1,4,64,128]{3,2,1,0:T(8,128)}, u32[]{:S(2)}) copy-start(f32[1,4,64,128]{3,2,1,0:T(8,128)} %residuals.1) | copy-start | bytes 393220
  3.3 19.1 %collective-permute-start = (f32[18,64,128]{2,1,0:T(8,128)S(1)}, f32[18,64,128]{2,1,0:T(8,128)S(1)}, u32[]{:S(2)}, u32[]{:S(2)}) collective-permute-start(f32[18,64,128]{2,1,0:T(8,128)S(1)} %get-tuple-element.10), channel_id=1, source_target_pairs={{0,1},{1,2},{2,3},{3,4},{4,5},{5,6},{6,7},{7,8},{8,9},{9,10},{10,1... | collective-permute-start | bytes 1769480 | tf_op jit(solution)/shard_map/ppermute | solution.py:142
  6.7 16.8 %collective-permute-start.1 = (f32[18,64,128]{2,1,0:T(8,128)S(1)}, f32[18,64,128]{2,1,0:T(8,128)S(1)}, u32[]{:S(2)}, u32[]{:S(2)}) collective-permute-start(f32[18,64,128]{2,1,0:T(8,128)S(1)} %get-tuple-element.9), channel_id=1, source_target_pairs={{1,0},{2,1},{3,2},{4,3},{5,4},{6,5},{7,6},{8,7},{9,8},{10,9},{11,1... | collective-permute-start | bytes 1769480 | tf_op jit(solution)/shard_map/ppermute | solution.py:143
  23.5 1.0 %copy-start.4 = (f32[1,16,64,128]{3,2,1,0:T(8,128)S(1)}, f32[1,16,64,128]{3,2,1,0:T(8,128)}, u32[]{:S(2)}) copy-start(f32[1,16,64,128]{3,2,1,0:T(8,128)} %adj_old.1) | copy-start | bytes 1572868
  39.3 3.8 %collective-permute-start.2 = (f32[16,64,128]{2,1,0:T(8,128)S(1)}, f32[16,64,128]{2,1,0:T(8,128)S(1)}, u32[]{:S(2)}, u32[]{:S(2)}) collective-permute-start(f32[16,64,128]{2,1,0:T(8,128)S(1)} %get-tuple-element.8), channel_id=1, source_target_pairs={{0,16},{16,0},{32,48},{48,32},{64,80},{80,64},{96,112},{112,96},{1... | collective-permute-start | bytes 1572872 | tf_op jit(solution)/shard_map/ppermute | solution.py:166

commit v2 on v1

v2 whole, which is shorter than its diff:
```python
import functools

import jax
import jax.numpy as jnp
from jax import lax
from jax.experimental import pallas as pl
from jax.experimental.pallas import tpu as pltpu
from jax.sharding import PartitionSpec as P

PAD = 8
CHUNK = 2


class Lateral:
    def __init__(self, width, size):
        row = lax.broadcasted_iota(jnp.int32, (width, size), 0)
        column = lax.broadcasted_iota(jnp.int32, (width, size), 1)
        self.width, self.size = width, size
        self.top, self.bottom = row == 0, row == width - 1
        self.first, self.last = column == 0, column == size - 1

    def along(self, middle):
        left = jnp.where(self.first, 0.0, pltpu.roll(middle, 1, 1))
        right = jnp.where(self.last, 0.0, pltpu.roll(middle, self.size - 1, 1))
        return left + right

    def value(self, middle):
        above = jnp.where(self.top, 0.0, pltpu.roll(middle, 1, 0))
        below = jnp.where(self.bottom, 0.0, pltpu.roll(middle, self.width - 1, 0))
        return (above + below) + self.along(middle) - 6.0 * middle

    def plane(self, ref, z):
        middle = ref[z, PAD : PAD + self.width, :]
        total = ref[z, PAD - 1 : PAD - 1 + self.width, :] + ref[z, PAD + 1 : PAD + 1 + self.width, :]
        return total + self.along(middle) - 6.0 * middle, middle


def edges(steps, depth, vel, wave, wave_old, adj, adj_old, residuals, up, down):
    _, _, width, size = vel.shape
    lateral = Lateral(width, size).value
    source = jnp.where(lax.axis_index("dom") == 0, 1.0, 0.0)
    for out, top in ((down, False), (up, True)):
        at = [depth - 1 - k if top else k for k in range(steps)]
        v = [vel[0, z] for z in at]
        out[2 * steps] = v[0]
        out[2 * steps + 1] = v[1]
        now, old = [wave[0, z] for z in at], [wave_old[0, z] for z in at[:-1]]
        out[0] = now[0]
        for step in range(1, steps):
            new = []
            for k in range(steps - step):
                lap = lateral(now[k]) + now[k + 1]
                if k > 0:
                    lap = lap + now[k - 1]
                new.append(2.0 * now[k] - old[k] + v[k] * lap)
            now, old = new, now
            out[step] = now[0]
        now, old = [adj[0, z] for z in at], [adj_old[0, z] for z in at[:-1]]
        scaled = [c * q for c, q in zip(v, now)]
        out[steps] = scaled[0]
        for step in range(1, steps):
            new = []
            for k in range(steps - step):
                lap = lateral(scaled[k]) + scaled[k + 1]
                if k > 0:
                    lap = lap + scaled[k - 1]
                q = 2.0 * now[k] - old[k] + lap
                if k == 0 and not top:
                    q = q + source * residuals[0, step - 1]
                new.append(q)
            now, old = new, now
            scaled = [c * q for c, q in zip(v, now)]
            out[steps + step] = scaled[0]


def slab(steps, depth, *refs):
    vel, wave, wave_old, adj, adj_old, residuals = refs[:6]
    laps, adjoints, img = refs[6 : 6 + steps], refs[6 + steps : 6 + 2 * steps], refs[6 + 2 * steps]
    ps, ws = refs[7 + 2 * steps : 9 + 2 * steps], refs[9 + 2 * steps : 11 + 2 * steps]
    _, _, width, size = vel.shape
    lateral = Lateral(width, size).plane
    rows = slice(PAD, PAD + width)
    edge = jnp.zeros((depth + 2, PAD, size), jnp.float32)
    blank = jnp.zeros((width, size), jnp.float32)
    for ref in (*ps, *ws):
        ref[:, 0:PAD, :] = edge
        ref[:, PAD + width : 2 * PAD + width, :] = edge
        ref[0, rows, :] = blank
        ref[depth + 1, rows, :] = blank

    @pl.loop(0, depth)
    def _(z):
        ps[0][z + 1, rows, :] = wave[0, z]
        ws[0][z + 1, rows, :] = vel[0, z] * adj[0, z]

    surface = lax.axis_index("dom") == 0
    for step in range(steps):
        source, target = ws[step % 2], ws[(step + 1) % 2]
        now = (lambda z: adj[0, z]) if step == 0 else (lambda z, r=adjoints[step - 1]: r[z])
        old = (
            (lambda z: adj_old[0, z]) if step == 0
            else (lambda z: adj[0, z]) if step == 1
            else (lambda z, r=adjoints[step - 2]: r[z])
        )

        @pl.loop(0, depth, step=CHUNK)
        def _(begin):
            new = []
            for z in [begin + i for i in range(CHUNK)]:
                lap, _ = lateral(source, z + 1)
                lap = lap + (source[z, rows, :] + source[z + 2, rows, :])
                new.append(2.0 * now(z) - old(z) + lap)
            for i, q in enumerate(new):
                z = begin + i
                adjoints[step][z] = q
                if step < steps - 1:
                    target[z + 1, rows, :] = vel[0, z] * q

        @pl.when(surface)
        def _():
            q = adjoints[step][0] + residuals[0, step]
            adjoints[step][0] = q
            if step < steps - 1:
                target[1, rows, :] = vel[0, 0] * q

    for step in range(steps):
        source, target = ps[step % 2], ps[(step + 1) % 2]
        old = (lambda z: wave_old[0, z]) if step == 0 else (lambda z, r=target: r[z + 1, rows, :])

        @pl.loop(0, depth, step=CHUNK)
        def _(begin):
            new = []
            for z in [begin + i for i in range(CHUNK)]:
                lap, middle = lateral(source, z + 1)
                lap = lap + (source[z, rows, :] + source[z + 2, rows, :])
                term = lap * adjoints[steps - 1 - step][z]
                if step > 0:
                    term = term + img[z]
                field = 2.0 * middle - old(z) + vel[0, z] * lap if step < steps - 1 else None
                new.append((lap, term, field))
            for i, (lap, term, field) in enumerate(new):
                z = begin + i
                laps[step][z] = lap
                img[z] = term
                if field is not None:
                    target[z + 1, rows, :] = field


def finish(steps, depth, blocks, *refs):
    offset, count, vel, up, down, low, high = refs[:7]
    laps, adjoints, img = refs[7 : 7 + steps], refs[7 + steps : 7 + 2 * steps], refs[7 + 2 * steps]
    own, other, blocked = refs[8 + 2 * steps :]
    _, _, width, size = vel.shape
    lateral = Lateral(width, size).value
    span = width // blocks

    def store(z, plane):
        for j in range(blocks):
            blocked[j, z * span : (z + 1) * span, :] = plane[j * span : (j + 1) * span, :]

    for z in range(steps, depth - steps):
        store(z, img[z])

    for sent, got, top in ((down, low, False), (up, high, True)):
        at = [depth - 1 - k if top else k for k in range(steps)]
        here = [vel[0, z] for z in at]
        there = [got[2 * steps], got[2 * steps + 1]]

        def march(first, scale_field):
            f = [sent[first + n] for n in range(steps)]
            g = [got[first + n] for n in range(steps)]
            corrections, fields = [], []
            h_now, h_old, t_now, t_old = [], [], [], []
            for step in range(steps):
                if scale_field:
                    hs = [c * x for c, x in zip(here, h_now)]
                    ts = [c * x for c, x in zip(there, t_now)]
                else:
                    hs, ts = h_now, t_now
                laps_here = []
                for k in range(step + 1):
                    lap = g[step] if k == 0 else hs[k - 1]
                    if k == 0 and step > 0:
                        lap = lap + ts[0]
                    if k < len(hs):
                        lap = lap + lateral(hs[k])
                    if k + 1 < len(hs):
                        lap = lap + hs[k + 1]
                    laps_here.append(lap)
                corrections.append(laps_here)
                last = step == steps - 1
                new_h, new_t = [], []
                if scale_field or not last:
                    for k, lap in enumerate(laps_here):
                        x = lap if scale_field else here[k] * lap
                        if k < len(h_now):
                            x = x + 2.0 * h_now[k]
                        if k < len(h_old):
                            x = x - h_old[k]
                        new_h.append(x)
                if not last:
                    for k in range(min(step + 1, steps - 1 - step)):
                        lap = f[step] if k == 0 else ts[k - 1]
                        if k == 0 and step > 0:
                            lap = lap + hs[0]
                        if k < len(ts):
                            lap = lap + lateral(ts[k])
                        if k + 1 < len(ts):
                            lap = lap + ts[k + 1]
                        x = lap if scale_field else there[k] * lap
                        if k < len(t_now):
                            x = x + 2.0 * t_now[k]
                        if k < len(t_old):
                            x = x - t_old[k]
                        new_t.append(x)
                fields.append(new_h)
                h_now, h_old, t_now, t_old = new_h, h_now, new_t, t_now
            return corrections, fields

        more_laps, _ = march(0, False)
        _, more_adjoints = march(steps, True)
        for k, z in enumerate(at):
            total = None
            for n in range(steps):
                a = laps[n][z]
                if k < len(more_laps[n]):
                    a = a + more_laps[n][k]
                b = adjoints[steps - 1 - n][z]
                if k < len(more_adjoints[steps - 1 - n]):
                    b = b + more_adjoints[steps - 1 - n][k]
                total = a * b if total is None else total + a * b
            store(z, total)

    start, live = offset[0], count[0]
    odd = lax.rem(start + lax.axis_index("shot"), 2)
    zero = jnp.zeros((depth * span, size), jnp.float32)
    half = blocks // 2

    @pl.loop(0, half)
    def _(i):
        for ref, j in ((own, 2 * i + odd), (other, 2 * i + 1 - odd)):
            k = lax.div(start + j, 2)
            ref[k] = jnp.where(j < live, blocked[j], 0.0)
            ref[lax.rem(k + half, blocks)] = zero


def shards(vel, wave, wave_old, adj, adj_old, residuals, offset, count):
    _, depth, width, size = vel.shape
    steps = residuals.shape[1]
    shots, doms = lax.axis_size("shot"), lax.axis_size("dom")
    blocks = shots // 2
    span = width // blocks
    f32 = jnp.float32
    smem = pl.BlockSpec(memory_space=pltpu.SMEM)
    vmem = pl.BlockSpec(memory_space=pltpu.VMEM)
    room = pltpu.CompilerParams(vmem_limit_bytes=24 * 2**20)
    message = jax.ShapeDtypeStruct((2 * steps + 2, width, size), f32)
    field = jax.ShapeDtypeStruct((depth, width, size), f32)
    block = jax.ShapeDtypeStruct((blocks, depth * span, size), f32)

    up, down = pl.pallas_call(
        functools.partial(edges, steps, depth),
        out_shape=(message, message),
        in_specs=[vmem] * 6,
        out_specs=(vmem, vmem),
        compiler_params=room,
    )(vel, wave, wave_old, adj, adj_old, residuals)

    low = lax.ppermute(up, "dom", [(i, i + 1) for i in range(doms - 1)])
    high = lax.ppermute(down, "dom", [(i + 1, i) for i in range(doms - 1)])

    padded = pltpu.VMEM((depth + 2, width + 2 * PAD, size), f32)
    inner = pl.pallas_call(
        functools.partial(slab, steps, depth),
        out_shape=(field,) * (2 * steps + 1),
        in_specs=[vmem] * 6,
        out_specs=(vmem,) * (2 * steps + 1),
        scratch_shapes=[padded] * 4,
        cost_estimate=pl.CostEstimate(flops=40_000_000, bytes_accessed=16_000_000, transcendentals=0),
        compiler_params=room,
    )(vel, wave, wave_old, adj, adj_old, residuals)

    own, other = pl.pallas_call(
        functools.partial(finish, steps, depth, blocks),
        out_shape=(block, block),
        in_specs=[smem, smem] + [vmem] * (6 + 2 * steps),
        out_specs=(vmem, vmem),
        scratch_shapes=[pltpu.VMEM((blocks, depth * span, size), f32)],
        compiler_params=room,
    )(offset, count, vel, up, down, low, high, *inner)

    pair = [(s, s + 1 - 2 * (s % 2)) for s in range(shots)]
    both = own + lax.ppermute(other, "shot", pair)
    groups = [[2 * k + c for k in range(blocks)] for c in range(2)]
    parts = lax.all_to_all(both, "shot", 0, 0, tiled=True, axis_index_groups=groups)
    return jnp.sum(parts, axis=0).reshape(1, depth, span, size)


def solution(mesh):
    field = P("shot", "dom", None, None)
    placed = (field,) * 5 + (P("shot", None, None, None), P("shot"), P("shot"))
    return jax.shard_map(shards, mesh=mesh, in_specs=placed, out_specs=field, check_vma=False)
```

time: 82.3 us -> 66.3 us (0.81)
  waiting for transfers between devices: 12.9 us -> 1.88 us
  Pallas kernels: 16.4 us -> 8.98 us
  local copies, waits for them, and re-layouts: 4.27 us -> 6.11 us
    ppermute x2, waiting for transfers between devices: 11 us -> 0.01 us  [the longest x1 0.01 us: shards(): high = lax.ppermute(down, 'dom', [(i + 1, i) for i in range(doms - 1)])]
    pallas_call x2 -> x3, Pallas kernels: 16.4 us -> 8.98 us  [the longest x1 7.14 us: shards(): pl.pallas_call(functools.partial(slab, steps, depth), out_shape=(field,)...]
    unnamed x16 -> x12, local copies, waits for them, and re-layouts: 3.24 us -> 6.11 us
    concatenate x1 -> x0, local copies, waits for them, and re-layouts: 1.04 us -> none  [shards(): high = lax.ppermute(jnp.concatenate(down), 'dom', backward)]
  transfers between devices with their start and end apart: 3 -> 3, of which waited for: 3 -> 1; matrix products, arithmetic and copies ran while one was open for 0% -> 0% of each run, Pallas kernels for 0% -> 11%
where the time goes in v2:
time: 66.3 us; the launch traced here: 65.9 us
  blocking collectives  37 us (56%)
  starting transfers between devices  9.87 us (15%)
  Pallas kernels  8.98 us (14%)
  local copies, waits for them, and re-layouts  6.11 us (9%)
  waiting for transfers between devices  1.88 us (3%)
  between operations  1.37 us (2%)
  other arithmetic  0.73 us (1%)
    all_to_all x1, blocking collectives, shards(): lax.all_to_all(both, 'shot', 0, 0, tiled=True, axis_index_groups=groups)  37 us
    pallas_call x1, Pallas kernels, shards(): pl.pallas_call(functools.partial(slab, steps, depth), out_shape=(field,)...  7.14 us
    unnamed x12, local copies, waits for them, and re-layouts  6.11 us
    ppermute x1, starting transfers between devices, shards(): high = lax.ppermute(down, 'dom', [(i + 1, i) for i in range(doms - 1)])  4.55 us
    ppermute x1, starting transfers between devices, shards(): low = lax.ppermute(up, 'dom', [(i, i + 1) for i in range(doms - 1)])  3.4 us
    ppermute x1, starting transfers between devices, shards(): both = own + lax.ppermute(other, 'shot', pair)  1.92 us
    ppermute x1, waiting for transfers between devices, shards(): both = own + lax.ppermute(other, 'shot', pair)  1.88 us
  transfers between devices with their start and end apart: 3, of which 1 were waited for; matrix products, arithmetic and copies ran while one was open for 0% of the time, Pallas kernels for 11%

profile of v2, /device:TPU:8, one launch (start us, length us, event | category | flops | bytes accessed | tf_op | source)
XLA Modules:
  0.0 65.9 jit_solution(12423870084610168879)
XLA Ops:
  0.0 0.0 copy-start
  0.0 1.0 %copy-done = f32[1,16,64,128]{3,2,1,0:T(8,128)S(1)} copy-done((f32[1,16,64,128]{3,2,1,0:T(8,128)S(1)}, f32[1,16,64,128]{3,2,1,0:T(8,128)}, u32[]{:S(2)}) %copy-start) | copy-done | bytes 524312
  1.0 0.0 copy-start.1
  1.0 1.0 %copy-done.1 = f32[1,16,64,128]{3,2,1,0:T(8,128)S(1)} copy-done((f32[1,16,64,128]{3,2,1,0:T(8,128)S(1)}, f32[1,16,64,128]{3,2,1,0:T(8,128)}, u32[]{:S(2)}) %copy-start.1) | copy-done | bytes 524312
  2.1 0.0 copy-start.2
  2.1 1.0 %copy-done.2 = f32[1,16,64,128]{3,2,1,0:T(8,128)S(1)} copy-done((f32[1,16,64,128]{3,2,1,0:T(8,128)S(1)}, f32[1,16,64,128]{3,2,1,0:T(8,128)}, u32[]{:S(2)}) %copy-start.2) | copy-done | bytes 524312
  3.1 0.0 copy-start.3
  3.1 1.0 %copy-done.3 = f32[1,16,64,128]{3,2,1,0:T(8,128)S(1)} copy-done((f32[1,16,64,128]{3,2,1,0:T(8,128)S(1)}, f32[1,16,64,128]{3,2,1,0:T(8,128)}, u32[]{:S(2)}) %copy-start.3) | copy-done | bytes 524312
  4.2 0.0 copy-start.4
  4.2 1.0 %copy-done.4 = f32[1,16,64,128]{3,2,1,0:T(8,128)S(1)} copy-done((f32[1,16,64,128]{3,2,1,0:T(8,128)S(1)}, f32[1,16,64,128]{3,2,1,0:T(8,128)}, u32[]{:S(2)}) %copy-start.4) | copy-done | bytes 524312
  5.2 0.0 copy-start.5
  5.2 0.9 %copy-done.5 = f32[1,4,64,128]{3,2,1,0:T(8,128)S(1)} copy-done((f32[1,4,64,128]{3,2,1,0:T(8,128)S(1)}, f32[1,4,64,128]{3,2,1,0:T(8,128)}, u32[]{:S(2)}) %copy-start.5) | copy-done | bytes 131096
  6.1 0.7 %shard_map.82 = (f32[10,64,128]{2,1,0:T(8,128)S(1)}, f32[10,64,128]{2,1,0:T(8,128)S(1)}) custom-call(f32[1,16,64,128]{3,2,1,0:T(8,128)S(1)} %copy-done, f32[1,16,64,128]{3,2,1,0:T(8,128)S(1)} %copy-done.1, f32[1,16,64,128]{3,2,1,0:T(8,128)S(1)} %copy-done.2, f32[1,16,64,128]{3,2,1,0:T(8,128)S(1)} %copy-done.3, f32[1,16,64,128]{3,2,1,0:T(8,128)S(1)} %copy-done.4, ...), custom_call_target="tpu_custom_call" | custom-call | tf_op jit(solution)/shard_map/pallas_call | solution.py:261
  6.8 3.4 %collective-permute-start = (f32[10,64,128]{2,1,0:T(8,128)S(1)}, f32[10,64,128]{2,1,0:T(8,128)S(1)}, u32[]{:S(2)}, u32[]{:S(2)}) collective-permute-start(f32[10,64,128]{2,1,0:T(8,128)S(1)} %get-tuple-element.18.refs_3_), channel_id=1, source_target_pairs={{0,1},{1,2},{2,3},{3,4},{4,5},{5,6},{6,7},{7,8},{8,9},{9,10},{10,1... | collective-permute-start | bytes 983048 | tf_op jit(solution)/shard_map/ppermute | solution.py:269
  10.2 4.6 %collective-permute-start.1 = (f32[10,64,128]{2,1,0:T(8,128)S(1)}, f32[10,64,128]{2,1,0:T(8,128)S(1)}, u32[]{:S(2)}, u32[]{:S(2)}) collective-permute-start(f32[10,64,128]{2,1,0:T(8,128)S(1)} %get-tuple-element.19.refs_4_), channel_id=1, source_target_pairs={{1,0},{2,1},{3,2},{4,3},{5,4},{6,5},{7,6},{8,7},{9,8},{10,9},{11,1... | collective-permute-start | bytes 983048 | tf_op jit(solution)/shard_map/ppermute | solution.py:270
  16.1 7.1 %shard_map.83 = (f32[16,64,128]{2,1,0:T(8,128)S(1)}, f32[16,64,128]{2,1,0:T(8,128)S(1)}, f32[16,64,128]{2,1,0:T(8,128)S(1)}, f32[16,64,128]{2,1,0:T(8,128)S(1)},...) custom-call(f32[1,16,64,128]{3,2,1,0:T(8,128)S(1)} %copy-done, ...), custom_call_target="tpu_custom_call" | custom-call | flops 40000000 | bytes 16000000 | tf_op jit(solution)/shard_map/pallas_call | solution.py:273
  23.2 0.0 collective-permute-done.refs_5_
  23.2 0.0 collective-permute-done.1.refs_6_
  23.2 1.2 %shard_map.84 = (f32[16,64,128]{2,1,0:T(8,128)S(1)}, f32[16,64,128]{2,1,0:T(8,128)S(1)}) custom-call(s32[1]{0:T(128)S(6)} %copy.9.refs_0_, s32[1]{0:T(128)S(6)} %copy.10.refs_1_, f32[1,16,64,128]{3,2,1,0:T(8,128)S(1)} %copy-done, f32[10,64,128]{2,1,0:T(8,128)S(1)} %get-tuple-element.18.refs_3_, f32[10,64,128]{2,1,0:T(8,128)S(1)} %get-tuple-element.19.refs_4_, ...), custom_call_target="tpu_custom_call" | custom-call | tf_op jit(solution)/shard_map/pallas_call | solution.py:283
  24.4 1.9 %collective-permute-start.2 = (f32[16,64,128]{2,1,0:T(8,128)S(1)}, f32[16,64,128]{2,1,0:T(8,128)S(1)}, u32[]{:S(2)}, u32[]{:S(2)}) collective-permute-start(f32[16,64,128]{2,1,0:T(8,128)S(1)} %get-tuple-element.30), channel_id=1, source_target_pairs={{0,16},{16,0},{32,48},{48,32},{64,80},{80,64},{96,112},{112,96},{1... | collective-permute-start | bytes 1572872 | tf_op jit(solution)/shard_map/ppermute | solution.py:293
  26.3 1.9 %collective-permute-done.2 = f32[16,64,128]{2,1,0:T(8,128)S(1)} collective-permute-done((f32[16,64,128]{2,1,0:T(8,128)S(1)}, f32[16,64,128]{2,1,0:T(8,128)S(1)}, u32[]{:S(2)}, u32[]{:S(2)}) %collective-permute-start.2) | collective-permute-done | bytes 524320 | tf_op jit(solution)/shard_map/ppermute | solution.py:293
  28.2 0.1 add.3
  28.3 37.0 %all_to_all.5 = f32[16,64,128]{2,1,0:T(8,128)S(1)} all-to-all(f32[16,64,128]{2,1,0:T(8,128)S(1)} %add.3), channel_id=1, replica_groups={{0,32,64,96,128,160,192,224,256,288,320,352,384,416,448,480},{16,48,80,..., dimensions={0} | all-to-all | bytes 1048576 | tf_op jit(solution)/shard_map/all_to_all | solution.py:295
  65.2 0.6 reduce_sum.9
Async XLA Ops:
  0.0 1.0 %copy-start = (f32[1,16,64,128]{3,2,1,0:T(8,128)S(1)}, f32[1,16,64,128]{3,2,1,0:T(8,128)}, u32[]{:S(2)}) copy-start(f32[1,16,64,128]{3,2,1,0:T(8,128)} %refs_2_.3) | copy-start | bytes 1572868
  1.0 1.0 %copy-start.1 = (f32[1,16,64,128]{3,2,1,0:T(8,128)S(1)}, f32[1,16,64,128]{3,2,1,0:T(8,128)}, u32[]{:S(2)}) copy-start(f32[1,16,64,128]{3,2,1,0:T(8,128)} %refs_1_.2) | copy-start | bytes 1572868
  2.1 1.0 %copy-start.2 = (f32[1,16,64,128]{3,2,1,0:T(8,128)S(1)}, f32[1,16,64,128]{3,2,1,0:T(8,128)}, u32[]{:S(2)}) copy-start(f32[1,16,64,128]{3,2,1,0:T(8,128)} %refs_2_.2) | copy-start | bytes 1572868
  3.1 1.0 %copy-start.3 = (f32[1,16,64,128]{3,2,1,0:T(8,128)S(1)}, f32[1,16,64,128]{3,2,1,0:T(8,128)}, u32[]{:S(2)}) copy-start(f32[1,16,64,128]{3,2,1,0:T(8,128)} %refs_3_.1) | copy-start | bytes 1572868
  4.2 1.0 %copy-start.4 = (f32[1,16,64,128]{3,2,1,0:T(8,128)S(1)}, f32[1,16,64,128]{3,2,1,0:T(8,128)}, u32[]{:S(2)}) copy-start(f32[1,16,64,128]{3,2,1,0:T(8,128)} %refs_4_.1) | copy-start | bytes 1572868
  5.2 0.9 %copy-start.5 = (f32[1,4,64,128]{3,2,1,0:T(8,128)S(1)}, f32[1,4,64,128]{3,2,1,0:T(8,128)}, u32[]{:S(2)}) copy-start(f32[1,4,64,128]{3,2,1,0:T(8,128)} %refs_5_.1) | copy-start | bytes 393220
  6.8 16.4 %collective-permute-start = (f32[10,64,128]{2,1,0:T(8,128)S(1)}, f32[10,64,128]{2,1,0:T(8,128)S(1)}, u32[]{:S(2)}, u32[]{:S(2)}) collective-permute-start(f32[10,64,128]{2,1,0:T(8,128)S(1)} %get-tuple-element.18.refs_3_), channel_id=1, source_target_pairs={{0,1},{1,2},{2,3},{3,4},{4,5},{5,6},{6,7},{7,8},{8,9},{9,10},{10,1... | collective-permute-start | bytes 983048 | tf_op jit(solution)/shard_map/ppermute | solution.py:269
  10.2 13.0 %collective-permute-start.1 = (f32[10,64,128]{2,1,0:T(8,128)S(1)}, f32[10,64,128]{2,1,0:T(8,128)S(1)}, u32[]{:S(2)}, u32[]{:S(2)}) collective-permute-start(f32[10,64,128]{2,1,0:T(8,128)S(1)} %get-tuple-element.19.refs_4_), channel_id=1, source_target_pairs={{1,0},{2,1},{3,2},{4,3},{5,4},{6,5},{7,6},{8,7},{9,8},{10,9},{11,1... | collective-permute-start | bytes 983048 | tf_op jit(solution)/shard_map/ppermute | solution.py:270
  24.4 3.8 %collective-permute-start.2 = (f32[16,64,128]{2,1,0:T(8,128)S(1)}, f32[16,64,128]{2,1,0:T(8,128)S(1)}, u32[]{:S(2)}, u32[]{:S(2)}) collective-permute-start(f32[16,64,128]{2,1,0:T(8,128)S(1)} %get-tuple-element.30), channel_id=1, source_target_pairs={{0,16},{16,0},{32,48},{48,32},{64,80},{80,64},{96,112},{112,96},{1... | collective-permute-start | bytes 1572872 | tf_op jit(solution)/shard_map/ppermute | solution.py:293

commit v3 on v2

--- a/solution.py
+++ b/solution.py
@@ -7,7 +7,6 @@
 from jax.experimental.pallas import tpu as pltpu
 from jax.sharding import PartitionSpec as P
 
-PAD = 8
 CHUNK = 2
 
 
@@ -19,32 +18,36 @@
         self.top, self.bottom = row == 0, row == width - 1
         self.first, self.last = column == 0, column == size - 1
 
-    def along(self, middle):
+    def __call__(self, middle):
+        above = jnp.where(self.top, 0.0, pltpu.roll(middle, 1, 0))
+        below = jnp.where(self.bottom, 0.0, pltpu.roll(middle, self.width - 1, 0))
         left = jnp.where(self.first, 0.0, pltpu.roll(middle, 1, 1))
         right = jnp.where(self.last, 0.0, pltpu.roll(middle, self.size - 1, 1))
-        return left + right
-
-    def value(self, middle):
-        above = jnp.where(self.top, 0.0, pltpu.roll(middle, 1, 0))
-        below = jnp.where(self.bottom, 0.0, pltpu.roll(middle, self.width - 1, 0))
-        return (above + below) + self.along(middle) - 6.0 * middle
-
-    def plane(self, ref, z):
-        middle = ref[z, PAD : PAD + self.width, :]
-        total = ref[z, PAD - 1 : PAD - 1 + self.width, :] + ref[z, PAD + 1 : PAD + 1 + self.width, :]
-        return total + self.along(middle) - 6.0 * middle, middle
-
-
-def edges(steps, depth, vel, wave, wave_old, adj, adj_old, residuals, up, down):
+        return (above + below) + (left + right) - 6.0 * middle
+
+
+def edges(steps, depth, vel, wave, wave_old, adj, adj_old, residuals, up, down, *scratch):
     _, _, width, size = vel.shape
-    lateral = Lateral(width, size).value
+    lateral = Lateral(width, size)
+    fetched, first_residuals, sems, sem = scratch[:5], scratch[5], scratch[6], scratch[7]
+    copies = []
+    for i, (ref, held) in enumerate(zip((vel, wave, wave_old, adj, adj_old), fetched)):
+        for side, begin in enumerate((0, depth - steps)):
+            copies.append(pltpu.make_async_copy(ref.at[0, pl.ds(begin, steps)], held.at[side], sems.at[i, side]))
+    copies.append(pltpu.make_async_copy(residuals.at[0], first_residuals, sem))
+    for copy in copies:
+        copy.start()
+    for copy in copies:
+        copy.wait()
+    vel, wave, wave_old, adj, adj_old = fetched
     source = jnp.where(lax.axis_index("dom") == 0, 1.0, 0.0)
     for out, top in ((down, False), (up, True)):
-        at = [depth - 1 - k if top else k for k in range(steps)]
-        v = [vel[0, z] for z in at]
+        side = int(top)
+        at = [steps - 1 - k if top else k for k in range(steps)]
+        v = [vel[side, z] for z in at]
         out[2 * steps] = v[0]
         out[2 * steps + 1] = v[1]
-        now, old = [wave[0, z] for z in at], [wave_old[0, z] for z in at[:-1]]
+        now, old = [wave[side, z] for z in at], [wave_old[side, z] for z in at[:-1]]
         out[0] = now[0]
         for step in range(1, steps):
             new = []
@@ -55,7 +58,7 @@
                 new.append(2.0 * now[k] - old[k] + v[k] * lap)
             now, old = new, now
             out[step] = now[0]
-        now, old = [adj[0, z] for z in at], [adj_old[0, z] for z in at[:-1]]
+        now, old = [adj[side, z] for z in at], [adj_old[side, z] for z in at[:-1]]
         scaled = [c * q for c, q in zip(v, now)]
         out[steps] = scaled[0]
         for step in range(1, steps):
@@ -66,7 +69,7 @@
                     lap = lap + scaled[k - 1]
                 q = 2.0 * now[k] - old[k] + lap
                 if k == 0 and not top:
-                    q = q + source * residuals[0, step - 1]
+                    q = q + source * first_residuals[step - 1]
                 new.append(q)
             now, old = new, now
             scaled = [c * q for c, q in zip(v, now)]
@@ -74,84 +77,81 @@
 
 
 def slab(steps, depth, *refs):
-    vel, wave, wave_old, adj, adj_old, residuals = refs[:6]
-    laps, adjoints, img = refs[6 : 6 + steps], refs[6 + steps : 6 + 2 * steps], refs[6 + 2 * steps]
-    ps, ws = refs[7 + 2 * steps : 9 + 2 * steps], refs[9 + 2 * steps : 11 + 2 * steps]
-    _, _, width, size = vel.shape
-    lateral = Lateral(width, size).plane
-    rows = slice(PAD, PAD + width)
-    edge = jnp.zeros((depth + 2, PAD, size), jnp.float32)
+    vel, wave, wave_old, adj, adj_old, residuals = [ref.at[0] for ref in refs[:6]]
+    refs = refs[6:]
+    laps, adjoints, img = refs[:steps], refs[steps : 2 * steps], refs[2 * steps]
+    refs = refs[2 * steps + 1 :]
+    ps, ws = refs[:2], refs[2:]
+    _, width, size = vel.shape
+    lateral = Lateral(width, size)
     blank = jnp.zeros((width, size), jnp.float32)
     for ref in (*ps, *ws):
-        ref[:, 0:PAD, :] = edge
-        ref[:, PAD + width : 2 * PAD + width, :] = edge
-        ref[0, rows, :] = blank
-        ref[depth + 1, rows, :] = blank
-
-    @pl.loop(0, depth)
-    def _(z):
-        ps[0][z + 1, rows, :] = wave[0, z]
-        ws[0][z + 1, rows, :] = vel[0, z] * adj[0, z]
+        ref[0] = blank
+        ref[depth + 1] = blank
+
+    @pl.loop(0, depth, step=CHUNK)
+    def _(begin):
+        for z in [begin + i for i in range(CHUNK)]:
+            ps[0][z + 1] = wave[z]
+            ws[0][z + 1] = vel[z] * adj[z]
 
     surface = lax.axis_index("dom") == 0
+    fields = (adj_old, adj, *adjoints)
     for step in range(steps):
         source, target = ws[step % 2], ws[(step + 1) % 2]
-        now = (lambda z: adj[0, z]) if step == 0 else (lambda z, r=adjoints[step - 1]: r[z])
-        old = (
-            (lambda z: adj_old[0, z]) if step == 0
-            else (lambda z: adj[0, z]) if step == 1
-            else (lambda z, r=adjoints[step - 2]: r[z])
-        )
+        old, now, new_field = fields[step : step + 3]
 
         @pl.loop(0, depth, step=CHUNK)
         def _(begin):
             new = []
             for z in [begin + i for i in range(CHUNK)]:
-                lap, _ = lateral(source, z + 1)
-                lap = lap + (source[z, rows, :] + source[z + 2, rows, :])
-                new.append(2.0 * now(z) - old(z) + lap)
+                lap = lateral(source[z + 1]) + (source[z] + source[z + 2])
+                new.append(2.0 * now[z] - old[z] + lap)
             for i, q in enumerate(new):
-                z = begin + i
-                adjoints[step][z] = q
-                if step < steps - 1:
-                    target[z + 1, rows, :] = vel[0, z] * q
+                new_field[begin + i] = q
+            if step < steps - 1:
+                scaled = [vel[begin + i] * q for i, q in enumerate(new)]
+                for i, w in enumerate(scaled):
+                    target[begin + i + 1] = w
 
         @pl.when(surface)
         def _():
-            q = adjoints[step][0] + residuals[0, step]
-            adjoints[step][0] = q
+            q = new_field[0] + residuals[step]
+            new_field[0] = q
             if step < steps - 1:
-                target[1, rows, :] = vel[0, 0] * q
+                target[1] = vel[0] * q
 
     for step in range(steps):
         source, target = ps[step % 2], ps[(step + 1) % 2]
-        old = (lambda z: wave_old[0, z]) if step == 0 else (lambda z, r=target: r[z + 1, rows, :])
 
         @pl.loop(0, depth, step=CHUNK)
         def _(begin):
             new = []
             for z in [begin + i for i in range(CHUNK)]:
-                lap, middle = lateral(source, z + 1)
-                lap = lap + (source[z, rows, :] + source[z + 2, rows, :])
+                middle = source[z + 1]
+                lap = lateral(middle) + (source[z] + source[z + 2])
                 term = lap * adjoints[steps - 1 - step][z]
                 if step > 0:
                     term = term + img[z]
-                field = 2.0 * middle - old(z) + vel[0, z] * lap if step < steps - 1 else None
+                field = None
+                if step < steps - 1:
+                    old = wave_old[z] if step == 0 else target[z + 1]
+                    field = 2.0 * middle - old + vel[z] * lap
                 new.append((lap, term, field))
             for i, (lap, term, field) in enumerate(new):
-                z = begin + i
-                laps[step][z] = lap
-                img[z] = term
+                laps[step][begin + i] = lap
+                img[begin + i] = term
                 if field is not None:
-                    target[z + 1, rows, :] = field
+                    target[begin + i + 1] = field
 
 
 def finish(steps, depth, blocks, *refs):
     offset, count, vel, up, down, low, high = refs[:7]
+    vel = vel.at[0]
     laps, adjoints, img = refs[7 : 7 + steps], refs[7 + steps : 7 + 2 * steps], refs[7 + 2 * steps]
     own, other, blocked = refs[8 + 2 * steps :]
-    _, _, width, size = vel.shape
-    lateral = Lateral(width, size).value
+    _, width, size = vel.shape
+    lateral = Lateral(width, size)
     span = width // blocks
 
     def store(z, plane):
@@ -163,7 +163,7 @@
 
     for sent, got, top in ((down, low, False), (up, high, True)):
         at = [depth - 1 - k if top else k for k in range(steps)]
-        here = [vel[0, z] for z in at]
+        here = [vel[z] for z in at]
         there = [got[2 * steps], got[2 * steps + 1]]
 
         def march(first, scale_field):
@@ -251,6 +251,7 @@
     blocks = shots // 2
     span = width // blocks
     f32 = jnp.float32
+    hbm = pl.BlockSpec(memory_space=pltpu.HBM)
     smem = pl.BlockSpec(memory_space=pltpu.SMEM)
     vmem = pl.BlockSpec(memory_space=pltpu.VMEM)
     room = pltpu.CompilerParams(vmem_limit_bytes=24 * 2**20)
@@ -261,21 +262,22 @@
     up, down = pl.pallas_call(
         functools.partial(edges, steps, depth),
         out_shape=(message, message),
-        in_specs=[vmem] * 6,
+        in_specs=[hbm] * 6,
         out_specs=(vmem, vmem),
-        compiler_params=room,
+        scratch_shapes=[pltpu.VMEM((2, steps, width, size), f32)] * 5
+        + [pltpu.VMEM((steps, width, size), f32), pltpu.SemaphoreType.DMA((5, 2)), pltpu.SemaphoreType.DMA],
+        compiler_params=pltpu.CompilerParams(vmem_limit_bytes=60 * 2**20),
     )(vel, wave, wave_old, adj, adj_old, residuals)
 
     low = lax.ppermute(up, "dom", [(i, i + 1) for i in range(doms - 1)])
     high = lax.ppermute(down, "dom", [(i + 1, i) for i in range(doms - 1)])
 
-    padded = pltpu.VMEM((depth + 2, width + 2 * PAD, size), f32)
     inner = pl.pallas_call(
         functools.partial(slab, steps, depth),
         out_shape=(field,) * (2 * steps + 1),
         in_specs=[vmem] * 6,
         out_specs=(vmem,) * (2 * steps + 1),
-        scratch_shapes=[padded] * 4,
+        scratch_shapes=[pltpu.VMEM((depth + 2, width, size), f32)] * 4,
         cost_estimate=pl.CostEstimate(flops=40_000_000, bytes_accessed=16_000_000, transcendentals=0),
         compiler_params=room,
     )(vel, wave, wave_old, adj, adj_old, residuals)

time: 66.3 us -> 62.4 us (0.941)
  local copies, waits for them, and re-layouts: 6.11 us -> 0.03 us
  Pallas kernels: 8.98 us -> 11.3 us
    unnamed x12 -> x16, local copies, waits for them, and re-layouts: 6.11 us -> 0.03 us
    pallas_call x1, Pallas kernels: 0.68 us -> 3.07 us  [shards(): pl.pallas_call(functools.partial(edges, steps, depth), out_shape=(message...]
where the time goes in v3:
time: 62.4 us; the launch traced here: 62.2 us
  blocking collectives  37 us (59%)
  Pallas kernels  11.3 us (18%)
  starting transfers between devices  9.87 us (16%)
  waiting for transfers between devices  1.88 us (3%)
  between operations  1.47 us (2%)
  other arithmetic  0.7 us (1%)
    all_to_all x1, blocking collectives, shards(): lax.all_to_all(both, 'shot', 0, 0, tiled=True, axis_index_groups=groups)  37 us
    pallas_call x1, Pallas kernels, shards(): pl.pallas_call(functools.partial(slab, steps, depth), out_shape=(field,)...  7.05 us
    ppermute x1, starting transfers between devices, shards(): high = lax.ppermute(down, 'dom', [(i + 1, i) for i in range(doms - 1)])  4.55 us
    ppermute x1, starting transfers between devices, shards(): low = lax.ppermute(up, 'dom', [(i, i + 1) for i in range(doms - 1)])  3.4 us
    pallas_call x1, Pallas kernels, shards(): pl.pallas_call(functools.partial(edges, steps, depth), out_shape=(message...  3.07 us
    ppermute x1, starting transfers between devices, shards(): both = own + lax.ppermute(other, 'shot', pair)  1.92 us
    ppermute x1, waiting for transfers between devices, shards(): both = own + lax.ppermute(other, 'shot', pair)  1.88 us
  transfers between devices with their start and end apart: 3, of which 1 were waited for; matrix products, arithmetic and copies ran while one was open for 0% of the time, Pallas kernels for 11%

profile of v3, /device:TPU:8, one launch (start us, length us, event | category | flops | bytes accessed | tf_op | source)
XLA Modules:
  0.0 62.2 jit_solution(14839132197392402341)
XLA Ops:
  0.0 0.0 copy-start
  0.0 0.0 copy-start.5
  0.0 0.0 copy-start.4
  0.0 0.0 copy-start.3
  0.0 0.0 copy-start.2
  0.0 0.0 copy-start.1
  0.0 3.1 %shard_map.82 = (f32[10,64,128]{2,1,0:T(8,128)}, f32[10,64,128]{2,1,0:T(8,128)}) custom-call(f32[1,16,64,128]{3,2,1,0:T(8,128)} %refs_2_.3, f32[1,16,64,128]{3,2,1,0:T(8,128)} %refs_1_.2, f32[1,16,64,128]{3,2,1,0:T(8,128)} %refs_2_.2, f32[1,16,64,128]{3,2,1,0:T(8,128)} %refs_3_.1, f32[1,16,64,128]{3,2,1,0:T(8,128)} %refs_4_.1, f32[1,4,64,128]{3,2,1,0:T(8,128)} %refs_5_.1), custom_call_target="tpu_custom_call" | custom-call | tf_op jit(solution)/shard_map/pallas_call | solution.py:262
  3.1 3.4 %collective-permute-start = (f32[10,64,128]{2,1,0:T(8,128)}, f32[10,64,128]{2,1,0:T(8,128)S(1)}, u32[]{:S(2)}, u32[]{:S(2)}) collective-permute-start(f32[10,64,128]{2,1,0:T(8,128)} %get-tuple-element.18.refs_3_), channel_id=1, source_target_pairs={{0,1},{1,2},{2,3},{3,4},{4,5},{5,6},{6,7},{7,8},{8,9},{9,10},{10,1... | collective-permute-start | bytes 983048 | tf_op jit(solution)/shard_map/ppermute | solution.py:272
  6.5 4.6 %collective-permute-start.1 = (f32[10,64,128]{2,1,0:T(8,128)}, f32[10,64,128]{2,1,0:T(8,128)S(1)}, u32[]{:S(2)}, u32[]{:S(2)}) collective-permute-start(f32[10,64,128]{2,1,0:T(8,128)} %get-tuple-element.19.refs_4_), channel_id=1, source_target_pairs={{1,0},{2,1},{3,2},{4,3},{5,4},{6,5},{7,6},{8,7},{9,8},{10,9},{11,1... | collective-permute-start | bytes 983048 | tf_op jit(solution)/shard_map/ppermute | solution.py:273
  12.4 0.0 copy-done
  12.4 0.0 copy-done.5
  12.4 0.0 copy-done.4
  12.4 0.0 copy-done.3
  12.4 0.0 copy-done.2
  12.4 0.0 copy-done.1
  12.4 0.0 copy-start.6
  12.4 0.0 copy-start.7
  12.5 7.1 %shard_map.83 = (f32[16,64,128]{2,1,0:T(8,128)S(1)}, f32[16,64,128]{2,1,0:T(8,128)S(1)}, f32[16,64,128]{2,1,0:T(8,128)S(1)}, f32[16,64,128]{2,1,0:T(8,128)S(1)},...) custom-call(f32[1,16,64,128]{3,2,1,0:T(8,128)S(1)} %copy-done, ...), custom_call_target="tpu_custom_call" | custom-call | flops 40000000 | bytes 16000000 | tf_op jit(solution)/shard_map/pallas_call | solution.py:275
  19.5 0.0 collective-permute-done.refs_5_
  19.5 0.0 collective-permute-done.1.refs_6_
  19.5 0.0 copy-done.6
  19.6 0.0 copy-done.7
  19.6 1.2 %shard_map.84 = (f32[16,64,128]{2,1,0:T(8,128)S(1)}, f32[16,64,128]{2,1,0:T(8,128)S(1)}) custom-call(s32[1]{0:T(128)S(6)} %copy.9.refs_0_, s32[1]{0:T(128)S(6)} %copy.10.refs_1_, f32[1,16,64,128]{3,2,1,0:T(8,128)S(1)} %copy-done, f32[10,64,128]{2,1,0:T(8,128)S(1)} %copy-done.6, f32[10,64,128]{2,1,0:T(8,128)S(1)} %copy-done.7, ...), custom_call_target="tpu_custom_call" | custom-call | tf_op jit(solution)/shard_map/pallas_call | solution.py:285
  20.7 1.9 %collective-permute-start.2 = (f32[16,64,128]{2,1,0:T(8,128)S(1)}, f32[16,64,128]{2,1,0:T(8,128)S(1)}, u32[]{:S(2)}, u32[]{:S(2)}) collective-permute-start(f32[16,64,128]{2,1,0:T(8,128)S(1)} %get-tuple-element.30), channel_id=1, source_target_pairs={{0,16},{16,0},{32,48},{48,32},{64,80},{80,64},{96,112},{112,96},{1... | collective-permute-start | bytes 1572872 | tf_op jit(solution)/shard_map/ppermute | solution.py:295
  22.7 1.9 %collective-permute-done.2 = f32[16,64,128]{2,1,0:T(8,128)S(1)} collective-permute-done((f32[16,64,128]{2,1,0:T(8,128)S(1)}, f32[16,64,128]{2,1,0:T(8,128)S(1)}, u32[]{:S(2)}, u32[]{:S(2)}) %collective-permute-start.2) | collective-permute-done | bytes 524320 | tf_op jit(solution)/shard_map/ppermute | solution.py:295
  24.5 0.1 add.3
  24.6 37.0 %all_to_all.5 = f32[16,64,128]{2,1,0:T(8,128)S(1)} all-to-all(f32[16,64,128]{2,1,0:T(8,128)S(1)} %add.3), channel_id=1, replica_groups={{0,32,64,96,128,160,192,224,256,288,320,352,384,416,448,480},{16,48,80,..., dimensions={0} | all-to-all | bytes 1048576 | tf_op jit(solution)/shard_map/all_to_all | solution.py:297
  61.5 0.6 %reduce_sum.9 = f32[64,128]{1,0:T(8,128)} reduce(f32[16,64,128]{2,1,0:T(8,128)S(1)} %all_to_all.5, f32[]{:T(128)} %constant.0.clone.1), dimensions={0}, to_apply=%region_0.0 | reduce | flops 122880 | bytes 557060 | tf_op jit(solution)/shard_map/reduce_sum | solution.py:298
Async XLA Ops:
  0.0 12.4 %copy-start = (f32[1,16,64,128]{3,2,1,0:T(8,128)S(1)}, f32[1,16,64,128]{3,2,1,0:T(8,128)}, u32[]{:S(2)}) copy-start(f32[1,16,64,128]{3,2,1,0:T(8,128)} %refs_2_.3) | copy-start | bytes 1572868
  0.0 12.4 %copy-start.5 = (f32[1,4,64,128]{3,2,1,0:T(8,128)S(1)}, f32[1,4,64,128]{3,2,1,0:T(8,128)}, u32[]{:S(2)}) copy-start(f32[1,4,64,128]{3,2,1,0:T(8,128)} %refs_5_.1) | copy-start | bytes 393220
  0.0 12.4 %copy-start.4 = (f32[1,16,64,128]{3,2,1,0:T(8,128)S(1)}, f32[1,16,64,128]{3,2,1,0:T(8,128)}, u32[]{:S(2)}) copy-start(f32[1,16,64,128]{3,2,1,0:T(8,128)} %refs_4_.1) | copy-start | bytes 1572868
  0.0 12.4 %copy-start.3 = (f32[1,16,64,128]{3,2,1,0:T(8,128)S(1)}, f32[1,16,64,128]{3,2,1,0:T(8,128)}, u32[]{:S(2)}) copy-start(f32[1,16,64,128]{3,2,1,0:T(8,128)} %refs_3_.1) | copy-start | bytes 1572868
  0.0 12.4 %copy-start.2 = (f32[1,16,64,128]{3,2,1,0:T(8,128)S(1)}, f32[1,16,64,128]{3,2,1,0:T(8,128)}, u32[]{:S(2)}) copy-start(f32[1,16,64,128]{3,2,1,0:T(8,128)} %refs_2_.2) | copy-start | bytes 1572868
  0.0 12.4 %copy-start.1 = (f32[1,16,64,128]{3,2,1,0:T(8,128)S(1)}, f32[1,16,64,128]{3,2,1,0:T(8,128)}, u32[]{:S(2)}) copy-start(f32[1,16,64,128]{3,2,1,0:T(8,128)} %refs_1_.2) | copy-start | bytes 1572868
  3.1 16.4 %collective-permute-start = (f32[10,64,128]{2,1,0:T(8,128)}, f32[10,64,128]{2,1,0:T(8,128)S(1)}, u32[]{:S(2)}, u32[]{:S(2)}) collective-permute-start(f32[10,64,128]{2,1,0:T(8,128)} %get-tuple-element.18.refs_3_), channel_id=1, source_target_pairs={{0,1},{1,2},{2,3},{3,4},{4,5},{5,6},{6,7},{7,8},{8,9},{9,10},{10,1... | collective-permute-start | bytes 983048 | tf_op jit(solution)/shard_map/ppermute | solution.py:272
  6.5 13.0 %collective-permute-start.1 = (f32[10,64,128]{2,1,0:T(8,128)}, f32[10,64,128]{2,1,0:T(8,128)S(1)}, u32[]{:S(2)}, u32[]{:S(2)}) collective-permute-start(f32[10,64,128]{2,1,0:T(8,128)} %get-tuple-element.19.refs_4_), channel_id=1, source_target_pairs={{1,0},{2,1},{3,2},{4,3},{5,4},{6,5},{7,6},{8,7},{9,8},{10,9},{11,1... | collective-permute-start | bytes 983048 | tf_op jit(solution)/shard_map/ppermute | solution.py:273
  12.4 7.1 %copy-start.6 = (f32[10,64,128]{2,1,0:T(8,128)S(1)}, f32[10,64,128]{2,1,0:T(8,128)}, u32[]{:S(2)}) copy-start(f32[10,64,128]{2,1,0:T(8,128)} %get-tuple-element.18.refs_3_) | copy-start | bytes 983044
  12.4 7.1 %copy-start.7 = (f32[10,64,128]{2,1,0:T(8,128)S(1)}, f32[10,64,128]{2,1,0:T(8,128)}, u32[]{:S(2)}) copy-start(f32[10,64,128]{2,1,0:T(8,128)} %get-tuple-element.19.refs_4_) | copy-start | bytes 983044
  20.7 3.8 %collective-permute-start.2 = (f32[16,64,128]{2,1,0:T(8,128)S(1)}, f32[16,64,128]{2,1,0:T(8,128)S(1)}, u32[]{:S(2)}, u32[]{:S(2)}) collective-permute-start(f32[16,64,128]{2,1,0:T(8,128)S(1)} %get-tuple-element.30), channel_id=1, source_target_pairs={{0,16},{16,0},{32,48},{48,32},{64,80},{80,64},{96,112},{112,96},{1... | collective-permute-start | bytes 1572872 | tf_op jit(solution)/shard_map/ppermute | solution.py:295

commit v4 on v3

--- a/solution.py
+++ b/solution.py
@@ -6,8 +6,6 @@
 from jax.experimental import pallas as pl
 from jax.experimental.pallas import tpu as pltpu
 from jax.sharding import PartitionSpec as P
-
-CHUNK = 2
 
 
 class Lateral:
@@ -26,21 +24,19 @@
         return (above + below) + (left + right) - 6.0 * middle
 
 
-def edges(steps, depth, vel, wave, wave_old, adj, adj_old, residuals, up, down, *scratch):
+def edges(steps, depth, vel, wave, wave_old, adj, adj_old, up, down, *scratch):
     _, _, width, size = vel.shape
     lateral = Lateral(width, size)
-    fetched, first_residuals, sems, sem = scratch[:5], scratch[5], scratch[6], scratch[7]
+    fetched, sems = scratch[:5], scratch[5]
     copies = []
     for i, (ref, held) in enumerate(zip((vel, wave, wave_old, adj, adj_old), fetched)):
         for side, begin in enumerate((0, depth - steps)):
             copies.append(pltpu.make_async_copy(ref.at[0, pl.ds(begin, steps)], held.at[side], sems.at[i, side]))
-    copies.append(pltpu.make_async_copy(residuals.at[0], first_residuals, sem))
     for copy in copies:
         copy.start()
     for copy in copies:
         copy.wait()
     vel, wave, wave_old, adj, adj_old = fetched
-    source = jnp.where(lax.axis_index("dom") == 0, 1.0, 0.0)
     for out, top in ((down, False), (up, True)):
         side = int(top)
         at = [steps - 1 - k if top else k for k in range(steps)]
@@ -67,10 +63,7 @@
                 lap = lateral(scaled[k]) + scaled[k + 1]
                 if k > 0:
                     lap = lap + scaled[k - 1]
-                q = 2.0 * now[k] - old[k] + lap
-                if k == 0 and not top:
-                    q = q + source * first_residuals[step - 1]
-                new.append(q)
+                new.append(2.0 * now[k] - old[k] + lap)
             now, old = new, now
             scaled = [c * q for c, q in zip(v, now)]
             out[steps + step] = scaled[0]
@@ -89,60 +82,37 @@
         ref[0] = blank
         ref[depth + 1] = blank
 
-    @pl.loop(0, depth, step=CHUNK)
-    def _(begin):
-        for z in [begin + i for i in range(CHUNK)]:
-            ps[0][z + 1] = wave[z]
-            ws[0][z + 1] = vel[z] * adj[z]
-
-    surface = lax.axis_index("dom") == 0
+    for z in range(depth):
+        ps[0][z + 1] = wave[z]
+        ws[0][z + 1] = vel[z] * adj[z]
+
+    surface = jnp.where(lax.axis_index("dom") == 0, 1.0, 0.0)
     fields = (adj_old, adj, *adjoints)
     for step in range(steps):
         source, target = ws[step % 2], ws[(step + 1) % 2]
-        old, now, new_field = fields[step : step + 3]
-
-        @pl.loop(0, depth, step=CHUNK)
-        def _(begin):
-            new = []
-            for z in [begin + i for i in range(CHUNK)]:
-                lap = lateral(source[z + 1]) + (source[z] + source[z + 2])
-                new.append(2.0 * now[z] - old[z] + lap)
-            for i, q in enumerate(new):
-                new_field[begin + i] = q
+        old, now, new = fields[step : step + 3]
+        for z in range(depth):
+            lap = lateral(source[z + 1]) + (source[z] + source[z + 2])
+            q = 2.0 * now[z] - old[z] + lap
+            if z == 0:
+                q = q + surface * residuals[step]
+            new[z] = q
             if step < steps - 1:
-                scaled = [vel[begin + i] * q for i, q in enumerate(new)]
-                for i, w in enumerate(scaled):
-                    target[begin + i + 1] = w
-
-        @pl.when(surface)
-        def _():
-            q = new_field[0] + residuals[step]
-            new_field[0] = q
-            if step < steps - 1:
-                target[1] = vel[0] * q
+                target[z + 1] = vel[z] * q
 
     for step in range(steps):
         source, target = ps[step % 2], ps[(step + 1) % 2]
-
-        @pl.loop(0, depth, step=CHUNK)
-        def _(begin):
-            new = []
-            for z in [begin + i for i in range(CHUNK)]:
-                middle = source[z + 1]
-                lap = lateral(middle) + (source[z] + source[z + 2])
-                term = lap * adjoints[steps - 1 - step][z]
-                if step > 0:
-                    term = term + img[z]
-                field = None
-                if step < steps - 1:
-                    old = wave_old[z] if step == 0 else target[z + 1]
-                    field = 2.0 * middle - old + vel[z] * lap
-                new.append((lap, term, field))
-            for i, (lap, term, field) in enumerate(new):
-                laps[step][begin + i] = lap
-                img[begin + i] = term
-                if field is not None:
-                    target[begin + i + 1] = field
+        for z in range(depth):
+            middle = source[z + 1]
+            lap = lateral(middle) + (source[z] + source[z + 2])
+            term = lap * adjoints[steps - 1 - step][z]
+            if step > 0:
+                term = term + img[z]
+            laps[step][z] = lap
+            img[z] = term
+            if step < steps - 1:
+                old = wave_old[z] if step == 0 else target[z + 1]
+                target[z + 1] = 2.0 * middle - old + vel[z] * lap
 
 
 def finish(steps, depth, blocks, *refs):
@@ -262,12 +232,11 @@
     up, down = pl.pallas_call(
         functools.partial(edges, steps, depth),
         out_shape=(message, message),
-        in_specs=[hbm] * 6,
+        in_specs=[hbm] * 5,
         out_specs=(vmem, vmem),
-        scratch_shapes=[pltpu.VMEM((2, steps, width, size), f32)] * 5
-        + [pltpu.VMEM((steps, width, size), f32), pltpu.SemaphoreType.DMA((5, 2)), pltpu.SemaphoreType.DMA],
-        compiler_params=pltpu.CompilerParams(vmem_limit_bytes=60 * 2**20),
-    )(vel, wave, wave_old, adj, adj_old, residuals)
+        scratch_shapes=[pltpu.VMEM((2, steps, width, size), f32)] * 5 + [pltpu.SemaphoreType.DMA((5, 2))],
+        compiler_params=pltpu.CompilerParams(vmem_limit_bytes=53 * 2**20),
+    )(vel, wave, wave_old, adj, adj_old)
 
     low = lax.ppermute(up, "dom", [(i, i + 1) for i in range(doms - 1)])
     high = lax.ppermute(down, "dom", [(i + 1, i) for i in range(doms - 1)])

time: 62.4 us -> 59.8 us (0.958)
  Pallas kernels: 11.3 us -> 5.94 us
  waiting for transfers between devices: 1.88 us -> 3.78 us
  local copies, waits for them, and re-layouts: 0.03 us -> 0.92 us
    pallas_call x1, Pallas kernels: 7.05 us -> 2.5 us  [shards(): pl.pallas_call(functools.partial(slab, steps, depth), out_shape=(field,)...]
    ppermute x1, waiting for transfers between devices: 0.01 us -> 1.18 us  [shards(): high = lax.ppermute(down, 'dom', [(i + 1, i) for i in range(doms - 1)])]
    unnamed x16 -> x12, local copies, waits for them, and re-layouts: 0.03 us -> 0.92 us
    pallas_call x1, Pallas kernels: 3.07 us -> 2.29 us  [shards(): pl.pallas_call(functools.partial(edges, steps, depth), out_shape=(message...]
    ppermute x1, waiting for transfers between devices: 0.01 us -> 0.73 us  [shards(): low = lax.ppermute(up, 'dom', [(i, i + 1) for i in range(doms - 1)])]
  transfers between devices with their start and end apart: 3 -> 3, of which waited for: 1 -> 3; matrix products, arithmetic and copies ran while one was open for 0% -> 0% of each run, Pallas kernels for 11% -> 4%
where the time goes in v4:
time: 59.8 us; the launch traced here: 59.6 us
  blocking collectives  37 us (62%)
  starting transfers between devices  9.87 us (17%)
  Pallas kernels  5.94 us (10%)
  waiting for transfers between devices  3.78 us (6%)
  between operations  1.41 us (2%)
  local copies, waits for them, and re-layouts  0.92 us (2%)
  other arithmetic  0.73 us (1%)
    all_to_all x1, blocking collectives, shards(): lax.all_to_all(both, 'shot', 0, 0, tiled=True, axis_index_groups=groups)  37 us
    ppermute x1, starting transfers between devices, shards(): high = lax.ppermute(down, 'dom', [(i + 1, i) for i in range(doms - 1)])  4.55 us
    ppermute x1, starting transfers between devices, shards(): low = lax.ppermute(up, 'dom', [(i, i + 1) for i in range(doms - 1)])  3.4 us
    pallas_call x1, Pallas kernels, shards(): pl.pallas_call(functools.partial(slab, steps, depth), out_shape=(field,)...  2.5 us
    pallas_call x1, Pallas kernels, shards(): pl.pallas_call(functools.partial(edges, steps, depth), out_shape=(message...  2.29 us
    ppermute x1, starting transfers between devices, shards(): both = own + lax.ppermute(other, 'shot', pair)  1.92 us
    ppermute x1, waiting for transfers between devices, shards(): both = own + lax.ppermute(other, 'shot', pair)  1.88 us
  transfers between devices with their start and end apart: 3, of which 3 were waited for; matrix products, arithmetic and copies ran while one was open for 0% of the time, Pallas kernels for 4%

profile of v4, /device:TPU:8, one launch (start us, length us, event | category | flops | bytes accessed | tf_op | source)
XLA Modules:
  0.0 59.6 jit_solution(7092961413547756592)
XLA Ops:
  0.0 0.0 copy-start
  0.0 0.0 copy-start.4
  0.0 0.0 copy-start.3
  0.0 0.0 copy-start.2
  0.0 0.0 copy-start.1
  0.0 2.3 %shard_map.82 = (f32[10,64,128]{2,1,0:T(8,128)S(1)}, f32[10,64,128]{2,1,0:T(8,128)S(1)}) custom-call(f32[1,16,64,128]{3,2,1,0:T(8,128)} %refs_2_.3, f32[1,16,64,128]{3,2,1,0:T(8,128)} %refs_1_.2, f32[1,16,64,128]{3,2,1,0:T(8,128)} %refs_2_.2, f32[1,16,64,128]{3,2,1,0:T(8,128)} %refs_3_.1, f32[1,16,64,128]{3,2,1,0:T(8,128)} %refs_4_.1), custom_call_target="tpu_custom_call" | custom-call | tf_op jit(solution)/shard_map/pallas_call | solution.py:232
  2.3 3.4 %collective-permute-start = (f32[10,64,128]{2,1,0:T(8,128)S(1)}, f32[10,64,128]{2,1,0:T(8,128)S(1)}, u32[]{:S(2)}, u32[]{:S(2)}) collective-permute-start(f32[10,64,128]{2,1,0:T(8,128)S(1)} %get-tuple-element.18.refs_3_), channel_id=1, source_target_pairs={{0,1},{1,2},{2,3},{3,4},{4,5},{5,6},{6,7},{7,8},{8,9},{9,10},{10,1... | collective-permute-start | bytes 983048 | tf_op jit(solution)/shard_map/ppermute | solution.py:241
  5.7 4.6 %collective-permute-start.1 = (f32[10,64,128]{2,1,0:T(8,128)S(1)}, f32[10,64,128]{2,1,0:T(8,128)S(1)}, u32[]{:S(2)}, u32[]{:S(2)}) collective-permute-start(f32[10,64,128]{2,1,0:T(8,128)S(1)} %get-tuple-element.19.refs_4_), channel_id=1, source_target_pairs={{1,0},{2,1},{3,2},{4,3},{5,4},{6,5},{7,6},{8,7},{9,8},{10,9},{11,1... | collective-permute-start | bytes 983048 | tf_op jit(solution)/shard_map/ppermute | solution.py:242
  11.6 0.0 copy-done
  11.6 0.0 copy-done.4
  11.6 0.0 copy-done.3
  11.6 0.0 copy-done.2
  11.6 0.0 copy-done.1
  11.6 0.0 copy-start.5
  11.6 0.9 %copy-done.5 = f32[1,4,64,128]{3,2,1,0:T(8,128)S(1)} copy-done((f32[1,4,64,128]{3,2,1,0:T(8,128)S(1)}, f32[1,4,64,128]{3,2,1,0:T(8,128)}, u32[]{:S(2)}) %copy-start.5) | copy-done | bytes 131096
  12.5 2.5 %shard_map.83 = (f32[16,64,128]{2,1,0:T(8,128)S(1)}, f32[16,64,128]{2,1,0:T(8,128)S(1)}, f32[16,64,128]{2,1,0:T(8,128)S(1)}, f32[16,64,128]{2,1,0:T(8,128)S(1)},...) custom-call(f32[1,16,64,128]{3,2,1,0:T(8,128)S(1)} %copy-done, ...), custom_call_target="tpu_custom_call" | custom-call | flops 40000000 | bytes 16000000 | tf_op jit(solution)/shard_map/pallas_call | solution.py:244
  15.1 0.7 %collective-permute-done.refs_5_ = f32[10,64,128]{2,1,0:T(8,128)S(1)} collective-permute-done((f32[10,64,128]{2,1,0:T(8,128)S(1)}, f32[10,64,128]{2,1,0:T(8,128)S(1)}, u32[]{:S(2)}, u32[]{:S(2)}) %collective-permute-start) | collective-permute-done | bytes 327712 | tf_op jit(solution)/shard_map/ppermute | solution.py:241
  15.8 1.2 %collective-permute-done.1.refs_6_ = f32[10,64,128]{2,1,0:T(8,128)S(1)} collective-permute-done((f32[10,64,128]{2,1,0:T(8,128)S(1)}, f32[10,64,128]{2,1,0:T(8,128)S(1)}, u32[]{:S(2)}, u32[]{:S(2)}) %collective-permute-start.1) | collective-permute-done | bytes 327712 | tf_op jit(solution)/shard_map/ppermute | solution.py:242
  17.0 1.2 %shard_map.84 = (f32[16,64,128]{2,1,0:T(8,128)S(1)}, f32[16,64,128]{2,1,0:T(8,128)S(1)}) custom-call(s32[1]{0:T(128)S(6)} %copy.9.refs_0_, s32[1]{0:T(128)S(6)} %copy.10.refs_1_, f32[1,16,64,128]{3,2,1,0:T(8,128)S(1)} %copy-done, f32[10,64,128]{2,1,0:T(8,128)S(1)} %get-tuple-element.18.refs_3_, f32[10,64,128]{2,1,0:T(8,128)S(1)} %get-tuple-element.19.refs_4_, ...), custom_call_target="tpu_custom_call" | custom-call | tf_op jit(solution)/shard_map/pallas_call | solution.py:254
  18.1 1.9 %collective-permute-start.2 = (f32[16,64,128]{2,1,0:T(8,128)S(1)}, f32[16,64,128]{2,1,0:T(8,128)S(1)}, u32[]{:S(2)}, u32[]{:S(2)}) collective-permute-start(f32[16,64,128]{2,1,0:T(8,128)S(1)} %get-tuple-element.30), channel_id=1, source_target_pairs={{0,16},{16,0},{32,48},{48,32},{64,80},{80,64},{96,112},{112,96},{1... | collective-permute-start | bytes 1572872 | tf_op jit(solution)/shard_map/ppermute | solution.py:264
  20.1 1.9 %collective-permute-done.2 = f32[16,64,128]{2,1,0:T(8,128)S(1)} collective-permute-done((f32[16,64,128]{2,1,0:T(8,128)S(1)}, f32[16,64,128]{2,1,0:T(8,128)S(1)}, u32[]{:S(2)}, u32[]{:S(2)}) %collective-permute-start.2) | collective-permute-done | bytes 524320 | tf_op jit(solution)/shard_map/ppermute | solution.py:264
  21.9 0.1 add.3
  22.0 37.0 %all_to_all.5 = f32[16,64,128]{2,1,0:T(8,128)S(1)} all-to-all(f32[16,64,128]{2,1,0:T(8,128)S(1)} %add.3), channel_id=1, replica_groups={{0,32,64,96,128,160,192,224,256,288,320,352,384,416,448,480},{16,48,80,..., dimensions={0} | all-to-all | bytes 1048576 | tf_op jit(solution)/shard_map/all_to_all | solution.py:266
  59.0 0.6 %reduce_sum.9 = f32[64,128]{1,0:T(8,128)} reduce(f32[16,64,128]{2,1,0:T(8,128)S(1)} %all_to_all.5, f32[]{:T(128)} %constant.0.clone.1), dimensions={0}, to_apply=%region_0.0 | reduce | flops 122880 | bytes 557060 | tf_op jit(solution)/shard_map/reduce_sum | solution.py:267
Async XLA Ops:
  0.0 11.6 %copy-start = (f32[1,16,64,128]{3,2,1,0:T(8,128)S(1)}, f32[1,16,64,128]{3,2,1,0:T(8,128)}, u32[]{:S(2)}) copy-start(f32[1,16,64,128]{3,2,1,0:T(8,128)} %refs_2_.3) | copy-start | bytes 1572868
  0.0 11.6 %copy-start.4 = (f32[1,16,64,128]{3,2,1,0:T(8,128)S(1)}, f32[1,16,64,128]{3,2,1,0:T(8,128)}, u32[]{:S(2)}) copy-start(f32[1,16,64,128]{3,2,1,0:T(8,128)} %refs_4_.1) | copy-start | bytes 1572868
  0.0 11.6 %copy-start.3 = (f32[1,16,64,128]{3,2,1,0:T(8,128)S(1)}, f32[1,16,64,128]{3,2,1,0:T(8,128)}, u32[]{:S(2)}) copy-start(f32[1,16,64,128]{3,2,1,0:T(8,128)} %refs_3_.1) | copy-start | bytes 1572868
  0.0 11.6 %copy-start.2 = (f32[1,16,64,128]{3,2,1,0:T(8,128)S(1)}, f32[1,16,64,128]{3,2,1,0:T(8,128)}, u32[]{:S(2)}) copy-start(f32[1,16,64,128]{3,2,1,0:T(8,128)} %refs_2_.2) | copy-start | bytes 1572868
  0.0 11.6 %copy-start.1 = (f32[1,16,64,128]{3,2,1,0:T(8,128)S(1)}, f32[1,16,64,128]{3,2,1,0:T(8,128)}, u32[]{:S(2)}) copy-start(f32[1,16,64,128]{3,2,1,0:T(8,128)} %refs_1_.2) | copy-start | bytes 1572868
  2.3 13.5 %collective-permute-start = (f32[10,64,128]{2,1,0:T(8,128)S(1)}, f32[10,64,128]{2,1,0:T(8,128)S(1)}, u32[]{:S(2)}, u32[]{:S(2)}) collective-permute-start(f32[10,64,128]{2,1,0:T(8,128)S(1)} %get-tuple-element.18.refs_3_), channel_id=1, source_target_pairs={{0,1},{1,2},{2,3},{3,4},{4,5},{5,6},{6,7},{7,8},{8,9},{9,10},{10,1... | collective-permute-start | bytes 983048 | tf_op jit(solution)/shard_map/ppermute | solution.py:241
  5.7 11.2 %collective-permute-start.1 = (f32[10,64,128]{2,1,0:T(8,128)S(1)}, f32[10,64,128]{2,1,0:T(8,128)S(1)}, u32[]{:S(2)}, u32[]{:S(2)}) collective-permute-start(f32[10,64,128]{2,1,0:T(8,128)S(1)} %get-tuple-element.19.refs_4_), channel_id=1, source_target_pairs={{1,0},{2,1},{3,2},{4,3},{5,4},{6,5},{7,6},{8,7},{9,8},{10,9},{11,1... | collective-permute-start | bytes 983048 | tf_op jit(solution)/shard_map/ppermute | solution.py:242
  11.6 0.9 %copy-start.5 = (f32[1,4,64,128]{3,2,1,0:T(8,128)S(1)}, f32[1,4,64,128]{3,2,1,0:T(8,128)}, u32[]{:S(2)}) copy-start(f32[1,4,64,128]{3,2,1,0:T(8,128)} %refs_5_.1) | copy-start | bytes 393220
  18.1 3.8 %collective-permute-start.2 = (f32[16,64,128]{2,1,0:T(8,128)S(1)}, f32[16,64,128]{2,1,0:T(8,128)S(1)}, u32[]{:S(2)}, u32[]{:S(2)}) collective-permute-start(f32[16,64,128]{2,1,0:T(8,128)S(1)} %get-tuple-element.30), channel_id=1, source_target_pairs={{0,16},{16,0},{32,48},{48,32},{64,80},{80,64},{96,112},{112,96},{1... | collective-permute-start | bytes 1572872 | tf_op jit(solution)/shard_map/ppermute | solution.py:264

commit v5 on v4

--- a/solution.py
+++ b/solution.py
@@ -214,6 +214,15 @@
             ref[lax.rem(k + half, blocks)] = zero
 
 
+def totals(parts, kept, sent):
+    side = lax.rem(lax.div(lax.axis_index("shot"), 2), 2)
+    for out, at in ((sent, 1 - side), (kept, side)):
+        total = parts[0, at]
+        for source in range(1, parts.shape[0]):
+            total = total + parts[source, at]
+        out[...] = total
+
+
 def shards(vel, wave, wave_old, adj, adj_old, residuals, offset, count):
     _, depth, width, size = vel.shape
     steps = residuals.shape[1]
@@ -262,9 +271,18 @@
 
     pair = [(s, s + 1 - 2 * (s % 2)) for s in range(shots)]
     both = own + lax.ppermute(other, "shot", pair)
-    groups = [[2 * k + c for k in range(blocks)] for c in range(2)]
-    parts = lax.all_to_all(both, "shot", 0, 0, tiled=True, axis_index_groups=groups)
-    return jnp.sum(parts, axis=0).reshape(1, depth, span, size)
+    rows = depth * span
+    layers = shots // 4
+    groups = [[4 * z + r for z in range(layers)] for r in range(4)]
+    parts = lax.all_to_all(
+        both.reshape(layers, 2, rows, size), "shot", 0, 0, tiled=True, axis_index_groups=groups
+    )
+    part = jax.ShapeDtypeStruct((rows, size), f32)
+    kept, sent = pl.pallas_call(
+        totals, out_shape=(part, part), in_specs=[vmem], out_specs=(vmem, vmem), compiler_params=room
+    )(parts)
+    across = [(s, s + 2 - 4 * (s // 2 % 2)) for s in range(shots)]
+    return (kept + lax.ppermute(sent, "shot", across)).reshape(1, depth, span, size)
 
 
 def solution(mesh):

time: 59.8 us -> 62.6 us (1.047)
  the two profiles are of different devices: /device:TPU:8 before, /device:TPU:22 now
where the time goes in v5:
time: 62.6 us; the launch traced here: 62.4 us
  blocking collectives  27.9 us (45%)
  starting transfers between devices  12.8 us (20%)
  waiting for transfers between devices  12.6 us (20%)
  Pallas kernels  5.97 us (10%)
  between operations  1.42 us (2%)
  local copies, waits for them, and re-layouts  0.92 us (1%)
  other arithmetic  0.7 us (1%)
    all_to_all x1, blocking collectives, shards(): lax.all_to_all(both.reshape(layers, 2, rows, size), 'shot', 0, 0, tiled=T...  27.9 us
    ppermute x1, waiting for transfers between devices, shards(): high = lax.ppermute(down, 'dom', [(i + 1, i) for i in range(doms - 1)])  5.24 us
    ppermute x1, starting transfers between devices, shards(): lax.ppermute(sent, 'shot', across)  5.04 us
    ppermute x1, waiting for transfers between devices, shards(): lax.ppermute(sent, 'shot', across)  4.8 us
    ppermute x1, starting transfers between devices, shards(): low = lax.ppermute(up, 'dom', [(i, i + 1) for i in range(doms - 1)])  3.4 us
    pallas_call x1, Pallas kernels, shards(): pl.pallas_call(functools.partial(slab, steps, depth), out_shape=(field,)...  2.5 us
    ppermute x1, starting transfers between devices, shards(): high = lax.ppermute(down, 'dom', [(i + 1, i) for i in range(doms - 1)])  2.44 us
    pallas_call x1, Pallas kernels, shards(): pl.pallas_call(functools.partial(edges, steps, depth), out_shape=(message...  2.29 us
  transfers between devices with their start and end apart: 4, of which 4 were waited for; matrix products, arithmetic and copies ran while one was open for 0% of the time, Pallas kernels for 4%

profile of v5, /device:TPU:22, one launch (start us, length us, event | category | flops | bytes accessed | tf_op | source)
XLA Modules:
  0.0 62.4 jit_solution(603341287650512673)
XLA Ops:
  0.0 0.0 copy-start
  0.0 0.0 copy-start.4
  0.0 0.0 copy-start.3
  0.0 0.0 copy-start.2
  0.0 0.0 copy-start.1
  0.0 2.3 %shard_map.82 = (f32[10,64,128]{2,1,0:T(8,128)S(1)}, f32[10,64,128]{2,1,0:T(8,128)S(1)}) custom-call(f32[1,16,64,128]{3,2,1,0:T(8,128)} %refs_2_.3, f32[1,16,64,128]{3,2,1,0:T(8,128)} %refs_1_.2, f32[1,16,64,128]{3,2,1,0:T(8,128)} %refs_2_.2, f32[1,16,64,128]{3,2,1,0:T(8,128)} %refs_3_.1, f32[1,16,64,128]{3,2,1,0:T(8,128)} %refs_4_.1), custom_call_target="tpu_custom_call" | custom-call | tf_op jit(solution)/shard_map/pallas_call | solution.py:241
  2.3 3.4 %collective-permute-start = (f32[10,64,128]{2,1,0:T(8,128)S(1)}, f32[10,64,128]{2,1,0:T(8,128)S(1)}, u32[]{:S(2)}, u32[]{:S(2)}) collective-permute-start(f32[10,64,128]{2,1,0:T(8,128)S(1)} %get-tuple-element.20.refs_3_), channel_id=1, source_target_pairs={{0,1},{1,2},{2,3},{3,4},{4,5},{5,6},{6,7},{7,8},{8,9},{9,10},{10,1... | collective-permute-start | bytes 983048 | tf_op jit(solution)/shard_map/ppermute | solution.py:250
  5.7 2.4 %collective-permute-start.1 = (f32[10,64,128]{2,1,0:T(8,128)S(1)}, f32[10,64,128]{2,1,0:T(8,128)S(1)}, u32[]{:S(2)}, u32[]{:S(2)}) collective-permute-start(f32[10,64,128]{2,1,0:T(8,128)S(1)} %get-tuple-element.21.refs_4_), channel_id=1, source_target_pairs={{1,0},{2,1},{3,2},{4,3},{5,4},{6,5},{7,6},{8,7},{9,8},{10,9},{11,1... | collective-permute-start | bytes 983048 | tf_op jit(solution)/shard_map/ppermute | solution.py:251
  9.5 0.0 copy-done
  9.5 0.0 copy-done.4
  9.5 0.0 copy-done.3
  9.5 0.0 copy-done.2
  9.5 0.0 copy-done.1
  9.5 0.0 copy-start.5
  9.5 0.9 %copy-done.5 = f32[1,4,64,128]{3,2,1,0:T(8,128)S(1)} copy-done((f32[1,4,64,128]{3,2,1,0:T(8,128)S(1)}, f32[1,4,64,128]{3,2,1,0:T(8,128)}, u32[]{:S(2)}) %copy-start.5) | copy-done | bytes 131096
  10.4 2.5 %shard_map.83 = (f32[16,64,128]{2,1,0:T(8,128)S(1)}, f32[16,64,128]{2,1,0:T(8,128)S(1)}, f32[16,64,128]{2,1,0:T(8,128)S(1)}, f32[16,64,128]{2,1,0:T(8,128)S(1)},...) custom-call(f32[1,16,64,128]{3,2,1,0:T(8,128)S(1)} %copy-done, ...), custom_call_target="tpu_custom_call" | custom-call | flops 40000000 | bytes 16000000 | tf_op jit(solution)/shard_map/pallas_call | solution.py:253
  12.9 0.7 %collective-permute-done.refs_5_ = f32[10,64,128]{2,1,0:T(8,128)S(1)} collective-permute-done((f32[10,64,128]{2,1,0:T(8,128)S(1)}, f32[10,64,128]{2,1,0:T(8,128)S(1)}, u32[]{:S(2)}, u32[]{:S(2)}) %collective-permute-start) | collective-permute-done | bytes 327712 | tf_op jit(solution)/shard_map/ppermute | solution.py:250
  13.7 5.2 %collective-permute-done.1.refs_6_ = f32[10,64,128]{2,1,0:T(8,128)S(1)} collective-permute-done((f32[10,64,128]{2,1,0:T(8,128)S(1)}, f32[10,64,128]{2,1,0:T(8,128)S(1)}, u32[]{:S(2)}, u32[]{:S(2)}) %collective-permute-start.1) | collective-permute-done | bytes 327712 | tf_op jit(solution)/shard_map/ppermute | solution.py:251
  18.9 1.2 %shard_map.84 = (f32[16,64,128]{2,1,0:T(8,128)S(1)}, f32[16,64,128]{2,1,0:T(8,128)S(1)}) custom-call(s32[1]{0:T(128)S(6)} %copy.9.refs_0_, s32[1]{0:T(128)S(6)} %copy.10.refs_1_, f32[1,16,64,128]{3,2,1,0:T(8,128)S(1)} %copy-done, f32[10,64,128]{2,1,0:T(8,128)S(1)} %get-tuple-element.20.refs_3_, f32[10,64,128]{2,1,0:T(8,128)S(1)} %get-tuple-element.21.refs_4_, ...), custom_call_target="tpu_custom_call" | custom-call | tf_op jit(solution)/shard_map/pallas_call | solution.py:263
  20.1 1.9 %collective-permute-start.2 = (f32[16,64,128]{2,1,0:T(8,128)S(1)}, f32[16,64,128]{2,1,0:T(8,128)S(1)}, u32[]{:S(2)}, u32[]{:S(2)}) collective-permute-start(f32[16,64,128]{2,1,0:T(8,128)S(1)} %get-tuple-element.32), channel_id=1, source_target_pairs={{0,16},{16,0},{32,48},{48,32},{64,80},{80,64},{96,112},{112,96},{1... | collective-permute-start | bytes 1572872 | tf_op jit(solution)/shard_map/ppermute | solution.py:273
  22.0 1.9 %collective-permute-done.2 = f32[16,64,128]{2,1,0:T(8,128)S(1)} collective-permute-done((f32[16,64,128]{2,1,0:T(8,128)S(1)}, f32[16,64,128]{2,1,0:T(8,128)S(1)}, u32[]{:S(2)}, u32[]{:S(2)}) %collective-permute-start.2) | collective-permute-done | bytes 524320 | tf_op jit(solution)/shard_map/ppermute | solution.py:273
  23.9 0.1 add.6
  24.0 27.9 %all_to_all.5.parts = f32[8,2,64,128]{3,2,1,0:T(8,128)S(1)} all-to-all(f32[8,2,64,128]{3,2,1,0:T(8,128)S(1)} %bitcast.2), channel_id=1, replica_groups={{0,64,128,192,256,320,384,448},{16,80,144,208,272,336,400,464},{32,96,1..., dimensions={0} | all-to-all | bytes 1048576 | tf_op jit(solution)/shard_map/all_to_all | solution.py:277
  51.9 5.0 %collective-permute-start.3 = (f32[64,128]{1,0:T(8,128)S(1)}, f32[64,128]{1,0:T(8,128)S(1)}, u32[]{:S(2)}, u32[]{:S(2)}) collective-permute-start(f32[64,128]{1,0:T(8,128)S(1)} %get-tuple-element.34), channel_id=1, source_target_pairs={{0,32},{16,48},{32,0},{48,16},{64,96},{80,112},{96,64},{112,80},{1... | collective-permute-start | bytes 98312 | tf_op jit(solution)/shard_map/ppermute | solution.py:285
  56.9 4.8 %collective-permute-done.3 = f32[64,128]{1,0:T(8,128)S(1)} collective-permute-done((f32[64,128]{1,0:T(8,128)S(1)}, f32[64,128]{1,0:T(8,128)S(1)}, u32[]{:S(2)}, u32[]{:S(2)}) %collective-permute-start.3) | collective-permute-done | bytes 32800 | tf_op jit(solution)/shard_map/ppermute | solution.py:285
  61.7 0.6 add.7
  (1 shorter events, 0.0 us)
Async XLA Ops:
  0.0 9.5 %copy-start = (f32[1,16,64,128]{3,2,1,0:T(8,128)S(1)}, f32[1,16,64,128]{3,2,1,0:T(8,128)}, u32[]{:S(2)}) copy-start(f32[1,16,64,128]{3,2,1,0:T(8,128)} %refs_2_.3) | copy-start | bytes 1572868
  0.0 9.5 %copy-start.4 = (f32[1,16,64,128]{3,2,1,0:T(8,128)S(1)}, f32[1,16,64,128]{3,2,1,0:T(8,128)}, u32[]{:S(2)}) copy-start(f32[1,16,64,128]{3,2,1,0:T(8,128)} %refs_4_.1) | copy-start | bytes 1572868
  0.0 9.5 %copy-start.3 = (f32[1,16,64,128]{3,2,1,0:T(8,128)S(1)}, f32[1,16,64,128]{3,2,1,0:T(8,128)}, u32[]{:S(2)}) copy-start(f32[1,16,64,128]{3,2,1,0:T(8,128)} %refs_3_.1) | copy-start | bytes 1572868
  0.0 9.5 %copy-start.2 = (f32[1,16,64,128]{3,2,1,0:T(8,128)S(1)}, f32[1,16,64,128]{3,2,1,0:T(8,128)}, u32[]{:S(2)}) copy-start(f32[1,16,64,128]{3,2,1,0:T(8,128)} %refs_2_.2) | copy-start | bytes 1572868
  0.0 9.5 %copy-start.1 = (f32[1,16,64,128]{3,2,1,0:T(8,128)S(1)}, f32[1,16,64,128]{3,2,1,0:T(8,128)}, u32[]{:S(2)}) copy-start(f32[1,16,64,128]{3,2,1,0:T(8,128)} %refs_1_.2) | copy-start | bytes 1572868
  2.3 11.3 %collective-permute-start = (f32[10,64,128]{2,1,0:T(8,128)S(1)}, f32[10,64,128]{2,1,0:T(8,128)S(1)}, u32[]{:S(2)}, u32[]{:S(2)}) collective-permute-start(f32[10,64,128]{2,1,0:T(8,128)S(1)} %get-tuple-element.20.refs_3_), channel_id=1, source_target_pairs={{0,1},{1,2},{2,3},{3,4},{4,5},{5,6},{6,7},{7,8},{8,9},{9,10},{10,1... | collective-permute-start | bytes 983048 | tf_op jit(solution)/shard_map/ppermute | solution.py:250
  5.7 13.2 %collective-permute-start.1 = (f32[10,64,128]{2,1,0:T(8,128)S(1)}, f32[10,64,128]{2,1,0:T(8,128)S(1)}, u32[]{:S(2)}, u32[]{:S(2)}) collective-permute-start(f32[10,64,128]{2,1,0:T(8,128)S(1)} %get-tuple-element.21.refs_4_), channel_id=1, source_target_pairs={{1,0},{2,1},{3,2},{4,3},{5,4},{6,5},{7,6},{8,7},{9,8},{10,9},{11,1... | collective-permute-start | bytes 983048 | tf_op jit(solution)/shard_map/ppermute | solution.py:251
  9.5 0.9 %copy-start.5 = (f32[1,4,64,128]{3,2,1,0:T(8,128)S(1)}, f32[1,4,64,128]{3,2,1,0:T(8,128)}, u32[]{:S(2)}) copy-start(f32[1,4,64,128]{3,2,1,0:T(8,128)} %refs_5_.1) | copy-start | bytes 393220
  20.1 3.8 %collective-permute-start.2 = (f32[16,64,128]{2,1,0:T(8,128)S(1)}, f32[16,64,128]{2,1,0:T(8,128)S(1)}, u32[]{:S(2)}, u32[]{:S(2)}) collective-permute-start(f32[16,64,128]{2,1,0:T(8,128)S(1)} %get-tuple-element.32), channel_id=1, source_target_pairs={{0,16},{16,0},{32,48},{48,32},{64,80},{80,64},{96,112},{112,96},{1... | collective-permute-start | bytes 1572872 | tf_op jit(solution)/shard_map/ppermute | solution.py:273
  51.9 9.8 %collective-permute-start.3 = (f32[64,128]{1,0:T(8,128)S(1)}, f32[64,128]{1,0:T(8,128)S(1)}, u32[]{:S(2)}, u32[]{:S(2)}) collective-permute-start(f32[64,128]{1,0:T(8,128)S(1)} %get-tuple-element.34), channel_id=1, source_target_pairs={{0,32},{16,48},{32,0},{48,16},{64,96},{80,112},{96,64},{112,80},{1... | collective-permute-start | bytes 98312 | tf_op jit(solution)/shard_map/ppermute | solution.py:285

commit v6 on v4

--- a/solution.py
+++ b/solution.py
@@ -24,22 +24,29 @@
         return (above + below) + (left + right) - 6.0 * middle
 
 
-def edges(steps, depth, vel, wave, wave_old, adj, adj_old, up, down, *scratch):
+def sides():
+    odd = lax.rem(lax.axis_index("dom"), 2)
+    return odd, 1 - odd
+
+
+def edges(steps, depth, vel, wave, wave_old, adj, adj_old, first, second, *scratch):
     _, _, width, size = vel.shape
     lateral = Lateral(width, size)
     fetched, sems = scratch[:5], scratch[5]
-    copies = []
-    for i, (ref, held) in enumerate(zip((vel, wave, wave_old, adj, adj_old), fetched)):
-        for side, begin in enumerate((0, depth - steps)):
-            copies.append(pltpu.make_async_copy(ref.at[0, pl.ds(begin, steps)], held.at[side], sems.at[i, side]))
-    for copy in copies:
+    copies = [
+        [
+            pltpu.make_async_copy(ref.at[0, pl.ds(side * (depth - steps), steps)], held.at[at], sems.at[at, i])
+            for i, (ref, held) in enumerate(zip((vel, wave, wave_old, adj, adj_old), fetched))
+        ]
+        for at, side in enumerate(sides())
+    ]
+    for copy in copies[0] + copies[1]:
         copy.start()
-    for copy in copies:
-        copy.wait()
     vel, wave, wave_old, adj, adj_old = fetched
-    for out, top in ((down, False), (up, True)):
-        side = int(top)
-        at = [steps - 1 - k if top else k for k in range(steps)]
+    for side, (out, top) in enumerate(zip((first, second), sides())):
+        for copy in copies[side]:
+            copy.wait()
+        at = [k + top * (steps - 1 - 2 * k) for k in range(steps)]
         v = [vel[side, z] for z in at]
         out[2 * steps] = v[0]
         out[2 * steps + 1] = v[1]
@@ -116,10 +123,10 @@
 
 
 def finish(steps, depth, blocks, *refs):
-    offset, count, vel, up, down, low, high = refs[:7]
+    offset, count, vel, first, second, from_first, from_second = refs[:7]
     vel = vel.at[0]
     laps, adjoints, img = refs[7 : 7 + steps], refs[7 + steps : 7 + 2 * steps], refs[7 + 2 * steps]
-    own, other, blocked = refs[8 + 2 * steps :]
+    own, other, blocked, outer = refs[8 + 2 * steps :]
     _, width, size = vel.shape
     lateral = Lateral(width, size)
     span = width // blocks
@@ -131,8 +138,8 @@
     for z in range(steps, depth - steps):
         store(z, img[z])
 
-    for sent, got, top in ((down, low, False), (up, high, True)):
-        at = [depth - 1 - k if top else k for k in range(steps)]
+    for sent, got, top in zip((first, second), (from_first, from_second), sides()):
+        at = [k + top * (depth - 1 - 2 * k) for k in range(steps)]
         here = [vel[z] for z in at]
         there = [got[2 * steps], got[2 * steps + 1]]
 
@@ -199,7 +206,10 @@
                 if k < len(more_adjoints[steps - 1 - n]):
                     b = b + more_adjoints[steps - 1 - n][k]
                 total = a * b if total is None else total + a * b
-            store(z, total)
+            outer[z] = total
+
+    for z in (*range(steps), *range(depth - steps, depth)):
+        store(z, outer[z])
 
     start, live = offset[0], count[0]
     odd = lax.rem(start + lax.axis_index("shot"), 2)
@@ -229,17 +239,20 @@
     field = jax.ShapeDtypeStruct((depth, width, size), f32)
     block = jax.ShapeDtypeStruct((blocks, depth * span, size), f32)
 
-    up, down = pl.pallas_call(
+    first, second = pl.pallas_call(
         functools.partial(edges, steps, depth),
         out_shape=(message, message),
         in_specs=[hbm] * 5,
         out_specs=(vmem, vmem),
-        scratch_shapes=[pltpu.VMEM((2, steps, width, size), f32)] * 5 + [pltpu.SemaphoreType.DMA((5, 2))],
+        scratch_shapes=[pltpu.VMEM((2, steps, width, size), f32)] * 5 + [pltpu.SemaphoreType.DMA((2, 5))],
         compiler_params=pltpu.CompilerParams(vmem_limit_bytes=53 * 2**20),
     )(vel, wave, wave_old, adj, adj_old)
 
-    low = lax.ppermute(up, "dom", [(i, i + 1) for i in range(doms - 1)])
-    high = lax.ppermute(down, "dom", [(i + 1, i) for i in range(doms - 1)])
+    def exchange(message, begin):
+        lower = range(begin, doms - 1, 2)
+        return lax.ppermute(message, "dom", [(i, i + 1) for i in lower] + [(i + 1, i) for i in lower])
+
+    from_first, from_second = exchange(first, 1), exchange(second, 0)
 
     inner = pl.pallas_call(
         functools.partial(slab, steps, depth),
@@ -256,9 +269,9 @@
         out_shape=(block, block),
         in_specs=[smem, smem] + [vmem] * (6 + 2 * steps),
         out_specs=(vmem, vmem),
-        scratch_shapes=[pltpu.VMEM((blocks, depth * span, size), f32)],
+        scratch_shapes=[pltpu.VMEM((blocks, depth * span, size), f32), pltpu.VMEM((depth, width, size), f32)],
         compiler_params=room,
-    )(offset, count, vel, up, down, low, high, *inner)
+    )(offset, count, vel, first, second, from_first, from_second, *inner)
 
     pair = [(s, s + 1 - 2 * (s % 2)) for s in range(shots)]
     both = own + lax.ppermute(other, "shot", pair)

time: 59.8 us -> 61.7 us (1.032)
  waiting for transfers between devices: 3.78 us -> 5.93 us
  starting transfers between devices: 9.87 us -> 8.72 us
  blocking collectives: 37 us -> 37.9 us
    ppermute x2, waiting for transfers between devices: 1.91 us -> 4.05 us  [exchange(): lax.ppermute(message, 'dom', [(i, i + 1) for i in lower] + [(i + 1, i) fo...]
    ppermute x2, starting transfers between devices: 7.95 us -> 6.8 us  [exchange(): lax.ppermute(message, 'dom', [(i, i + 1) for i in lower] + [(i + 1, i) fo...]
    all_to_all x1, blocking collectives: 37 us -> 37.9 us  [shards(): lax.all_to_all(both, 'shot', 0, 0, tiled=True, axis_index_groups=groups)]
where the time goes in v6:
time: 61.7 us; the launch traced here: 61.4 us
  blocking collectives  37.9 us (61%)
  starting transfers between devices  8.72 us (14%)
  waiting for transfers between devices  5.93 us (10%)
  Pallas kernels  5.89 us (10%)
  between operations  1.41 us (2%)
  local copies, waits for them, and re-layouts  0.92 us (1%)
  other arithmetic  0.73 us (1%)
    all_to_all x1, blocking collectives, shards(): lax.all_to_all(both, 'shot', 0, 0, tiled=True, axis_index_groups=groups)  37.9 us
    ppermute x2, starting transfers between devices, exchange(): lax.ppermute(message, 'dom', [(i, i + 1) for i in lower] + [(i + 1, i) fo...  6.8 us
    ppermute x2, waiting for transfers between devices, exchange(): lax.ppermute(message, 'dom', [(i, i + 1) for i in lower] + [(i + 1, i) fo...  4.05 us
    pallas_call x1, Pallas kernels, shards(): pl.pallas_call(functools.partial(slab, steps, depth), out_shape=(field,)...  2.5 us
    pallas_call x1, Pallas kernels, shards(): pl.pallas_call(functools.partial(edges, steps, depth), out_shape=(message...  2.16 us
    ppermute x1, starting transfers between devices, shards(): both = own + lax.ppermute(other, 'shot', pair)  1.92 us
    ppermute x1, waiting for transfers between devices, shards(): both = own + lax.ppermute(other, 'shot', pair)  1.88 us
  transfers between devices with their start and end apart: 3, of which 3 were waited for; matrix products, arithmetic and copies ran while one was open for 0% of the time, Pallas kernels for 4%

profile of v6, /device:TPU:8, one launch (start us, length us, event | category | flops | bytes accessed | tf_op | source)
XLA Modules:
  0.0 61.4 jit_solution(5265938467736664650)
XLA Ops:
  0.0 0.0 copy-start
  0.0 0.0 copy-start.4
  0.0 0.0 copy-start.3
  0.0 0.0 copy-start.2
  0.0 0.0 copy-start.1
  0.0 2.2 %shard_map.82 = (f32[10,64,128]{2,1,0:T(8,128)S(1)}, f32[10,64,128]{2,1,0:T(8,128)S(1)}) custom-call(f32[1,16,64,128]{3,2,1,0:T(8,128)} %refs_2_.3, f32[1,16,64,128]{3,2,1,0:T(8,128)} %refs_1_.2, f32[1,16,64,128]{3,2,1,0:T(8,128)} %refs_2_.2, f32[1,16,64,128]{3,2,1,0:T(8,128)} %refs_3_.1, f32[1,16,64,128]{3,2,1,0:T(8,128)} %refs_4_.1), custom_call_target="tpu_custom_call" | custom-call | tf_op jit(solution)/shard_map/pallas_call | solution.py:242
  2.2 4.6 %collective-permute-start = (f32[10,64,128]{2,1,0:T(8,128)S(1)}, f32[10,64,128]{2,1,0:T(8,128)S(1)}, u32[]{:S(2)}, u32[]{:S(2)}) collective-permute-start(f32[10,64,128]{2,1,0:T(8,128)S(1)} %get-tuple-element.18.refs_3_), channel_id=1, source_target_pairs={{1,2},{3,4},{5,6},{7,8},{9,10},{11,12},{13,14},{2,1},{4,3},{6,5},{... | collective-permute-start | bytes 983048 | tf_op jit(solution)/shard_map/ppermute | solution.py:253
  6.8 2.2 %collective-permute-start.1 = (f32[10,64,128]{2,1,0:T(8,128)S(1)}, f32[10,64,128]{2,1,0:T(8,128)S(1)}, u32[]{:S(2)}, u32[]{:S(2)}) collective-permute-start(f32[10,64,128]{2,1,0:T(8,128)S(1)} %get-tuple-element.19.refs_4_), channel_id=1, source_target_pairs={{0,1},{2,3},{4,5},{6,7},{8,9},{10,11},{12,13},{14,15},{1,0},{3,2},... | collective-permute-start | bytes 983048 | tf_op jit(solution)/shard_map/ppermute | solution.py:253
  10.3 0.0 copy-done
  10.3 0.0 copy-done.4
  10.3 0.0 copy-done.3
  10.3 0.0 copy-done.2
  10.4 0.0 copy-done.1
  10.4 0.0 copy-start.5
  10.4 0.9 %copy-done.5 = f32[1,4,64,128]{3,2,1,0:T(8,128)S(1)} copy-done((f32[1,4,64,128]{3,2,1,0:T(8,128)S(1)}, f32[1,4,64,128]{3,2,1,0:T(8,128)}, u32[]{:S(2)}) %copy-start.5) | copy-done | bytes 131096
  11.3 2.5 %shard_map.83 = (f32[16,64,128]{2,1,0:T(8,128)S(1)}, f32[16,64,128]{2,1,0:T(8,128)S(1)}, f32[16,64,128]{2,1,0:T(8,128)S(1)}, f32[16,64,128]{2,1,0:T(8,128)S(1)},...) custom-call(f32[1,16,64,128]{3,2,1,0:T(8,128)S(1)} %copy-done, ...), custom_call_target="tpu_custom_call" | custom-call | flops 40000000 | bytes 16000000 | tf_op jit(solution)/shard_map/pallas_call | solution.py:257
  13.8 1.9 %collective-permute-done.refs_5_ = f32[10,64,128]{2,1,0:T(8,128)S(1)} collective-permute-done((f32[10,64,128]{2,1,0:T(8,128)S(1)}, f32[10,64,128]{2,1,0:T(8,128)S(1)}, u32[]{:S(2)}, u32[]{:S(2)}) %collective-permute-start) | collective-permute-done | bytes 327712 | tf_op jit(solution)/shard_map/ppermute | solution.py:253
  15.7 2.2 %collective-permute-done.1.refs_6_ = f32[10,64,128]{2,1,0:T(8,128)S(1)} collective-permute-done((f32[10,64,128]{2,1,0:T(8,128)S(1)}, f32[10,64,128]{2,1,0:T(8,128)S(1)}, u32[]{:S(2)}, u32[]{:S(2)}) %collective-permute-start.1) | collective-permute-done | bytes 327712 | tf_op jit(solution)/shard_map/ppermute | solution.py:253
  17.8 1.2 %shard_map.84 = (f32[16,64,128]{2,1,0:T(8,128)S(1)}, f32[16,64,128]{2,1,0:T(8,128)S(1)}) custom-call(s32[1]{0:T(128)S(6)} %copy.9.refs_0_, s32[1]{0:T(128)S(6)} %copy.10.refs_1_, f32[1,16,64,128]{3,2,1,0:T(8,128)S(1)} %copy-done, f32[10,64,128]{2,1,0:T(8,128)S(1)} %get-tuple-element.18.refs_3_, f32[10,64,128]{2,1,0:T(8,128)S(1)} %get-tuple-element.19.refs_4_, ...), custom_call_target="tpu_custom_call" | custom-call | tf_op jit(solution)/shard_map/pallas_call | solution.py:267
  19.1 1.9 %collective-permute-start.2 = (f32[16,64,128]{2,1,0:T(8,128)S(1)}, f32[16,64,128]{2,1,0:T(8,128)S(1)}, u32[]{:S(2)}, u32[]{:S(2)}) collective-permute-start(f32[16,64,128]{2,1,0:T(8,128)S(1)} %get-tuple-element.30), channel_id=1, source_target_pairs={{0,16},{16,0},{32,48},{48,32},{64,80},{80,64},{96,112},{112,96},{1... | collective-permute-start | bytes 1572872 | tf_op jit(solution)/shard_map/ppermute | solution.py:277
  21.0 1.9 %collective-permute-done.2 = f32[16,64,128]{2,1,0:T(8,128)S(1)} collective-permute-done((f32[16,64,128]{2,1,0:T(8,128)S(1)}, f32[16,64,128]{2,1,0:T(8,128)S(1)}, u32[]{:S(2)}, u32[]{:S(2)}) %collective-permute-start.2) | collective-permute-done | bytes 524320 | tf_op jit(solution)/shard_map/ppermute | solution.py:277
  22.9 0.1 add.3
  22.9 37.9 %all_to_all.5 = f32[16,64,128]{2,1,0:T(8,128)S(1)} all-to-all(f32[16,64,128]{2,1,0:T(8,128)S(1)} %add.3), channel_id=1, replica_groups={{0,32,64,96,128,160,192,224,256,288,320,352,384,416,448,480},{16,48,80,..., dimensions={0} | all-to-all | bytes 1048576 | tf_op jit(solution)/shard_map/all_to_all | solution.py:279
  60.8 0.6 %reduce_sum.9 = f32[64,128]{1,0:T(8,128)} reduce(f32[16,64,128]{2,1,0:T(8,128)S(1)} %all_to_all.5, f32[]{:T(128)} %constant.0.clone.1), dimensions={0}, to_apply=%region_0.0 | reduce | flops 122880 | bytes 557060 | tf_op jit(solution)/shard_map/reduce_sum | solution.py:280
Async XLA Ops:
  0.0 10.3 %copy-start = (f32[1,16,64,128]{3,2,1,0:T(8,128)S(1)}, f32[1,16,64,128]{3,2,1,0:T(8,128)}, u32[]{:S(2)}) copy-start(f32[1,16,64,128]{3,2,1,0:T(8,128)} %refs_2_.3) | copy-start | bytes 1572868
  0.0 10.3 %copy-start.4 = (f32[1,16,64,128]{3,2,1,0:T(8,128)S(1)}, f32[1,16,64,128]{3,2,1,0:T(8,128)}, u32[]{:S(2)}) copy-start(f32[1,16,64,128]{3,2,1,0:T(8,128)} %refs_4_.1) | copy-start | bytes 1572868
  0.0 10.3 %copy-start.3 = (f32[1,16,64,128]{3,2,1,0:T(8,128)S(1)}, f32[1,16,64,128]{3,2,1,0:T(8,128)}, u32[]{:S(2)}) copy-start(f32[1,16,64,128]{3,2,1,0:T(8,128)} %refs_3_.1) | copy-start | bytes 1572868
  0.0 10.3 %copy-start.2 = (f32[1,16,64,128]{3,2,1,0:T(8,128)S(1)}, f32[1,16,64,128]{3,2,1,0:T(8,128)}, u32[]{:S(2)}) copy-start(f32[1,16,64,128]{3,2,1,0:T(8,128)} %refs_2_.2) | copy-start | bytes 1572868
  0.0 10.3 %copy-start.1 = (f32[1,16,64,128]{3,2,1,0:T(8,128)S(1)}, f32[1,16,64,128]{3,2,1,0:T(8,128)}, u32[]{:S(2)}) copy-start(f32[1,16,64,128]{3,2,1,0:T(8,128)} %refs_1_.2) | copy-start | bytes 1572868
  2.2 13.5 %collective-permute-start = (f32[10,64,128]{2,1,0:T(8,128)S(1)}, f32[10,64,128]{2,1,0:T(8,128)S(1)}, u32[]{:S(2)}, u32[]{:S(2)}) collective-permute-start(f32[10,64,128]{2,1,0:T(8,128)S(1)} %get-tuple-element.18.refs_3_), channel_id=1, source_target_pairs={{1,2},{3,4},{5,6},{7,8},{9,10},{11,12},{13,14},{2,1},{4,3},{6,5},{... | collective-permute-start | bytes 983048 | tf_op jit(solution)/shard_map/ppermute | solution.py:253
  6.8 11.1 %collective-permute-start.1 = (f32[10,64,128]{2,1,0:T(8,128)S(1)}, f32[10,64,128]{2,1,0:T(8,128)S(1)}, u32[]{:S(2)}, u32[]{:S(2)}) collective-permute-start(f32[10,64,128]{2,1,0:T(8,128)S(1)} %get-tuple-element.19.refs_4_), channel_id=1, source_target_pairs={{0,1},{2,3},{4,5},{6,7},{8,9},{10,11},{12,13},{14,15},{1,0},{3,2},... | collective-permute-start | bytes 983048 | tf_op jit(solution)/shard_map/ppermute | solution.py:253
  10.4 0.9 %copy-start.5 = (f32[1,4,64,128]{3,2,1,0:T(8,128)S(1)}, f32[1,4,64,128]{3,2,1,0:T(8,128)}, u32[]{:S(2)}) copy-start(f32[1,4,64,128]{3,2,1,0:T(8,128)} %refs_5_.1) | copy-start | bytes 393220
  19.1 3.8 %collective-permute-start.2 = (f32[16,64,128]{2,1,0:T(8,128)S(1)}, f32[16,64,128]{2,1,0:T(8,128)S(1)}, u32[]{:S(2)}, u32[]{:S(2)}) collective-permute-start(f32[16,64,128]{2,1,0:T(8,128)S(1)} %get-tuple-element.30), channel_id=1, source_target_pairs={{0,16},{16,0},{32,48},{48,32},{64,80},{80,64},{96,112},{112,96},{1... | collective-permute-start | bytes 1572872 | tf_op jit(solution)/shard_map/ppermute | solution.py:277

commit v7 on v6

--- a/solution.py
+++ b/solution.py
@@ -26,7 +26,7 @@
 
 def sides():
     odd = lax.rem(lax.axis_index("dom"), 2)
-    return odd, 1 - odd
+    return 1 - odd, odd
 
 
 def edges(steps, depth, vel, wave, wave_old, adj, adj_old, first, second, *scratch):
@@ -252,7 +252,7 @@
         lower = range(begin, doms - 1, 2)
         return lax.ppermute(message, "dom", [(i, i + 1) for i in lower] + [(i + 1, i) for i in lower])
 
-    from_first, from_second = exchange(first, 1), exchange(second, 0)
+    from_first, from_second = exchange(first, 0), exchange(second, 1)
 
     inner = pl.pallas_call(
         functools.partial(slab, steps, depth),

time: 61.7 us -> 61.7 us (level)
  blocking collectives: 37.9 us -> 37 us
    all_to_all x1, blocking collectives: 37.9 us -> 37 us  [shards(): lax.all_to_all(both, 'shot', 0, 0, tiled=True, axis_index_groups=groups)]
  transfers between devices with their start and end apart: 3 -> 3, of which waited for: 3 -> 2; matrix products, arithmetic and copies ran while one was open for 0% -> 0% of each run, Pallas kernels for 4% -> 4%
where the time goes in v7:
time: 61.7 us; the launch traced here: 61.5 us
  blocking collectives  37 us (60%)
  starting transfers between devices  9.21 us (15%)
  waiting for transfers between devices  6.38 us (10%)
  Pallas kernels  5.89 us (10%)
  between operations  1.42 us (2%)
  local copies, waits for them, and re-layouts  0.92 us (1%)
  other arithmetic  0.73 us (1%)
    all_to_all x1, blocking collectives, shards(): lax.all_to_all(both, 'shot', 0, 0, tiled=True, axis_index_groups=groups)  37 us
    ppermute x2, starting transfers between devices, exchange(): lax.ppermute(message, 'dom', [(i, i + 1) for i in lower] + [(i + 1, i) fo...  7.29 us
    ppermute x2, waiting for transfers between devices, exchange(): lax.ppermute(message, 'dom', [(i, i + 1) for i in lower] + [(i + 1, i) fo...  4.51 us
    pallas_call x1, Pallas kernels, shards(): pl.pallas_call(functools.partial(slab, steps, depth), out_shape=(field,)...  2.5 us
    pallas_call x1, Pallas kernels, shards(): pl.pallas_call(functools.partial(edges, steps, depth), out_shape=(message...  2.17 us
    ppermute x1, starting transfers between devices, shards(): both = own + lax.ppermute(other, 'shot', pair)  1.92 us
    ppermute x1, waiting for transfers between devices, shards(): both = own + lax.ppermute(other, 'shot', pair)  1.88 us
  transfers between devices with their start and end apart: 3, of which 2 were waited for; matrix products, arithmetic and copies ran while one was open for 0% of the time, Pallas kernels for 4%

profile of v7, /device:TPU:8, one launch (start us, length us, event | category | flops | bytes accessed | tf_op | source)
XLA Modules:
  0.0 61.5 jit_solution(3205135575375210063)
XLA Ops:
  0.0 0.0 copy-start
  0.0 0.0 copy-start.4
  0.0 0.0 copy-start.3
  0.0 0.0 copy-start.2
  0.0 0.0 copy-start.1
  0.0 2.2 %shard_map.82 = (f32[10,64,128]{2,1,0:T(8,128)S(1)}, f32[10,64,128]{2,1,0:T(8,128)S(1)}) custom-call(f32[1,16,64,128]{3,2,1,0:T(8,128)} %refs_2_.3, f32[1,16,64,128]{3,2,1,0:T(8,128)} %refs_1_.2, f32[1,16,64,128]{3,2,1,0:T(8,128)} %refs_2_.2, f32[1,16,64,128]{3,2,1,0:T(8,128)} %refs_3_.1, f32[1,16,64,128]{3,2,1,0:T(8,128)} %refs_4_.1), custom_call_target="tpu_custom_call" | custom-call | tf_op jit(solution)/shard_map/pallas_call | solution.py:242
  2.2 3.4 %collective-permute-start = (f32[10,64,128]{2,1,0:T(8,128)S(1)}, f32[10,64,128]{2,1,0:T(8,128)S(1)}, u32[]{:S(2)}, u32[]{:S(2)}) collective-permute-start(f32[10,64,128]{2,1,0:T(8,128)S(1)} %get-tuple-element.18.refs_3_), channel_id=1, source_target_pairs={{0,1},{2,3},{4,5},{6,7},{8,9},{10,11},{12,13},{14,15},{1,0},{3,2},... | collective-permute-start | bytes 983048 | tf_op jit(solution)/shard_map/ppermute | solution.py:253
  5.6 3.9 %collective-permute-start.1 = (f32[10,64,128]{2,1,0:T(8,128)S(1)}, f32[10,64,128]{2,1,0:T(8,128)S(1)}, u32[]{:S(2)}, u32[]{:S(2)}) collective-permute-start(f32[10,64,128]{2,1,0:T(8,128)S(1)} %get-tuple-element.19.refs_4_), channel_id=1, source_target_pairs={{1,2},{3,4},{5,6},{7,8},{9,10},{11,12},{13,14},{2,1},{4,3},{6,5},{... | collective-permute-start | bytes 983048 | tf_op jit(solution)/shard_map/ppermute | solution.py:253
  10.8 0.0 copy-done
  10.8 0.0 copy-done.4
  10.8 0.0 copy-done.3
  10.8 0.0 copy-done.2
  10.8 0.0 copy-done.1
  10.9 0.0 copy-start.5
  10.9 0.9 %copy-done.5 = f32[1,4,64,128]{3,2,1,0:T(8,128)S(1)} copy-done((f32[1,4,64,128]{3,2,1,0:T(8,128)S(1)}, f32[1,4,64,128]{3,2,1,0:T(8,128)}, u32[]{:S(2)}) %copy-start.5) | copy-done | bytes 131096
  11.8 2.5 %shard_map.83 = (f32[16,64,128]{2,1,0:T(8,128)S(1)}, f32[16,64,128]{2,1,0:T(8,128)S(1)}, f32[16,64,128]{2,1,0:T(8,128)S(1)}, f32[16,64,128]{2,1,0:T(8,128)S(1)},...) custom-call(f32[1,16,64,128]{3,2,1,0:T(8,128)S(1)} %copy-done, ...), custom_call_target="tpu_custom_call" | custom-call | flops 40000000 | bytes 16000000 | tf_op jit(solution)/shard_map/pallas_call | solution.py:257
  14.3 0.0 collective-permute-done.refs_5_
  14.3 4.5 %collective-permute-done.1.refs_6_ = f32[10,64,128]{2,1,0:T(8,128)S(1)} collective-permute-done((f32[10,64,128]{2,1,0:T(8,128)S(1)}, f32[10,64,128]{2,1,0:T(8,128)S(1)}, u32[]{:S(2)}, u32[]{:S(2)}) %collective-permute-start.1) | collective-permute-done | bytes 327712 | tf_op jit(solution)/shard_map/ppermute | solution.py:253
  18.8 1.2 %shard_map.84 = (f32[16,64,128]{2,1,0:T(8,128)S(1)}, f32[16,64,128]{2,1,0:T(8,128)S(1)}) custom-call(s32[1]{0:T(128)S(6)} %copy.9.refs_0_, s32[1]{0:T(128)S(6)} %copy.10.refs_1_, f32[1,16,64,128]{3,2,1,0:T(8,128)S(1)} %copy-done, f32[10,64,128]{2,1,0:T(8,128)S(1)} %get-tuple-element.18.refs_3_, f32[10,64,128]{2,1,0:T(8,128)S(1)} %get-tuple-element.19.refs_4_, ...), custom_call_target="tpu_custom_call" | custom-call | tf_op jit(solution)/shard_map/pallas_call | solution.py:267
  20.0 1.9 %collective-permute-start.2 = (f32[16,64,128]{2,1,0:T(8,128)S(1)}, f32[16,64,128]{2,1,0:T(8,128)S(1)}, u32[]{:S(2)}, u32[]{:S(2)}) collective-permute-start(f32[16,64,128]{2,1,0:T(8,128)S(1)} %get-tuple-element.30), channel_id=1, source_target_pairs={{0,16},{16,0},{32,48},{48,32},{64,80},{80,64},{96,112},{112,96},{1... | collective-permute-start | bytes 1572872 | tf_op jit(solution)/shard_map/ppermute | solution.py:277
  21.9 1.9 %collective-permute-done.2 = f32[16,64,128]{2,1,0:T(8,128)S(1)} collective-permute-done((f32[16,64,128]{2,1,0:T(8,128)S(1)}, f32[16,64,128]{2,1,0:T(8,128)S(1)}, u32[]{:S(2)}, u32[]{:S(2)}) %collective-permute-start.2) | collective-permute-done | bytes 524320 | tf_op jit(solution)/shard_map/ppermute | solution.py:277
  23.8 0.1 add.3
  23.9 37.0 %all_to_all.5 = f32[16,64,128]{2,1,0:T(8,128)S(1)} all-to-all(f32[16,64,128]{2,1,0:T(8,128)S(1)} %add.3), channel_id=1, replica_groups={{0,32,64,96,128,160,192,224,256,288,320,352,384,416,448,480},{16,48,80,..., dimensions={0} | all-to-all | bytes 1048576 | tf_op jit(solution)/shard_map/all_to_all | solution.py:279
  60.9 0.6 %reduce_sum.9 = f32[64,128]{1,0:T(8,128)} reduce(f32[16,64,128]{2,1,0:T(8,128)S(1)} %all_to_all.5, f32[]{:T(128)} %constant.0.clone.1), dimensions={0}, to_apply=%region_0.0 | reduce | flops 122880 | bytes 557060 | tf_op jit(solution)/shard_map/reduce_sum | solution.py:280
Async XLA Ops:
  0.0 10.8 %copy-start = (f32[1,16,64,128]{3,2,1,0:T(8,128)S(1)}, f32[1,16,64,128]{3,2,1,0:T(8,128)}, u32[]{:S(2)}) copy-start(f32[1,16,64,128]{3,2,1,0:T(8,128)} %refs_2_.3) | copy-start | bytes 1572868
  0.0 10.8 %copy-start.4 = (f32[1,16,64,128]{3,2,1,0:T(8,128)S(1)}, f32[1,16,64,128]{3,2,1,0:T(8,128)}, u32[]{:S(2)}) copy-start(f32[1,16,64,128]{3,2,1,0:T(8,128)} %refs_4_.1) | copy-start | bytes 1572868
  0.0 10.8 %copy-start.3 = (f32[1,16,64,128]{3,2,1,0:T(8,128)S(1)}, f32[1,16,64,128]{3,2,1,0:T(8,128)}, u32[]{:S(2)}) copy-start(f32[1,16,64,128]{3,2,1,0:T(8,128)} %refs_3_.1) | copy-start | bytes 1572868
  0.0 10.8 %copy-start.2 = (f32[1,16,64,128]{3,2,1,0:T(8,128)S(1)}, f32[1,16,64,128]{3,2,1,0:T(8,128)}, u32[]{:S(2)}) copy-start(f32[1,16,64,128]{3,2,1,0:T(8,128)} %refs_2_.2) | copy-start | bytes 1572868
  0.0 10.8 %copy-start.1 = (f32[1,16,64,128]{3,2,1,0:T(8,128)S(1)}, f32[1,16,64,128]{3,2,1,0:T(8,128)}, u32[]{:S(2)}) copy-start(f32[1,16,64,128]{3,2,1,0:T(8,128)} %refs_1_.2) | copy-start | bytes 1572868
  2.2 12.1 %collective-permute-start = (f32[10,64,128]{2,1,0:T(8,128)S(1)}, f32[10,64,128]{2,1,0:T(8,128)S(1)}, u32[]{:S(2)}, u32[]{:S(2)}) collective-permute-start(f32[10,64,128]{2,1,0:T(8,128)S(1)} %get-tuple-element.18.refs_3_), channel_id=1, source_target_pairs={{0,1},{2,3},{4,5},{6,7},{8,9},{10,11},{12,13},{14,15},{1,0},{3,2},... | collective-permute-start | bytes 983048 | tf_op jit(solution)/shard_map/ppermute | solution.py:253
  5.6 13.2 %collective-permute-start.1 = (f32[10,64,128]{2,1,0:T(8,128)S(1)}, f32[10,64,128]{2,1,0:T(8,128)S(1)}, u32[]{:S(2)}, u32[]{:S(2)}) collective-permute-start(f32[10,64,128]{2,1,0:T(8,128)S(1)} %get-tuple-element.19.refs_4_), channel_id=1, source_target_pairs={{1,2},{3,4},{5,6},{7,8},{9,10},{11,12},{13,14},{2,1},{4,3},{6,5},{... | collective-permute-start | bytes 983048 | tf_op jit(solution)/shard_map/ppermute | solution.py:253
  10.9 0.9 %copy-start.5 = (f32[1,4,64,128]{3,2,1,0:T(8,128)S(1)}, f32[1,4,64,128]{3,2,1,0:T(8,128)}, u32[]{:S(2)}) copy-start(f32[1,4,64,128]{3,2,1,0:T(8,128)} %refs_5_.1) | copy-start | bytes 393220
  20.0 3.8 %collective-permute-start.2 = (f32[16,64,128]{2,1,0:T(8,128)S(1)}, f32[16,64,128]{2,1,0:T(8,128)S(1)}, u32[]{:S(2)}, u32[]{:S(2)}) collective-permute-start(f32[16,64,128]{2,1,0:T(8,128)S(1)} %get-tuple-element.30), channel_id=1, source_target_pairs={{0,16},{16,0},{32,48},{48,32},{64,80},{80,64},{96,112},{112,96},{1... | collective-permute-start | bytes 1572872 | tf_op jit(solution)/shard_map/ppermute | solution.py:277

commit v8 on v4

--- a/solution.py
+++ b/solution.py
@@ -28,17 +28,20 @@
     _, _, width, size = vel.shape
     lateral = Lateral(width, size)
     fetched, sems = scratch[:5], scratch[5]
-    copies = []
-    for i, (ref, held) in enumerate(zip((vel, wave, wave_old, adj, adj_old), fetched)):
-        for side, begin in enumerate((0, depth - steps)):
-            copies.append(pltpu.make_async_copy(ref.at[0, pl.ds(begin, steps)], held.at[side], sems.at[i, side]))
-    for copy in copies:
+    copies = [
+        [
+            pltpu.make_async_copy(ref.at[0, pl.ds(begin, steps)], held.at[side], sems.at[side, i])
+            for i, (ref, held) in enumerate(zip((vel, wave, wave_old, adj, adj_old), fetched))
+        ]
+        for side, begin in enumerate((0, depth - steps))
+    ]
+    for copy in copies[0] + copies[1]:
         copy.start()
-    for copy in copies:
-        copy.wait()
     vel, wave, wave_old, adj, adj_old = fetched
     for out, top in ((down, False), (up, True)):
         side = int(top)
+        for copy in copies[side]:
+            copy.wait()
         at = [steps - 1 - k if top else k for k in range(steps)]
         v = [vel[side, z] for z in at]
         out[2 * steps] = v[0]
@@ -113,6 +116,10 @@
             if step < steps - 1:
                 old = wave_old[z] if step == 0 else target[z + 1]
                 target[z + 1] = 2.0 * middle - old + vel[z] * lap
+
+
+def snake(k):
+    return k ^ (k // 2 % 2) if isinstance(k, int) else k + lax.rem(lax.div(k, 2), 2) * (1 - 2 * lax.rem(k, 2))
 
 
 def finish(steps, depth, blocks, *refs):
@@ -209,7 +216,7 @@
     @pl.loop(0, half)
     def _(i):
         for ref, j in ((own, 2 * i + odd), (other, 2 * i + 1 - odd)):
-            k = lax.div(start + j, 2)
+            k = snake(lax.div(start + j, 2))
             ref[k] = jnp.where(j < live, blocked[j], 0.0)
             ref[lax.rem(k + half, blocks)] = zero
 
@@ -234,7 +241,7 @@
         out_shape=(message, message),
         in_specs=[hbm] * 5,
         out_specs=(vmem, vmem),
-        scratch_shapes=[pltpu.VMEM((2, steps, width, size), f32)] * 5 + [pltpu.SemaphoreType.DMA((5, 2))],
+        scratch_shapes=[pltpu.VMEM((2, steps, width, size), f32)] * 5 + [pltpu.SemaphoreType.DMA((2, 5))],
         compiler_params=pltpu.CompilerParams(vmem_limit_bytes=53 * 2**20),
     )(vel, wave, wave_old, adj, adj_old)
 
@@ -262,7 +269,7 @@
 
     pair = [(s, s + 1 - 2 * (s % 2)) for s in range(shots)]
     both = own + lax.ppermute(other, "shot", pair)
-    groups = [[2 * k + c for k in range(blocks)] for c in range(2)]
+    groups = [[2 * snake(k) + c for k in range(blocks)] for c in range(2)]
     parts = lax.all_to_all(both, "shot", 0, 0, tiled=True, axis_index_groups=groups)
     return jnp.sum(parts, axis=0).reshape(1, depth, span, size)
 

time: 59.8 us -> 59.4 us (level)
  the two profiles are of different devices: /device:TPU:8 before, /device:TPU:22 now
where the time goes in v8:
time: 59.4 us; the launch traced here: 59.2 us
  blocking collectives  34.6 us (58%)
  waiting for transfers between devices  7.84 us (13%)
  starting transfers between devices  7.76 us (13%)
  Pallas kernels  5.89 us (10%)
  between operations  1.41 us (2%)
  local copies, waits for them, and re-layouts  0.92 us (2%)
  other arithmetic  0.73 us (1%)
    all_to_all x1, blocking collectives, shards(): lax.all_to_all(both, 'shot', 0, 0, tiled=True, axis_index_groups=groups)  34.6 us
    ppermute x1, waiting for transfers between devices, shards(): high = lax.ppermute(down, 'dom', [(i + 1, i) for i in range(doms - 1)])  5.24 us
    ppermute x1, starting transfers between devices, shards(): low = lax.ppermute(up, 'dom', [(i, i + 1) for i in range(doms - 1)])  3.4 us
    pallas_call x1, Pallas kernels, shards(): pl.pallas_call(functools.partial(slab, steps, depth), out_shape=(field,)...  2.5 us
    ppermute x1, starting transfers between devices, shards(): high = lax.ppermute(down, 'dom', [(i + 1, i) for i in range(doms - 1)])  2.44 us
    pallas_call x1, Pallas kernels, shards(): pl.pallas_call(functools.partial(edges, steps, depth), out_shape=(message...  2.15 us
    ppermute x1, starting transfers between devices, shards(): both = own + lax.ppermute(other, 'shot', pair)  1.92 us
    ppermute x1, waiting for transfers between devices, shards(): both = own + lax.ppermute(other, 'shot', pair)  1.88 us
  transfers between devices with their start and end apart: 3, of which 3 were waited for; matrix products, arithmetic and copies ran while one was open for 0% of the time, Pallas kernels for 4%

profile of v8, /device:TPU:22, one launch (start us, length us, event | category | flops | bytes accessed | tf_op | source)
XLA Modules:
  0.0 59.2 jit_solution(14087306896326370355)
XLA Ops:
  0.0 0.0 copy-start
  0.0 0.0 copy-start.4
  0.0 0.0 copy-start.3
  0.0 0.0 copy-start.2
  0.0 0.0 copy-start.1
  0.0 2.2 %shard_map.82 = (f32[10,64,128]{2,1,0:T(8,128)S(1)}, f32[10,64,128]{2,1,0:T(8,128)S(1)}) custom-call(f32[1,16,64,128]{3,2,1,0:T(8,128)} %refs_2_.3, f32[1,16,64,128]{3,2,1,0:T(8,128)} %refs_1_.2, f32[1,16,64,128]{3,2,1,0:T(8,128)} %refs_2_.2, f32[1,16,64,128]{3,2,1,0:T(8,128)} %refs_3_.1, f32[1,16,64,128]{3,2,1,0:T(8,128)} %refs_4_.1), custom_call_target="tpu_custom_call" | custom-call | tf_op jit(solution)/shard_map/pallas_call | solution.py:239
  2.2 3.4 %collective-permute-start = (f32[10,64,128]{2,1,0:T(8,128)S(1)}, f32[10,64,128]{2,1,0:T(8,128)S(1)}, u32[]{:S(2)}, u32[]{:S(2)}) collective-permute-start(f32[10,64,128]{2,1,0:T(8,128)S(1)} %get-tuple-element.18.refs_3_), channel_id=1, source_target_pairs={{0,1},{1,2},{2,3},{3,4},{4,5},{5,6},{6,7},{7,8},{8,9},{9,10},{10,1... | collective-permute-start | bytes 983048 | tf_op jit(solution)/shard_map/ppermute | solution.py:248
  5.6 2.4 %collective-permute-start.1 = (f32[10,64,128]{2,1,0:T(8,128)S(1)}, f32[10,64,128]{2,1,0:T(8,128)S(1)}, u32[]{:S(2)}, u32[]{:S(2)}) collective-permute-start(f32[10,64,128]{2,1,0:T(8,128)S(1)} %get-tuple-element.19.refs_4_), channel_id=1, source_target_pairs={{1,0},{2,1},{3,2},{4,3},{5,4},{6,5},{7,6},{8,7},{9,8},{10,9},{11,1... | collective-permute-start | bytes 983048 | tf_op jit(solution)/shard_map/ppermute | solution.py:249
  9.3 0.0 copy-done
  9.4 0.0 copy-done.4
  9.4 0.0 copy-done.3
  9.4 0.0 copy-done.2
  9.4 0.0 copy-done.1
  9.4 0.0 copy-start.5
  9.4 0.9 %copy-done.5 = f32[1,4,64,128]{3,2,1,0:T(8,128)S(1)} copy-done((f32[1,4,64,128]{3,2,1,0:T(8,128)S(1)}, f32[1,4,64,128]{3,2,1,0:T(8,128)}, u32[]{:S(2)}) %copy-start.5) | copy-done | bytes 131096
  10.3 2.5 %shard_map.83 = (f32[16,64,128]{2,1,0:T(8,128)S(1)}, f32[16,64,128]{2,1,0:T(8,128)S(1)}, f32[16,64,128]{2,1,0:T(8,128)S(1)}, f32[16,64,128]{2,1,0:T(8,128)S(1)},...) custom-call(f32[1,16,64,128]{3,2,1,0:T(8,128)S(1)} %copy-done, ...), custom_call_target="tpu_custom_call" | custom-call | flops 40000000 | bytes 16000000 | tf_op jit(solution)/shard_map/pallas_call | solution.py:251
  12.8 0.7 %collective-permute-done.refs_5_ = f32[10,64,128]{2,1,0:T(8,128)S(1)} collective-permute-done((f32[10,64,128]{2,1,0:T(8,128)S(1)}, f32[10,64,128]{2,1,0:T(8,128)S(1)}, u32[]{:S(2)}, u32[]{:S(2)}) %collective-permute-start) | collective-permute-done | bytes 327712 | tf_op jit(solution)/shard_map/ppermute | solution.py:248
  13.5 5.2 %collective-permute-done.1.refs_6_ = f32[10,64,128]{2,1,0:T(8,128)S(1)} collective-permute-done((f32[10,64,128]{2,1,0:T(8,128)S(1)}, f32[10,64,128]{2,1,0:T(8,128)S(1)}, u32[]{:S(2)}, u32[]{:S(2)}) %collective-permute-start.1) | collective-permute-done | bytes 327712 | tf_op jit(solution)/shard_map/ppermute | solution.py:249
  18.8 1.2 %shard_map.84 = (f32[16,64,128]{2,1,0:T(8,128)S(1)}, f32[16,64,128]{2,1,0:T(8,128)S(1)}) custom-call(s32[1]{0:T(128)S(6)} %copy.9.refs_0_, s32[1]{0:T(128)S(6)} %copy.10.refs_1_, f32[1,16,64,128]{3,2,1,0:T(8,128)S(1)} %copy-done, f32[10,64,128]{2,1,0:T(8,128)S(1)} %get-tuple-element.18.refs_3_, f32[10,64,128]{2,1,0:T(8,128)S(1)} %get-tuple-element.19.refs_4_, ...), custom_call_target="tpu_custom_call" | custom-call | tf_op jit(solution)/shard_map/pallas_call | solution.py:261
  20.0 1.9 %collective-permute-start.2 = (f32[16,64,128]{2,1,0:T(8,128)S(1)}, f32[16,64,128]{2,1,0:T(8,128)S(1)}, u32[]{:S(2)}, u32[]{:S(2)}) collective-permute-start(f32[16,64,128]{2,1,0:T(8,128)S(1)} %get-tuple-element.30), channel_id=1, source_target_pairs={{0,16},{16,0},{32,48},{48,32},{64,80},{80,64},{96,112},{112,96},{1... | collective-permute-start | bytes 1572872 | tf_op jit(solution)/shard_map/ppermute | solution.py:271
  21.9 1.9 %collective-permute-done.2 = f32[16,64,128]{2,1,0:T(8,128)S(1)} collective-permute-done((f32[16,64,128]{2,1,0:T(8,128)S(1)}, f32[16,64,128]{2,1,0:T(8,128)S(1)}, u32[]{:S(2)}, u32[]{:S(2)}) %collective-permute-start.2) | collective-permute-done | bytes 524320 | tf_op jit(solution)/shard_map/ppermute | solution.py:271
  23.8 0.1 add.3
  23.9 34.6 %all_to_all.5 = f32[16,64,128]{2,1,0:T(8,128)S(1)} all-to-all(f32[16,64,128]{2,1,0:T(8,128)S(1)} %add.3), channel_id=1, replica_groups={{0,32,96,64,128,160,224,192,256,288,352,320,384,416,480,448},{16,48,112..., dimensions={0} | all-to-all | bytes 1048576 | tf_op jit(solution)/shard_map/all_to_all | solution.py:273
  58.6 0.6 %reduce_sum.9 = f32[64,128]{1,0:T(8,128)} reduce(f32[16,64,128]{2,1,0:T(8,128)S(1)} %all_to_all.5, f32[]{:T(128)} %constant.0.clone.1), dimensions={0}, to_apply=%region_0.0 | reduce | flops 122880 | bytes 557060 | tf_op jit(solution)/shard_map/reduce_sum | solution.py:274
Async XLA Ops:
  0.0 9.3 %copy-start = (f32[1,16,64,128]{3,2,1,0:T(8,128)S(1)}, f32[1,16,64,128]{3,2,1,0:T(8,128)}, u32[]{:S(2)}) copy-start(f32[1,16,64,128]{3,2,1,0:T(8,128)} %refs_2_.3) | copy-start | bytes 1572868
  0.0 9.4 %copy-start.4 = (f32[1,16,64,128]{3,2,1,0:T(8,128)S(1)}, f32[1,16,64,128]{3,2,1,0:T(8,128)}, u32[]{:S(2)}) copy-start(f32[1,16,64,128]{3,2,1,0:T(8,128)} %refs_4_.1) | copy-start | bytes 1572868
  0.0 9.4 %copy-start.3 = (f32[1,16,64,128]{3,2,1,0:T(8,128)S(1)}, f32[1,16,64,128]{3,2,1,0:T(8,128)}, u32[]{:S(2)}) copy-start(f32[1,16,64,128]{3,2,1,0:T(8,128)} %refs_3_.1) | copy-start | bytes 1572868
  0.0 9.4 %copy-start.2 = (f32[1,16,64,128]{3,2,1,0:T(8,128)S(1)}, f32[1,16,64,128]{3,2,1,0:T(8,128)}, u32[]{:S(2)}) copy-start(f32[1,16,64,128]{3,2,1,0:T(8,128)} %refs_2_.2) | copy-start | bytes 1572868
  0.0 9.4 %copy-start.1 = (f32[1,16,64,128]{3,2,1,0:T(8,128)S(1)}, f32[1,16,64,128]{3,2,1,0:T(8,128)}, u32[]{:S(2)}) copy-start(f32[1,16,64,128]{3,2,1,0:T(8,128)} %refs_1_.2) | copy-start | bytes 1572868
  2.2 11.3 %collective-permute-start = (f32[10,64,128]{2,1,0:T(8,128)S(1)}, f32[10,64,128]{2,1,0:T(8,128)S(1)}, u32[]{:S(2)}, u32[]{:S(2)}) collective-permute-start(f32[10,64,128]{2,1,0:T(8,128)S(1)} %get-tuple-element.18.refs_3_), channel_id=1, source_target_pairs={{0,1},{1,2},{2,3},{3,4},{4,5},{5,6},{6,7},{7,8},{8,9},{9,10},{10,1... | collective-permute-start | bytes 983048 | tf_op jit(solution)/shard_map/ppermute | solution.py:248
  5.6 13.2 %collective-permute-start.1 = (f32[10,64,128]{2,1,0:T(8,128)S(1)}, f32[10,64,128]{2,1,0:T(8,128)S(1)}, u32[]{:S(2)}, u32[]{:S(2)}) collective-permute-start(f32[10,64,128]{2,1,0:T(8,128)S(1)} %get-tuple-element.19.refs_4_), channel_id=1, source_target_pairs={{1,0},{2,1},{3,2},{4,3},{5,4},{6,5},{7,6},{8,7},{9,8},{10,9},{11,1... | collective-permute-start | bytes 983048 | tf_op jit(solution)/shard_map/ppermute | solution.py:249
  9.4 0.9 %copy-start.5 = (f32[1,4,64,128]{3,2,1,0:T(8,128)S(1)}, f32[1,4,64,128]{3,2,1,0:T(8,128)}, u32[]{:S(2)}) copy-start(f32[1,4,64,128]{3,2,1,0:T(8,128)} %refs_5_.1) | copy-start | bytes 393220
  20.0 3.8 %collective-permute-start.2 = (f32[16,64,128]{2,1,0:T(8,128)S(1)}, f32[16,64,128]{2,1,0:T(8,128)S(1)}, u32[]{:S(2)}, u32[]{:S(2)}) collective-permute-start(f32[16,64,128]{2,1,0:T(8,128)S(1)} %get-tuple-element.30), channel_id=1, source_target_pairs={{0,16},{16,0},{32,48},{48,32},{64,80},{80,64},{96,112},{112,96},{1... | collective-permute-start | bytes 1572872 | tf_op jit(solution)/shard_map/ppermute | solution.py:271

commit v9 on v8

--- a/solution.py
+++ b/solution.py
@@ -24,7 +24,7 @@
         return (above + below) + (left + right) - 6.0 * middle
 
 
-def edges(steps, depth, vel, wave, wave_old, adj, adj_old, up, down, *scratch):
+def edges(steps, depth, vel, wave, wave_old, adj, adj_old, down, up, *scratch):
     _, _, width, size = vel.shape
     lateral = Lateral(width, size)
     fetched, sems = scratch[:5], scratch[5]
@@ -123,7 +123,7 @@
 
 
 def finish(steps, depth, blocks, *refs):
-    offset, count, vel, up, down, low, high = refs[:7]
+    offset, count, vel, down, up, high, low = refs[:7]
     vel = vel.at[0]
     laps, adjoints, img = refs[7 : 7 + steps], refs[7 + steps : 7 + 2 * steps], refs[7 + 2 * steps]
     own, other, blocked = refs[8 + 2 * steps :]
@@ -236,7 +236,7 @@
     field = jax.ShapeDtypeStruct((depth, width, size), f32)
     block = jax.ShapeDtypeStruct((blocks, depth * span, size), f32)
 
-    up, down = pl.pallas_call(
+    down, up = pl.pallas_call(
         functools.partial(edges, steps, depth),
         out_shape=(message, message),
         in_specs=[hbm] * 5,
@@ -245,8 +245,8 @@
         compiler_params=pltpu.CompilerParams(vmem_limit_bytes=53 * 2**20),
     )(vel, wave, wave_old, adj, adj_old)
 
+    high = lax.ppermute(down, "dom", [(i + 1, i) for i in range(doms - 1)])
     low = lax.ppermute(up, "dom", [(i, i + 1) for i in range(doms - 1)])
-    high = lax.ppermute(down, "dom", [(i + 1, i) for i in range(doms - 1)])
 
     inner = pl.pallas_call(
         functools.partial(slab, steps, depth),
@@ -265,7 +265,7 @@
         out_specs=(vmem, vmem),
         scratch_shapes=[pltpu.VMEM((blocks, depth * span, size), f32)],
         compiler_params=room,
-    )(offset, count, vel, up, down, low, high, *inner)
+    )(offset, count, vel, down, up, high, low, *inner)
 
     pair = [(s, s + 1 - 2 * (s % 2)) for s in range(shots)]
     both = own + lax.ppermute(other, "shot", pair)

time: 59.4 us -> 62.9 us (1.059)
  the two profiles are of different devices: /device:TPU:22 before, /device:TPU:8 now
where the time goes in v9:
time: 62.9 us; the launch traced here: 62.6 us
  blocking collectives  36.9 us (59%)
  starting transfers between devices  8.39 us (13%)
  waiting for transfers between devices  8.36 us (13%)
  Pallas kernels  5.89 us (9%)
  between operations  1.41 us (2%)
  local copies, waits for them, and re-layouts  0.92 us (1%)
  other arithmetic  0.73 us (1%)
    all_to_all x1, blocking collectives, shards(): lax.all_to_all(both, 'shot', 0, 0, tiled=True, axis_index_groups=groups)  36.9 us
    ppermute x1, waiting for transfers between devices, shards(): low = lax.ppermute(up, 'dom', [(i, i + 1) for i in range(doms - 1)])  6.23 us
    ppermute x1, starting transfers between devices, shards(): high = lax.ppermute(down, 'dom', [(i + 1, i) for i in range(doms - 1)])  4.55 us
    pallas_call x1, Pallas kernels, shards(): pl.pallas_call(functools.partial(slab, steps, depth), out_shape=(field,)...  2.5 us
    pallas_call x1, Pallas kernels, shards(): pl.pallas_call(functools.partial(edges, steps, depth), out_shape=(message...  2.15 us
    ppermute x1, starting transfers between devices, shards(): both = own + lax.ppermute(other, 'shot', pair)  1.92 us
    ppermute x1, starting transfers between devices, shards(): low = lax.ppermute(up, 'dom', [(i, i + 1) for i in range(doms - 1)])  1.92 us
    ppermute x1, waiting for transfers between devices, shards(): both = own + lax.ppermute(other, 'shot', pair)  1.88 us
  transfers between devices with their start and end apart: 3, of which 3 were waited for; matrix products, arithmetic and copies ran while one was open for 0% of the time, Pallas kernels for 4%

profile of v9, /device:TPU:8, one launch (start us, length us, event | category | flops | bytes accessed | tf_op | source)
XLA Modules:
  0.0 62.6 jit_solution(15260295165404751474)
XLA Ops:
  0.0 0.0 copy-start
  0.0 0.0 copy-start.4
  0.0 0.0 copy-start.3
  0.0 0.0 copy-start.2
  0.0 0.0 copy-start.1
  0.0 2.2 %shard_map.82 = (f32[10,64,128]{2,1,0:T(8,128)S(1)}, f32[10,64,128]{2,1,0:T(8,128)S(1)}) custom-call(f32[1,16,64,128]{3,2,1,0:T(8,128)} %refs_2_.3, f32[1,16,64,128]{3,2,1,0:T(8,128)} %refs_1_.2, f32[1,16,64,128]{3,2,1,0:T(8,128)} %refs_2_.2, f32[1,16,64,128]{3,2,1,0:T(8,128)} %refs_3_.1, f32[1,16,64,128]{3,2,1,0:T(8,128)} %refs_4_.1), custom_call_target="tpu_custom_call" | custom-call | tf_op jit(solution)/shard_map/pallas_call | solution.py:239
  2.2 4.6 %collective-permute-start = (f32[10,64,128]{2,1,0:T(8,128)S(1)}, f32[10,64,128]{2,1,0:T(8,128)S(1)}, u32[]{:S(2)}, u32[]{:S(2)}) collective-permute-start(f32[10,64,128]{2,1,0:T(8,128)S(1)} %get-tuple-element.18.refs_3_), channel_id=1, source_target_pairs={{1,0},{2,1},{3,2},{4,3},{5,4},{6,5},{7,6},{8,7},{9,8},{10,9},{11,1... | collective-permute-start | bytes 983048 | tf_op jit(solution)/shard_map/ppermute | solution.py:248
  6.7 1.9 %collective-permute-start.1 = (f32[10,64,128]{2,1,0:T(8,128)S(1)}, f32[10,64,128]{2,1,0:T(8,128)S(1)}, u32[]{:S(2)}, u32[]{:S(2)}) collective-permute-start(f32[10,64,128]{2,1,0:T(8,128)S(1)} %get-tuple-element.19.refs_4_), channel_id=1, source_target_pairs={{0,1},{1,2},{2,3},{3,4},{4,5},{5,6},{6,7},{7,8},{8,9},{9,10},{10,1... | collective-permute-start | bytes 983048 | tf_op jit(solution)/shard_map/ppermute | solution.py:249
  10.0 0.0 copy-done
  10.0 0.0 copy-done.4
  10.0 0.0 copy-done.3
  10.0 0.0 copy-done.2
  10.0 0.0 copy-done.1
  10.0 0.0 copy-start.5
  10.0 0.9 %copy-done.5 = f32[1,4,64,128]{3,2,1,0:T(8,128)S(1)} copy-done((f32[1,4,64,128]{3,2,1,0:T(8,128)S(1)}, f32[1,4,64,128]{3,2,1,0:T(8,128)}, u32[]{:S(2)}) %copy-start.5) | copy-done | bytes 131096
  10.9 2.5 %shard_map.83 = (f32[16,64,128]{2,1,0:T(8,128)S(1)}, f32[16,64,128]{2,1,0:T(8,128)S(1)}, f32[16,64,128]{2,1,0:T(8,128)S(1)}, f32[16,64,128]{2,1,0:T(8,128)S(1)},...) custom-call(f32[1,16,64,128]{3,2,1,0:T(8,128)S(1)} %copy-done, ...), custom_call_target="tpu_custom_call" | custom-call | flops 40000000 | bytes 16000000 | tf_op jit(solution)/shard_map/pallas_call | solution.py:251
  13.4 0.3 collective-permute-done.refs_5_
  13.7 6.2 %collective-permute-done.1.refs_6_ = f32[10,64,128]{2,1,0:T(8,128)S(1)} collective-permute-done((f32[10,64,128]{2,1,0:T(8,128)S(1)}, f32[10,64,128]{2,1,0:T(8,128)S(1)}, u32[]{:S(2)}, u32[]{:S(2)}) %collective-permute-start.1) | collective-permute-done | bytes 327712 | tf_op jit(solution)/shard_map/ppermute | solution.py:249
  19.9 1.2 %shard_map.84 = (f32[16,64,128]{2,1,0:T(8,128)S(1)}, f32[16,64,128]{2,1,0:T(8,128)S(1)}) custom-call(s32[1]{0:T(128)S(6)} %copy.9.refs_0_, s32[1]{0:T(128)S(6)} %copy.10.refs_1_, f32[1,16,64,128]{3,2,1,0:T(8,128)S(1)} %copy-done, f32[10,64,128]{2,1,0:T(8,128)S(1)} %get-tuple-element.18.refs_3_, f32[10,64,128]{2,1,0:T(8,128)S(1)} %get-tuple-element.19.refs_4_, ...), custom_call_target="tpu_custom_call" | custom-call | tf_op jit(solution)/shard_map/pallas_call | solution.py:261
  21.2 1.9 %collective-permute-start.2 = (f32[16,64,128]{2,1,0:T(8,128)S(1)}, f32[16,64,128]{2,1,0:T(8,128)S(1)}, u32[]{:S(2)}, u32[]{:S(2)}) collective-permute-start(f32[16,64,128]{2,1,0:T(8,128)S(1)} %get-tuple-element.30), channel_id=1, source_target_pairs={{0,16},{16,0},{32,48},{48,32},{64,80},{80,64},{96,112},{112,96},{1... | collective-permute-start | bytes 1572872 | tf_op jit(solution)/shard_map/ppermute | solution.py:271
  23.1 1.9 %collective-permute-done.2 = f32[16,64,128]{2,1,0:T(8,128)S(1)} collective-permute-done((f32[16,64,128]{2,1,0:T(8,128)S(1)}, f32[16,64,128]{2,1,0:T(8,128)S(1)}, u32[]{:S(2)}, u32[]{:S(2)}) %collective-permute-start.2) | collective-permute-done | bytes 524320 | tf_op jit(solution)/shard_map/ppermute | solution.py:271
  25.0 0.1 add.3
  25.1 36.9 %all_to_all.5 = f32[16,64,128]{2,1,0:T(8,128)S(1)} all-to-all(f32[16,64,128]{2,1,0:T(8,128)S(1)} %add.3), channel_id=1, replica_groups={{0,32,96,64,128,160,224,192,256,288,352,320,384,416,480,448},{16,48,112..., dimensions={0} | all-to-all | bytes 1048576 | tf_op jit(solution)/shard_map/all_to_all | solution.py:273
  62.0 0.6 %reduce_sum.9 = f32[64,128]{1,0:T(8,128)} reduce(f32[16,64,128]{2,1,0:T(8,128)S(1)} %all_to_all.5, f32[]{:T(128)} %constant.0.clone.1), dimensions={0}, to_apply=%region_0.0 | reduce | flops 122880 | bytes 557060 | tf_op jit(solution)/shard_map/reduce_sum | solution.py:274
Async XLA Ops:
  0.0 10.0 %copy-start = (f32[1,16,64,128]{3,2,1,0:T(8,128)S(1)}, f32[1,16,64,128]{3,2,1,0:T(8,128)}, u32[]{:S(2)}) copy-start(f32[1,16,64,128]{3,2,1,0:T(8,128)} %refs_2_.3) | copy-start | bytes 1572868
  0.0 10.0 %copy-start.4 = (f32[1,16,64,128]{3,2,1,0:T(8,128)S(1)}, f32[1,16,64,128]{3,2,1,0:T(8,128)}, u32[]{:S(2)}) copy-start(f32[1,16,64,128]{3,2,1,0:T(8,128)} %refs_4_.1) | copy-start | bytes 1572868
  0.0 10.0 %copy-start.3 = (f32[1,16,64,128]{3,2,1,0:T(8,128)S(1)}, f32[1,16,64,128]{3,2,1,0:T(8,128)}, u32[]{:S(2)}) copy-start(f32[1,16,64,128]{3,2,1,0:T(8,128)} %refs_3_.1) | copy-start | bytes 1572868
  0.0 10.0 %copy-start.2 = (f32[1,16,64,128]{3,2,1,0:T(8,128)S(1)}, f32[1,16,64,128]{3,2,1,0:T(8,128)}, u32[]{:S(2)}) copy-start(f32[1,16,64,128]{3,2,1,0:T(8,128)} %refs_2_.2) | copy-start | bytes 1572868
  0.0 10.0 %copy-start.1 = (f32[1,16,64,128]{3,2,1,0:T(8,128)S(1)}, f32[1,16,64,128]{3,2,1,0:T(8,128)}, u32[]{:S(2)}) copy-start(f32[1,16,64,128]{3,2,1,0:T(8,128)} %refs_1_.2) | copy-start | bytes 1572868
  2.2 11.5 %collective-permute-start = (f32[10,64,128]{2,1,0:T(8,128)S(1)}, f32[10,64,128]{2,1,0:T(8,128)S(1)}, u32[]{:S(2)}, u32[]{:S(2)}) collective-permute-start(f32[10,64,128]{2,1,0:T(8,128)S(1)} %get-tuple-element.18.refs_3_), channel_id=1, source_target_pairs={{1,0},{2,1},{3,2},{4,3},{5,4},{6,5},{7,6},{8,7},{9,8},{10,9},{11,1... | collective-permute-start | bytes 983048 | tf_op jit(solution)/shard_map/ppermute | solution.py:248
  6.7 13.2 %collective-permute-start.1 = (f32[10,64,128]{2,1,0:T(8,128)S(1)}, f32[10,64,128]{2,1,0:T(8,128)S(1)}, u32[]{:S(2)}, u32[]{:S(2)}) collective-permute-start(f32[10,64,128]{2,1,0:T(8,128)S(1)} %get-tuple-element.19.refs_4_), channel_id=1, source_target_pairs={{0,1},{1,2},{2,3},{3,4},{4,5},{5,6},{6,7},{7,8},{8,9},{9,10},{10,1... | collective-permute-start | bytes 983048 | tf_op jit(solution)/shard_map/ppermute | solution.py:249
  10.0 0.9 %copy-start.5 = (f32[1,4,64,128]{3,2,1,0:T(8,128)S(1)}, f32[1,4,64,128]{3,2,1,0:T(8,128)}, u32[]{:S(2)}) copy-start(f32[1,4,64,128]{3,2,1,0:T(8,128)} %refs_5_.1) | copy-start | bytes 393220
  21.2 3.8 %collective-permute-start.2 = (f32[16,64,128]{2,1,0:T(8,128)S(1)}, f32[16,64,128]{2,1,0:T(8,128)S(1)}, u32[]{:S(2)}, u32[]{:S(2)}) collective-permute-start(f32[16,64,128]{2,1,0:T(8,128)S(1)} %get-tuple-element.30), channel_id=1, source_target_pairs={{0,16},{16,0},{32,48},{48,32},{64,80},{80,64},{96,112},{112,96},{1... | collective-permute-start | bytes 1572872 | tf_op jit(solution)/shard_map/ppermute | solution.py:271

commit v10 on v8

--- a/solution.py
+++ b/solution.py
@@ -116,10 +116,6 @@
             if step < steps - 1:
                 old = wave_old[z] if step == 0 else target[z + 1]
                 target[z + 1] = 2.0 * middle - old + vel[z] * lap
-
-
-def snake(k):
-    return k ^ (k // 2 % 2) if isinstance(k, int) else k + lax.rem(lax.div(k, 2), 2) * (1 - 2 * lax.rem(k, 2))
 
 
 def finish(steps, depth, blocks, *refs):
@@ -216,7 +212,7 @@
     @pl.loop(0, half)
     def _(i):
         for ref, j in ((own, 2 * i + odd), (other, 2 * i + 1 - odd)):
-            k = snake(lax.div(start + j, 2))
+            k = lax.div(start + j, 2)
             ref[k] = jnp.where(j < live, blocked[j], 0.0)
             ref[lax.rem(k + half, blocks)] = zero
 
@@ -269,7 +265,7 @@
 
     pair = [(s, s + 1 - 2 * (s % 2)) for s in range(shots)]
     both = own + lax.ppermute(other, "shot", pair)
-    groups = [[2 * snake(k) + c for k in range(blocks)] for c in range(2)]
+    groups = [[2 * k + c for k in range(blocks)] for c in range(2)]
     parts = lax.all_to_all(both, "shot", 0, 0, tiled=True, axis_index_groups=groups)
     return jnp.sum(parts, axis=0).reshape(1, depth, span, size)
 

time: 59.4 us -> 59.7 us (level)
  the two profiles are of different devices: /device:TPU:22 before, /device:TPU:8 now
where the time goes in v10:
time: 59.7 us; the launch traced here: 59.5 us
  blocking collectives  37 us (62%)
  starting transfers between devices  9.87 us (17%)
  Pallas kernels  5.81 us (10%)
  waiting for transfers between devices  3.78 us (6%)
  between operations  1.41 us (2%)
  local copies, waits for them, and re-layouts  0.92 us (2%)
  other arithmetic  0.73 us (1%)
    all_to_all x1, blocking collectives, shards(): lax.all_to_all(both, 'shot', 0, 0, tiled=True, axis_index_groups=groups)  37 us
    ppermute x1, starting transfers between devices, shards(): high = lax.ppermute(down, 'dom', [(i + 1, i) for i in range(doms - 1)])  4.55 us
    ppermute x1, starting transfers between devices, shards(): low = lax.ppermute(up, 'dom', [(i, i + 1) for i in range(doms - 1)])  3.4 us
    pallas_call x1, Pallas kernels, shards(): pl.pallas_call(functools.partial(slab, steps, depth), out_shape=(field,)...  2.5 us
    pallas_call x1, Pallas kernels, shards(): pl.pallas_call(functools.partial(edges, steps, depth), out_shape=(message...  2.15 us
    ppermute x1, starting transfers between devices, shards(): both = own + lax.ppermute(other, 'shot', pair)  1.92 us
    ppermute x1, waiting for transfers between devices, shards(): both = own + lax.ppermute(other, 'shot', pair)  1.88 us
  transfers between devices with their start and end apart: 3, of which 3 were waited for; matrix products, arithmetic and copies ran while one was open for 0% of the time, Pallas kernels for 4%

profile of v10, /device:TPU:8, one launch (start us, length us, event | category | flops | bytes accessed | tf_op | source)
XLA Modules:
  0.0 59.5 jit_solution(15414416920935308935)
XLA Ops:
  0.0 0.0 copy-start
  0.0 0.0 copy-start.4
  0.0 0.0 copy-start.3
  0.0 0.0 copy-start.2
  0.0 0.0 copy-start.1
  0.0 2.2 %shard_map.82 = (f32[10,64,128]{2,1,0:T(8,128)S(1)}, f32[10,64,128]{2,1,0:T(8,128)S(1)}) custom-call(f32[1,16,64,128]{3,2,1,0:T(8,128)} %refs_2_.3, f32[1,16,64,128]{3,2,1,0:T(8,128)} %refs_1_.2, f32[1,16,64,128]{3,2,1,0:T(8,128)} %refs_2_.2, f32[1,16,64,128]{3,2,1,0:T(8,128)} %refs_3_.1, f32[1,16,64,128]{3,2,1,0:T(8,128)} %refs_4_.1), custom_call_target="tpu_custom_call" | custom-call | tf_op jit(solution)/shard_map/pallas_call | solution.py:235
  2.2 3.4 %collective-permute-start = (f32[10,64,128]{2,1,0:T(8,128)S(1)}, f32[10,64,128]{2,1,0:T(8,128)S(1)}, u32[]{:S(2)}, u32[]{:S(2)}) collective-permute-start(f32[10,64,128]{2,1,0:T(8,128)S(1)} %get-tuple-element.18.refs_3_), channel_id=1, source_target_pairs={{0,1},{1,2},{2,3},{3,4},{4,5},{5,6},{6,7},{7,8},{8,9},{9,10},{10,1... | collective-permute-start | bytes 983048 | tf_op jit(solution)/shard_map/ppermute | solution.py:244
  5.6 4.6 %collective-permute-start.1 = (f32[10,64,128]{2,1,0:T(8,128)S(1)}, f32[10,64,128]{2,1,0:T(8,128)S(1)}, u32[]{:S(2)}, u32[]{:S(2)}) collective-permute-start(f32[10,64,128]{2,1,0:T(8,128)S(1)} %get-tuple-element.19.refs_4_), channel_id=1, source_target_pairs={{1,0},{2,1},{3,2},{4,3},{5,4},{6,5},{7,6},{8,7},{9,8},{10,9},{11,1... | collective-permute-start | bytes 983048 | tf_op jit(solution)/shard_map/ppermute | solution.py:245
  11.5 0.0 copy-done
  11.5 0.0 copy-done.4
  11.5 0.0 copy-done.3
  11.5 0.0 copy-done.2
  11.5 0.0 copy-done.1
  11.5 0.0 copy-start.5
  11.5 0.9 %copy-done.5 = f32[1,4,64,128]{3,2,1,0:T(8,128)S(1)} copy-done((f32[1,4,64,128]{3,2,1,0:T(8,128)S(1)}, f32[1,4,64,128]{3,2,1,0:T(8,128)}, u32[]{:S(2)}) %copy-start.5) | copy-done | bytes 131096
  12.4 2.5 %shard_map.83 = (f32[16,64,128]{2,1,0:T(8,128)S(1)}, f32[16,64,128]{2,1,0:T(8,128)S(1)}, f32[16,64,128]{2,1,0:T(8,128)S(1)}, f32[16,64,128]{2,1,0:T(8,128)S(1)},...) custom-call(f32[1,16,64,128]{3,2,1,0:T(8,128)S(1)} %copy-done, ...), custom_call_target="tpu_custom_call" | custom-call | flops 40000000 | bytes 16000000 | tf_op jit(solution)/shard_map/pallas_call | solution.py:247
  14.9 0.7 %collective-permute-done.refs_5_ = f32[10,64,128]{2,1,0:T(8,128)S(1)} collective-permute-done((f32[10,64,128]{2,1,0:T(8,128)S(1)}, f32[10,64,128]{2,1,0:T(8,128)S(1)}, u32[]{:S(2)}, u32[]{:S(2)}) %collective-permute-start) | collective-permute-done | bytes 327712 | tf_op jit(solution)/shard_map/ppermute | solution.py:244
  15.6 1.2 %collective-permute-done.1.refs_6_ = f32[10,64,128]{2,1,0:T(8,128)S(1)} collective-permute-done((f32[10,64,128]{2,1,0:T(8,128)S(1)}, f32[10,64,128]{2,1,0:T(8,128)S(1)}, u32[]{:S(2)}, u32[]{:S(2)}) %collective-permute-start.1) | collective-permute-done | bytes 327712 | tf_op jit(solution)/shard_map/ppermute | solution.py:245
  16.8 1.2 %shard_map.84 = (f32[16,64,128]{2,1,0:T(8,128)S(1)}, f32[16,64,128]{2,1,0:T(8,128)S(1)}) custom-call(s32[1]{0:T(128)S(6)} %copy.9.refs_0_, s32[1]{0:T(128)S(6)} %copy.10.refs_1_, f32[1,16,64,128]{3,2,1,0:T(8,128)S(1)} %copy-done, f32[10,64,128]{2,1,0:T(8,128)S(1)} %get-tuple-element.18.refs_3_, f32[10,64,128]{2,1,0:T(8,128)S(1)} %get-tuple-element.19.refs_4_, ...), custom_call_target="tpu_custom_call" | custom-call | tf_op jit(solution)/shard_map/pallas_call | solution.py:257
  18.0 1.9 %collective-permute-start.2 = (f32[16,64,128]{2,1,0:T(8,128)S(1)}, f32[16,64,128]{2,1,0:T(8,128)S(1)}, u32[]{:S(2)}, u32[]{:S(2)}) collective-permute-start(f32[16,64,128]{2,1,0:T(8,128)S(1)} %get-tuple-element.30), channel_id=1, source_target_pairs={{0,16},{16,0},{32,48},{48,32},{64,80},{80,64},{96,112},{112,96},{1... | collective-permute-start | bytes 1572872 | tf_op jit(solution)/shard_map/ppermute | solution.py:267
  19.9 1.9 %collective-permute-done.2 = f32[16,64,128]{2,1,0:T(8,128)S(1)} collective-permute-done((f32[16,64,128]{2,1,0:T(8,128)S(1)}, f32[16,64,128]{2,1,0:T(8,128)S(1)}, u32[]{:S(2)}, u32[]{:S(2)}) %collective-permute-start.2) | collective-permute-done | bytes 524320 | tf_op jit(solution)/shard_map/ppermute | solution.py:267
  21.8 0.1 add.3
  21.9 37.0 %all_to_all.5 = f32[16,64,128]{2,1,0:T(8,128)S(1)} all-to-all(f32[16,64,128]{2,1,0:T(8,128)S(1)} %add.3), channel_id=1, replica_groups={{0,32,64,96,128,160,192,224,256,288,320,352,384,416,448,480},{16,48,80,..., dimensions={0} | all-to-all | bytes 1048576 | tf_op jit(solution)/shard_map/all_to_all | solution.py:269
  58.8 0.6 %reduce_sum.9 = f32[64,128]{1,0:T(8,128)} reduce(f32[16,64,128]{2,1,0:T(8,128)S(1)} %all_to_all.5, f32[]{:T(128)} %constant.0.clone.1), dimensions={0}, to_apply=%region_0.0 | reduce | flops 122880 | bytes 557060 | tf_op jit(solution)/shard_map/reduce_sum | solution.py:270
Async XLA Ops:
  0.0 11.5 %copy-start = (f32[1,16,64,128]{3,2,1,0:T(8,128)S(1)}, f32[1,16,64,128]{3,2,1,0:T(8,128)}, u32[]{:S(2)}) copy-start(f32[1,16,64,128]{3,2,1,0:T(8,128)} %refs_2_.3) | copy-start | bytes 1572868
  0.0 11.5 %copy-start.4 = (f32[1,16,64,128]{3,2,1,0:T(8,128)S(1)}, f32[1,16,64,128]{3,2,1,0:T(8,128)}, u32[]{:S(2)}) copy-start(f32[1,16,64,128]{3,2,1,0:T(8,128)} %refs_4_.1) | copy-start | bytes 1572868
  0.0 11.5 %copy-start.3 = (f32[1,16,64,128]{3,2,1,0:T(8,128)S(1)}, f32[1,16,64,128]{3,2,1,0:T(8,128)}, u32[]{:S(2)}) copy-start(f32[1,16,64,128]{3,2,1,0:T(8,128)} %refs_3_.1) | copy-start | bytes 1572868
  0.0 11.5 %copy-start.2 = (f32[1,16,64,128]{3,2,1,0:T(8,128)S(1)}, f32[1,16,64,128]{3,2,1,0:T(8,128)}, u32[]{:S(2)}) copy-start(f32[1,16,64,128]{3,2,1,0:T(8,128)} %refs_2_.2) | copy-start | bytes 1572868
  0.0 11.5 %copy-start.1 = (f32[1,16,64,128]{3,2,1,0:T(8,128)S(1)}, f32[1,16,64,128]{3,2,1,0:T(8,128)}, u32[]{:S(2)}) copy-start(f32[1,16,64,128]{3,2,1,0:T(8,128)} %refs_1_.2) | copy-start | bytes 1572868
  2.2 13.5 %collective-permute-start = (f32[10,64,128]{2,1,0:T(8,128)S(1)}, f32[10,64,128]{2,1,0:T(8,128)S(1)}, u32[]{:S(2)}, u32[]{:S(2)}) collective-permute-start(f32[10,64,128]{2,1,0:T(8,128)S(1)} %get-tuple-element.18.refs_3_), channel_id=1, source_target_pairs={{0,1},{1,2},{2,3},{3,4},{4,5},{5,6},{6,7},{7,8},{8,9},{9,10},{10,1... | collective-permute-start | bytes 983048 | tf_op jit(solution)/shard_map/ppermute | solution.py:244
  5.6 11.2 %collective-permute-start.1 = (f32[10,64,128]{2,1,0:T(8,128)S(1)}, f32[10,64,128]{2,1,0:T(8,128)S(1)}, u32[]{:S(2)}, u32[]{:S(2)}) collective-permute-start(f32[10,64,128]{2,1,0:T(8,128)S(1)} %get-tuple-element.19.refs_4_), channel_id=1, source_target_pairs={{1,0},{2,1},{3,2},{4,3},{5,4},{6,5},{7,6},{8,7},{9,8},{10,9},{11,1... | collective-permute-start | bytes 983048 | tf_op jit(solution)/shard_map/ppermute | solution.py:245
  11.5 0.9 %copy-start.5 = (f32[1,4,64,128]{3,2,1,0:T(8,128)S(1)}, f32[1,4,64,128]{3,2,1,0:T(8,128)}, u32[]{:S(2)}) copy-start(f32[1,4,64,128]{3,2,1,0:T(8,128)} %refs_5_.1) | copy-start | bytes 393220
  18.0 3.8 %collective-permute-start.2 = (f32[16,64,128]{2,1,0:T(8,128)S(1)}, f32[16,64,128]{2,1,0:T(8,128)S(1)}, u32[]{:S(2)}, u32[]{:S(2)}) collective-permute-start(f32[16,64,128]{2,1,0:T(8,128)S(1)} %get-tuple-element.30), channel_id=1, source_target_pairs={{0,16},{16,0},{32,48},{48,32},{64,80},{80,64},{96,112},{112,96},{1... | collective-permute-start | bytes 1572872 | tf_op jit(solution)/shard_map/ppermute | solution.py:267
